TPU v7x, 32 devices: a whole 2x2x4 slice. The times are simulated.
32 devices in a mesh: groups: 2 (over x), space: 16 (over z, y, core).
Axes of the slice: x: 2, y: 2, z: 4, core: 2. Of those that a mesh axis runs over, the one named last changes fastest.
Arguments:
- snapshots: float32 [24576, 2048], P(('groups', 'space')), parts along dimension 0, may hold values from -6 to 6
- block_of: int32 [512], P(('groups', 'space')), parts along dimension 0, may hold values from 0 to 7
- mass_table: float32 [8, 4, 4], replicated, as said below
Outputs:
- gram: float32 [4096, 2048], P(('groups', 'space')), parts along dimension 0
There are 2 independent parts, one for each index of `groups`. A program takes and returns all parts, laid end to end along the dimension named above; an argument that names none is the same for every part. Nothing has to cross between parts.
Inputs may be any that keep to these rules, and one draw needn't show every extreme that they name: mass_table is symmetric; in each row the diagonal entry exceeds the sum of the other entries' magnitudes.
All inputs are finite; a program needn't handle non-finite values.
Results may differ from a plain program's by a relative error of at most 0.00005.
Values sent between devices are 32-bit elements; how exact they have to be, the bound alone decides.
No kernel may reach another device: no remote copies, remote signals or barrier semaphores. Data moves between devices by JAX's collectives and lax.ppermute only.
A program may use at most 128 MiB of HBM per device.

v0:
```python
import jax
import jax.numpy as jnp
from jax import lax
from jax.sharding import PartitionSpec as P


def per_device(snapshots, block_of, mass_table):
    highest = lax.Precision.HIGHEST
    nspace = lax.axis_size("space")
    rows = snapshots.shape[0]
    order = snapshots.shape[1]
    elems = block_of.shape[0]
    classes = mass_table.shape[0]
    nodes = mass_table.shape[1]
    fields = rows // (elems * nodes)
    onehot = (block_of[:, None] == jnp.arange(classes, dtype=jnp.int32)[None, :]).astype(
        jnp.float32
    )
    masses = jnp.dot(
        onehot,
        mass_table.reshape(classes, nodes * nodes),
        precision=highest,
        preferred_element_type=jnp.float32,
    ).reshape(elems, nodes, nodes)
    grouped = snapshots.reshape(elems, fields, nodes, order)
    weighted = jnp.einsum("eij,efjs->efis", masses, grouped, precision=highest).reshape(rows, order)
    weighted = weighted * (1.0 / (rows * nspace))
    return lax.psum_scatter(
        lax.dot_general(
            snapshots,
            weighted,
            (((0,), (0,)), ((), ())),
            precision=highest,
            preferred_element_type=jnp.float32,
        ),
        "space",
        scatter_dimension=0,
        tiled=True,
    )


def solution(mesh):
    return jax.shard_map(
        per_device,
        mesh=mesh,
        in_specs=(P(("groups", "space"), None), P(("groups", "space")), P()),
        out_specs=P(("groups", "space"), None),
        check_vma=False,
    )
```

profile of v0, /device:TPU:0, one launch (start us, length us, event | category | flops | bytes accessed | tf_op | source)
XLA Modules:
  0.0 274.9 jit_solution(8699761962802735461)
XLA Ops:
  6.5 0.0 copy-start
  6.5 0.0 reduce-scatter.2.cloned.1.call-start
  6.5 0.7 copy-done
  7.2 0.8 convolution_bitcast_fusion.1
  8.1 0.1 copy.6
  8.2 7.5 %reshape.13 = f32[16,12,4,2048]{3,2,1,0:T(4,128)} reshape(f32[768,2048]{1,0:T(8,128)} %param.3) | data formatting | bytes 12582912 | tf_op jit(solution)/shard_map/reshape | solution.py:25
  15.7 15.4 %multiply_bitcast_fusion = f32[16,12,4,2048]{3,2,1,0:T(4,128)} fusion(f32[16,4,4,1]{2,1,3,0:T(4,128)S(1)} %copy.6, f32[16,12,4,2048]{3,2,1,0:T(4,128)} %reshape.13), kind=kOutput, calls=%fused_computation.1 | convolution fusion | flops 77070336 | bytes 12583936 | tf_op jit(solution)/shard_map/eij,efjs->efis/dot_general | solution.py:26
  31.1 7.7 %mul.15 = f32[768,2048]{1,0:T(8,128)} reshape(f32[16,12,4,2048]{3,2,1,0:T(4,128)} %multiply_bitcast_fusion) | data formatting | bytes 12582912 | tf_op jit(solution)/shard_map/mul | solution.py:27
  38.8 45.3 %convolution_bitcast_fusion = f32[2048,2048]{0,1:T(8,128)} fusion(f32[768,2048]{1,0:T(8,128)} %mul.15, f32[768,2048]{1,0:T(8,128)} %param.3), kind=kOutput, calls=%fused_computation | convolution fusion | flops 38654705664 | bytes 29360128 | tf_op jit(solution)/shard_map/dot_general | solution.py:29
  84.1 0.0 reduce-scatter.2.cloned.1.call-update
  84.1 181.4 %reduce-scatter.2.cloned.1.call-done = f32[128,2048]{0,1:T(8,128)} async-done(((f32[2048,2048]{0,1:T(8,128)}), f32[128,2048]{0,1:T(8,128)}) %reduce-scatter.2.cloned.1.call-update) | async-done | bytes 1048592 | tf_op jit(solution)/shard_map/reduce_scatter | solution.py:28
  265.5 2.5 copy.4
Async XLA Ops:
  6.5 0.7 copy-start
  6.5 259.0 %reduce-scatter.2.cloned.1.call-start = ((), (), s32[]{:S(2)}) async-start(), calls=%async_computation.1 | async-start | bytes 17825792 | tf_op jit(solution)/shard_map/reduce_scatter | solution.py:28
Sparse Core Ops, SparseCore 0:
  84.2 181.2 reduce-scatter.1
where the time goes:
time: 275 us
  waiting for transfers between devices  181 us (66%)
  matrix products  61.6 us (22%)
  local copies, waits for them, and re-layouts  18.5 us (7%)
  between operations  13.4 us (5%)
    reduce_scatter x1, waiting for transfers between devices, per_device(): lax.psum_scatter(lax.dot_general(snapshots, weighted, (((0,), (0,)), ((),...  181 us
    dot_general x1, matrix products, per_device(): lax.dot_general(snapshots, weighted, (((0,), (0,)), ((), ())), precision=...  45.3 us
    dot_general x1, matrix products, per_device(): jnp.einsum('eij,efjs->efis', masses, grouped, precision=highest)  15.4 us
    mul x1, local copies, waits for them, and re-layouts, per_device(): weighted = weighted * (1.0 / (rows * nspace))  7.65 us
    reshape x1, local copies, waits for them, and re-layouts, per_device(): grouped = snapshots.reshape(elems, fields, nodes, order)  7.48 us
  transfers between devices with their start and end apart: 1, of which 1 were waited for; matrix products, arithmetic and copies ran while one was open for 0% of the time, Pallas kernels for 0%

commit v1 on v0

v1 whole, which is shorter than its diff:
```python
import functools

import jax
import jax.numpy as jnp
import numpy as np
from jax import lax
from jax.experimental import pallas as pl
from jax.experimental.pallas import tpu as pltpu
from jax.sharding import PartitionSpec as P

F32 = jnp.float32
BF16 = jnp.bfloat16
MIB = 1 << 20
CHIPS = 8
SUB = 128
TWO = 2 * SUB


def prep_kernel(scale, block_of, mass, x_hbm, xh, xl, wh, wl, x, table, dh, dl, sems):
    rows, order = x_hbm.shape
    classes, nodes = mass.shape[0], mass.shape[1]
    per_element = rows // block_of.shape[0]
    band = dh.shape[0]
    wide = order // 2
    copies = []
    for b in range(rows // band):
        for h in range(2):
            at = (pl.ds(b * band, band), pl.ds(h * wide, wide))
            copy = pltpu.make_async_copy(x_hbm.at[at], x.at[at], sems.at[2 * b + h])
            copy.start()
            copies.append(copy)
    row = lax.broadcasted_iota(jnp.int32, (8, band), 0)
    column = lax.broadcasted_iota(jnp.int32, (8, band), 1)
    for k in range(classes):
        tile = jnp.zeros((8, band), F32)
        for i in range(nodes):
            for j in range(nodes):
                here = (row % nodes == i) & (column % nodes == j)
                tile = jnp.where(here, mass[k, i, j] * scale, tile)
        table[8 * k : 8 * k + 8, :] = tile
    for b in range(rows // band):
        for g in range(band // 8):
            kind = block_of[(b * band + 8 * g) // per_element]
            tile = table[pl.ds(pl.multiple_of(kind * 8, 8), 8), :]
            tile = jnp.where((row + 8 * g) // nodes == column // nodes, tile, 0.0)
            high = tile.astype(BF16).astype(F32)
            dh[8 * g : 8 * g + 8, :] = high
            dl[8 * g : 8 * g + 8, :] = tile - high
        mh, ml = dh[...].astype(BF16), dl[...].astype(BF16)
        for h in range(2):
            copies[2 * b + h].wait()

            @pl.loop(0, wide // TWO)
            def _(t):
                at = (pl.ds(b * band, band), pl.ds(pl.multiple_of(h * wide + t * TWO, TWO), TWO))
                value = x[at]
                high = value.astype(BF16)
                low = (value - high.astype(F32)).astype(BF16)
                xh[at] = high
                xl[at] = low
                dot = functools.partial(jnp.dot, preferred_element_type=F32)
                weighted = dot(mh, high) + dot(mh, low) + dot(ml, high)
                high = weighted.astype(BF16)
                wh[at] = high
                wl[at] = (weighted - high.astype(F32)).astype(BF16)


def prepare(snapshots, block_of, mass_table, scale):
    rows, order = snapshots.shape
    band = TWO
    smem = pl.BlockSpec(memory_space=pltpu.SMEM)
    vmem = pl.BlockSpec(memory_space=pltpu.VMEM)
    return pl.pallas_call(
        functools.partial(prep_kernel, scale),
        out_shape=[pltpu.VMEM((rows, order), BF16)] * 4,
        in_specs=[smem, smem, pl.BlockSpec(memory_space=pl.ANY)],
        out_specs=[vmem] * 4,
        scratch_shapes=[
            pltpu.VMEM((rows, order), F32),
            pltpu.VMEM((8 * mass_table.shape[0], band), F32),
            pltpu.VMEM((band, band), F32),
            pltpu.VMEM((band, band), F32),
            pltpu.SemaphoreType.DMA((2 * (rows // band),)),
        ],
        compiler_params=pltpu.CompilerParams(vmem_limit_bytes=32 * MIB),
        cost_estimate=pl.CostEstimate(
            flops=6 * rows * order * band, bytes_accessed=6 * rows * order, transcendentals=0
        ),
        name="weighting",
    )(block_of, mass_table, snapshots)


WIDTHS = (5 * SUB, 4 * SUB)
LHS, K0, K1, K2, K3, K4A, K4B = range(7)
INSTANCES = {name: 7 * i for i, name in enumerate(("1A", "1B", "2A", "2B", "3A", "3B", "4A", "4B", "5"))}
CORE, R1, R2, R3, R4 = range(63, 68)
TABLE = 68


def ring_chip(p):
    p %= CHIPS
    return 2 * p if p < 4 else 2 * (CHIPS - 1 - p) + 1


def ring_device(p, core):
    return 2 * ring_chip(p) + core


def fourth(q, r):
    return r if q % CHIPS < 4 else 1 - r


def position_table():
    table = np.zeros((2 * CHIPS, TABLE), np.int32)

    def strip(q, half=None):
        at = TWO * ring_chip(q)
        cols = [TWO * ring_chip(q + k) for k in range(5)]
        fours = [cols[4] + SUB * fourth(q, r) for r in range(2)]
        if half is None:
            return [at] + cols[:4] + fours
        return [at + SUB * half] + cols[:4] + [fours[half]] * 2

    for p in range(CHIPS):
        for c in range(2):
            sign = 1 - 2 * c
            row = strip(p + 4, c) + strip(p + 4, 1 - c)
            for step in (2, 3, 4):
                row += strip(p + sign * (5 - step)) + strip(p - sign * (5 - step))
            row += strip(p)
            row += [SUB * c] + [TWO * ring_chip(p - k) for k in (1, 2, 3)]
            row += [TWO * ring_chip(p + 4) + SUB * (c if (p + 4) % CHIPS < 4 else 1 - c)]
            table[ring_device(p, c)] = row
    return table


def product(xh, xl, wh, wl, rows, at, width):
    def dot(a, b):
        return lax.dot_general(
            a[:, rows], b[:, pl.ds(at, width)], (((0,), (0,)), ((), ())), preferred_element_type=F32
        )

    return dot(xh, wh) + dot(xh, wl) + dot(xl, wh)


def strip_kernel(base, part, height, names, table, xh, xl, wh, wl, *refs):
    ins, out = refs[:-1], refs[-1]

    def entry(i):
        return pl.multiple_of(table[base + i], SUB)

    def put(r, n, c, w, value):
        for name, ref in zip(names, ins):
            if name == "same":
                value = value + ref[r : r + n, c : c + w]
        out[r : r + n, c : c + w] = value

    lhs = entry(LHS)
    c = 0
    if part == 0:
        for r in range(height // SUB):
            rows = pl.ds(pl.multiple_of(lhs + SUB * r, SUB), SUB)
            put(SUB * r, SUB, 0, SUB, product(xh, xl, wh, wl, rows, entry(K4A + r), SUB))
        c = SUB
    for k in (K3, K2) if part == 0 else (K1, K0):
        put(0, height, c, TWO, product(xh, xl, wh, wl, pl.ds(lhs, height), entry(k), TWO))
        c += TWO
    for name, ref in zip(names, ins):
        if name == "half":
            rows = pl.ds(pl.multiple_of(table[CORE], SUB), SUB)
            out[rows, :] = out[rows, :] + ref[...]


def strip(name, part, height, operands, table, same=(), half=()):
    width = WIDTHS[part]
    names = ("same",) * len(same) + ("half",) * len(half)
    vmem = pl.BlockSpec(memory_space=pltpu.VMEM)
    depth = operands[0].shape[0]
    pinned = [pltpu.with_memory_space_constraint(x, pltpu.VMEM) for x in operands]
    return pl.pallas_call(
        functools.partial(strip_kernel, INSTANCES[name], part, height, names),
        out_shape=jax.ShapeDtypeStruct((height, width), F32),
        in_specs=[pl.BlockSpec(memory_space=pltpu.SMEM)] + [vmem] * (4 + len(names)),
        out_specs=vmem,
        compiler_params=pltpu.CompilerParams(vmem_limit_bytes=20 * MIB),
        cost_estimate=pl.CostEstimate(
            flops=6 * height * width * depth,
            bytes_accessed=4 * height * width * (1 + len(names)),
            transcendentals=0,
        ),
        name=f"strip_{name}_{part}",
    )(table, *pinned, *same, *half)


def total_kernel(part, table, mine, other, own, *sends):
    core = pl.multiple_of(table[CORE], SUB)
    rows = pl.ds(core, SUB)
    own[...] = mine[rows, :] + other[rows, :]
    if part == 0:
        sends[0][...] = own[:, 0:SUB]
    at = (SUB, SUB + TWO) if part == 0 else (0,)
    for out, c in zip(sends[1:] if part == 0 else sends, at):
        columns = pl.ds(pl.multiple_of(core + c, SUB), SUB)
        out[...] = mine[:, columns] + other[:, columns]


def total(part, table, mine, other):
    vmem = pl.BlockSpec(memory_space=pltpu.VMEM)
    blocks = [(SUB, WIDTHS[part])]
    blocks += [(SUB, SUB), (TWO, SUB), (TWO, SUB)] if part == 0 else [(TWO, SUB)]
    return pl.pallas_call(
        functools.partial(total_kernel, part),
        out_shape=[jax.ShapeDtypeStruct(b, F32) for b in blocks],
        in_specs=[pl.BlockSpec(memory_space=pltpu.SMEM), vmem, vmem],
        out_specs=[vmem] * len(blocks),
        compiler_params=pltpu.CompilerParams(vmem_limit_bytes=20 * MIB),
        name=f"total_{part}",
    )(table, mine, other)


def place_kernel(table, own0, own1, r4, r3, r2, r1, out):
    def put(entry, width, value):
        out[:, pl.ds(pl.multiple_of(table[entry], SUB), width)] = value

    base = INSTANCES["5"]
    core = table[CORE] // SUB
    for r in range(2):

        @pl.when(core == r)
        def _():
            put(base + K4A + r, SUB, own0[:, 0:SUB])

    put(base + K3, TWO, own0[:, SUB : SUB + TWO])
    put(base + K2, TWO, own0[:, SUB + TWO :])
    put(base + K1, TWO, own1[:, 0:TWO])
    put(base + K0, TWO, own1[:, TWO:])
    put(R4, SUB, r4[...].T)
    put(R3, TWO, r3[...].T)
    put(R2, TWO, r2[...].T)
    put(R1, TWO, r1[...].T)


def place(table, *parts, order):
    vmem = pl.BlockSpec(memory_space=pltpu.VMEM)
    return pl.pallas_call(
        place_kernel,
        out_shape=jax.ShapeDtypeStruct((SUB, order), F32),
        in_specs=[pl.BlockSpec(memory_space=pltpu.SMEM)] + [vmem] * len(parts),
        out_specs=vmem,
        compiler_params=pltpu.CompilerParams(vmem_limit_bytes=20 * MIB),
        name="place",
    )(table, *parts)


def ring_gram(snapshots, block_of, mass_table, axis):
    rows, order = snapshots.shape
    ring, swap, fours = [], [], []
    far = {1: [], 2: [], 3: []}
    for p in range(CHIPS):
        for c in range(2):
            here = ring_device(p, c)
            ring.append((here, ring_device(p + 1 - 2 * c, c)))
            swap.append((here, ring_device(p, 1 - c)))
            fours.append((here, ring_device(p + 4, fourth(p, c))))
            for k in far:
                far[k].append((here, ring_device(p + k, c)))
    table = jnp.asarray(position_table())[lax.axis_index(axis)]
    operands = prepare(snapshots, block_of, mass_table, 1.0 / (rows * 2 * CHIPS))
    send = lambda x, pairs: lax.ppermute(x, axis, pairs)

    moving = [None, None]
    for part in range(2):
        other = send(strip("1B", part, SUB, operands, table), swap)
        moving[part] = strip("1A", part, SUB, operands, table, same=(other,))
    for step in ("2", "3", "4"):
        for part in range(2):
            other = send(strip(step + "B", part, TWO, operands, table), swap)
            came = send(moving[part], ring)
            same, half = ((other,), (came,)) if step == "2" else ((other, came), ())
            moving[part] = strip(step + "A", part, TWO, operands, table, same=same, half=half)
    own, got = [], []
    for part in range(2):
        came = send(moving[part], ring)
        mine = strip("5", part, TWO, operands, table, same=(came,))
        outs = total(part, table, mine, send(mine, swap))
        own.append(outs[0])
        if part == 0:
            got += [send(outs[1], fours), send(outs[2], far[3]), send(outs[3], far[2])]
        else:
            got += [send(outs[1], far[1])]
    return place(table, *own, *got, order=order)


def scattered_gram(snapshots, block_of, mass_table, axis):
    rows, order = snapshots.shape
    xh, xl, wh, wl = prepare(snapshots, block_of, mass_table, 1.0 / (rows * lax.axis_size(axis)))

    def dot(a, b):
        return lax.dot_general(a, b, (((0,), (0,)), ((), ())), preferred_element_type=F32)

    return lax.psum_scatter(
        dot(xh, wh) + (dot(xh, wl) + dot(xl, wh)), axis, scatter_dimension=0, tiled=True
    )


def per_device(snapshots, block_of, mass_table):
    axis = "space"
    ring = lax.axis_size(axis) == 2 * CHIPS and snapshots.shape[1] == 2 * CHIPS * SUB
    form = ring_gram if ring else scattered_gram
    return form(snapshots, block_of, mass_table, axis)


def solution(mesh):
    return jax.shard_map(
        per_device,
        mesh=mesh,
        in_specs=(P(("groups", "space"), None), P(("groups", "space")), P()),
        out_specs=P(("groups", "space"), None),
        check_vma=False,
    )
```

time: 275 us -> 104 us (0.38)
  waiting for transfers between devices: 181 us -> 33.4 us
  matrix products: 61.6 us -> 0 us
  Pallas kernels: 0 us -> 39.6 us
  starting transfers between devices: 0.01 us -> 24.7 us
  local copies, waits for them, and re-layouts: 18.5 us -> 4.92 us
  between operations: 13.4 us -> 0.28 us
    reduce_scatter x1 -> x0, waiting for transfers between devices: 181 us -> none  [per_device(): lax.psum_scatter(lax.dot_general(snapshots, weighted, (((0,), (0,)), ((),...]
    dot_general x3 -> x0, matrix products: 61.6 us -> none  [the longest x1 45.3 us: per_device(): lax.dot_general(snapshots, weighted, (((0,), (0,)), ((), ())), precision=...]
    pallas_call x0 -> x22, Pallas kernels: none -> 39.6 us  [the longest x18 28 us: strip(): pl.pallas_call(functools.partial(strip_kernel, INSTANCES[name], part, hei...]
    ppermute x0 -> x22, waiting for transfers between devices: none -> 33.4 us  [ring_gram(): send = lambda x, pairs: lax.ppermute(x, axis, pairs)]
    ppermute x0 -> x22, starting transfers between devices: none -> 24.7 us  [ring_gram(): send = lambda x, pairs: lax.ppermute(x, axis, pairs)]
    mul x1 -> x0, local copies, waits for them, and re-layouts: 7.65 us -> none  [per_device(): weighted = weighted * (1.0 / (rows * nspace))]
    reshape x1 -> x0, local copies, waits for them, and re-layouts: 7.48 us -> none  [per_device(): grouped = snapshots.reshape(elems, fields, nodes, order)]
    unnamed x2 -> x5, local copies, waits for them, and re-layouts: 0.69 us -> 4.23 us
  transfers between devices with their start and end apart: 1 -> 22, of which waited for: 1 -> 9; matrix products, arithmetic and copies ran while one was open for 0% -> 0% of each run, Pallas kernels for 0% -> 27%
where the time goes in v1:
time: 104 us; the launch traced here: 103 us
  Pallas kernels  39.6 us (38%)
  waiting for transfers between devices  33.4 us (32%)
  starting transfers between devices  24.7 us (24%)
  local copies, waits for them, and re-layouts  4.92 us (5%)
    ppermute x22, waiting for transfers between devices, ring_gram(): send = lambda x, pairs: lax.ppermute(x, axis, pairs)  33.4 us
    pallas_call x18, Pallas kernels, strip(): pl.pallas_call(functools.partial(strip_kernel, INSTANCES[name], part, hei...  28 us
    ppermute x22, starting transfers between devices, ring_gram(): send = lambda x, pairs: lax.ppermute(x, axis, pairs)  24.7 us
    pallas_call x1, Pallas kernels, prepare(): pl.pallas_call(functools.partial(prep_kernel, scale), out_shape=[pltpu.VM...  8.61 us
    unnamed x5, local copies, waits for them, and re-layouts  4.23 us
  transfers between devices with their start and end apart: 22, of which 9 were waited for; matrix products, arithmetic and copies ran while one was open for 0% of the time, Pallas kernels for 27%

profile of v1, /device:TPU:0, one launch (start us, length us, event | category | flops | bytes accessed | tf_op | source)
XLA Modules:
  0.0 102.8 jit_solution(4496657495287670796)
XLA Ops:
  1.5 2.8 %copy-done = f32[768,2048]{1,0:T(8,128)S(1)} copy-done((f32[768,2048]{1,0:T(8,128)S(1)}, f32[768,2048]{1,0:T(8,128)}, u32[]{:S(2)}) %copy-start) | copy-done | bytes 6291480
  4.9 8.6 %weighting.1 = (bf16[768,2048]{1,0:T(8,128)(2,1)S(1)}, bf16[768,2048]{1,0:T(8,128)(2,1)S(1)}, bf16[768,2048]{1,0:T(8,128)(2,1)S(1)}, bf16[768,2048]{1,0:T(8,128)(2,1)S(1)}) custom-call(s32[16]{0:T(128)S(1)} %copy-done.1, f32[8,4,4]{2,1,0:T(4,128)S(1)} %copy.5.mass, f32[768,2048]{1,0:T(8,128)S(1)} %copy-done), custom_call_target="tpu_custom_call" | custom-call | flops 2415919104 | bytes 9437184 | tf_op jit(solution)/shard_map/weighting/pallas_call | solution.py:73
  15.4 1.9 %strip_2B_0.1 = f32[256,640]{1,0:T(8,128)S(1)} custom-call(s32[68]{0:T(128)S(1)} %dynamic-slice_bitcast_fusion.table, bf16[768,2048]{1,0:T(8,128)(2,1)S(1)} %get-tuple-element.15.xh, bf16[768,2048]{1,0:T(8,128)(2,1)S(1)} %get-tuple-element.16.xl, bf16[768,2048]{1,0:T(8,128)(2,1)S(1)} %get-tuple-element.17.wh, bf16[768,2048]{1,0:T(8,128)(2,1)S(1)} %get-tuple-element.18.wl), custom_call_target="tpu_custom_call" | custom-call | flops 754974720 | bytes 655360 | tf_op jit(solution)/shard_map/strip_2B_0/pallas_call | solution.py:180
  18.8 3.1 %collective-permute-start.4 = (f32[128,640]{1,0:T(8,128)S(1)}, f32[128,640]{1,0:T(8,128)S(1)}, u32[]{:S(2)}, u32[]{:S(2)}) collective-permute-start(f32[128,640]{1,0:T(8,128)S(1)} %strip_1A_0.1), channel_id=1, source_target_pairs={{0,4},{1,3},{4,8},{5,1},{8,12},{9,5},{12,14},{13,9},{14,10},{15,13... | collective-permute-start | bytes 983048 | tf_op jit(solution)/shard_map/ppermute | solution.py:269
  25.1 1.9 %strip_3B_0.1 = f32[256,640]{1,0:T(8,128)S(1)} custom-call(s32[68]{0:T(128)S(1)} %dynamic-slice_bitcast_fusion.table, bf16[768,2048]{1,0:T(8,128)(2,1)S(1)} %get-tuple-element.15.xh, bf16[768,2048]{1,0:T(8,128)(2,1)S(1)} %get-tuple-element.16.xl, bf16[768,2048]{1,0:T(8,128)(2,1)S(1)} %get-tuple-element.17.wh, bf16[768,2048]{1,0:T(8,128)(2,1)S(1)} %get-tuple-element.18.wl), custom_call_target="tpu_custom_call" | custom-call | flops 754974720 | bytes 655360 | tf_op jit(solution)/shard_map/strip_3B_0/pallas_call | solution.py:180
  27.1 1.9 %strip_2A_0.1 = f32[256,640]{1,0:T(8,128)S(1)} custom-call(s32[68]{0:T(128)S(1)} %dynamic-slice_bitcast_fusion.table, bf16[768,2048]{1,0:T(8,128)(2,1)S(1)} %get-tuple-element.15.xh, bf16[768,2048]{1,0:T(8,128)(2,1)S(1)} %get-tuple-element.16.xl, bf16[768,2048]{1,0:T(8,128)(2,1)S(1)} %get-tuple-element.17.wh, bf16[768,2048]{1,0:T(8,128)(2,1)S(1)} %get-tuple-element.18.wl, ...), custom_call_target="tpu_custom_call" | custom-call | flops 754974720 | bytes 1966080 | tf_op jit(solution)/shard_map/strip_2A_0/pallas_call | solution.py:180
  29.0 2.0 %collective-permute-start.5 = (f32[256,640]{1,0:T(8,128)S(1)}, f32[256,640]{1,0:T(8,128)S(1)}, u32[]{:S(2)}, u32[]{:S(2)}) collective-permute-start(f32[256,640]{1,0:T(8,128)S(1)} %strip_2A_0.1), channel_id=1, source_target_pairs={{0,4},{1,3},{4,8},{5,1},{8,12},{9,5},{12,14},{13,9},{14,10},{15,13... | collective-permute-start | bytes 1966088 | tf_op jit(solution)/shard_map/ppermute | solution.py:269
  35.2 7.3 %collective-permute-done.13.refs_1_ = f32[128,512]{1,0:T(8,128)S(1)} collective-permute-done((f32[128,512]{1,0:T(8,128)S(1)}, f32[128,512]{1,0:T(8,128)S(1)}, u32[]{:S(2)}, u32[]{:S(2)}) %collective-permute-start.13) | collective-permute-done | bytes 262176 | tf_op jit(solution)/shard_map/ppermute | solution.py:269
  43.9 2.1 %collective-permute-start.14 = (f32[256,512]{1,0:T(8,128)S(1)}, f32[256,512]{1,0:T(8,128)S(1)}, u32[]{:S(2)}, u32[]{:S(2)}) collective-permute-start(f32[256,512]{1,0:T(8,128)S(1)} %strip_2A_1.1), channel_id=1, source_target_pairs={{0,4},{1,3},{4,8},{5,1},{8,12},{9,5},{12,14},{13,9},{14,10},{15,13... | collective-permute-start | bytes 1572872 | tf_op jit(solution)/shard_map/ppermute | solution.py:269
  46.0 1.9 %strip_4B_0.1 = f32[256,640]{1,0:T(8,128)S(1)} custom-call(s32[68]{0:T(128)S(1)} %dynamic-slice_bitcast_fusion.table, bf16[768,2048]{1,0:T(8,128)(2,1)S(1)} %get-tuple-element.15.xh, bf16[768,2048]{1,0:T(8,128)(2,1)S(1)} %get-tuple-element.16.xl, bf16[768,2048]{1,0:T(8,128)(2,1)S(1)} %get-tuple-element.17.wh, bf16[768,2048]{1,0:T(8,128)(2,1)S(1)} %get-tuple-element.18.wl), custom_call_target="tpu_custom_call" | custom-call | flops 754974720 | bytes 655360 | tf_op jit(solution)/shard_map/strip_4B_0/pallas_call | solution.py:180
  48.0 1.9 %strip_3A_0.1 = f32[256,640]{1,0:T(8,128)S(1)} custom-call(s32[68]{0:T(128)S(1)} %dynamic-slice_bitcast_fusion.table, bf16[768,2048]{1,0:T(8,128)(2,1)S(1)} %get-tuple-element.15.xh, bf16[768,2048]{1,0:T(8,128)(2,1)S(1)} %get-tuple-element.16.xl, bf16[768,2048]{1,0:T(8,128)(2,1)S(1)} %get-tuple-element.17.wh, bf16[768,2048]{1,0:T(8,128)(2,1)S(1)} %get-tuple-element.18.wl, ...), custom_call_target="tpu_custom_call" | custom-call | flops 754974720 | bytes 1966080 | tf_op jit(solution)/shard_map/strip_3A_0/pallas_call | solution.py:180
  54.7 1.9 %collective-permute-start.15 = (f32[256,512]{1,0:T(8,128)S(1)}, f32[256,512]{1,0:T(8,128)S(1)}, u32[]{:S(2)}, u32[]{:S(2)}) collective-permute-start(f32[256,512]{1,0:T(8,128)S(1)} %strip_3A_1.1), channel_id=1, source_target_pairs={{0,4},{1,3},{4,8},{5,1},{8,12},{9,5},{12,14},{13,9},{14,10},{15,13... | collective-permute-start | bytes 1572872 | tf_op jit(solution)/shard_map/ppermute | solution.py:269
  56.7 3.9 %collective-permute-done.6.refs_1_ = f32[256,640]{1,0:T(8,128)S(1)} collective-permute-done((f32[256,640]{1,0:T(8,128)S(1)}, f32[256,640]{1,0:T(8,128)S(1)}, u32[]{:S(2)}, u32[]{:S(2)}) %collective-permute-start.6) | collective-permute-done | bytes 655392 | tf_op jit(solution)/shard_map/ppermute | solution.py:269
  60.6 1.9 %strip_4A_0.1 = f32[256,640]{1,0:T(8,128)S(1)} custom-call(s32[68]{0:T(128)S(1)} %dynamic-slice_bitcast_fusion.table, bf16[768,2048]{1,0:T(8,128)(2,1)S(1)} %get-tuple-element.15.xh, bf16[768,2048]{1,0:T(8,128)(2,1)S(1)} %get-tuple-element.16.xl, bf16[768,2048]{1,0:T(8,128)(2,1)S(1)} %get-tuple-element.17.wh, bf16[768,2048]{1,0:T(8,128)(2,1)S(1)} %get-tuple-element.18.wl, ...), custom_call_target="tpu_custom_call" | custom-call | flops 754974720 | bytes 1966080 | tf_op jit(solution)/shard_map/strip_4A_0/pallas_call | solution.py:180
  64.2 2.0 %collective-permute-done.15.refs_1_ = f32[256,512]{1,0:T(8,128)S(1)} collective-permute-done((f32[256,512]{1,0:T(8,128)S(1)}, f32[256,512]{1,0:T(8,128)S(1)}, u32[]{:S(2)}, u32[]{:S(2)}) %collective-permute-start.15) | collective-permute-done | bytes 524320 | tf_op jit(solution)/shard_map/ppermute | solution.py:269
  69.3 3.9 %collective-permute-done.7.refs_0_ = f32[256,640]{1,0:T(8,128)S(1)} collective-permute-done((f32[256,640]{1,0:T(8,128)S(1)}, f32[256,640]{1,0:T(8,128)S(1)}, u32[]{:S(2)}, u32[]{:S(2)}) %collective-permute-start.7) | collective-permute-done | bytes 655392 | tf_op jit(solution)/shard_map/ppermute | solution.py:269
  73.2 1.9 %strip_5_0.1.mine = f32[256,640]{1,0:T(8,128)S(1)} custom-call(s32[68]{0:T(128)S(1)} %dynamic-slice_bitcast_fusion.table, bf16[768,2048]{1,0:T(8,128)(2,1)S(1)} %get-tuple-element.15.xh, bf16[768,2048]{1,0:T(8,128)(2,1)S(1)} %get-tuple-element.16.xl, bf16[768,2048]{1,0:T(8,128)(2,1)S(1)} %get-tuple-element.17.wh, ...), custom_call_target="tpu_custom_call" | custom-call | flops 754974720 | bytes 1310720 | tf_op jit(solution)/shard_map/strip_5_0/pallas_call | solution.py:180
  75.2 3.6 %collective-permute-done.16.refs_0_ = f32[256,512]{1,0:T(8,128)S(1)} collective-permute-done((f32[256,512]{1,0:T(8,128)S(1)}, f32[256,512]{1,0:T(8,128)S(1)}, u32[]{:S(2)}, u32[]{:S(2)}) %collective-permute-start.16) | collective-permute-done | bytes 524320 | tf_op jit(solution)/shard_map/ppermute | solution.py:269
  80.3 1.9 %collective-permute-done.17.other = f32[256,512]{1,0:T(8,128)S(1)} collective-permute-done((f32[256,512]{1,0:T(8,128)S(1)}, f32[256,512]{1,0:T(8,128)S(1)}, u32[]{:S(2)}, u32[]{:S(2)}) %collective-permute-start.17) | collective-permute-done | bytes 524320 | tf_op jit(solution)/shard_map/ppermute | solution.py:269
  85.1 3.6 %collective-permute-start.19 = (f32[256,128]{1,0:T(8,128)S(1)}, f32[256,128]{1,0:T(8,128)S(1)}, u32[]{:S(2)}, u32[]{:S(2)}) collective-permute-start(f32[256,128]{1,0:T(8,128)S(1)} %get-tuple-element.22), channel_id=1, source_target_pairs={{0,12},{1,13},{4,14},{5,15},{8,10},{9,11},{12,6},{13,7},{14,2},{15... | collective-permute-start | bytes 393224 | tf_op jit(solution)/shard_map/ppermute | solution.py:269
  88.8 1.8 %collective-permute-start.18 = (f32[128,128]{1,0:T(8,128)S(1)}, f32[128,128]{1,0:T(8,128)S(1)}, u32[]{:S(2)}, u32[]{:S(2)}) collective-permute-start(f32[128,128]{1,0:T(8,128)S(1)} %get-tuple-element.21), channel_id=1, source_target_pairs={{0,14},{1,15},{4,10},{5,11},{8,6},{9,7},{12,2},{13,3},{14,1},{15,0... | collective-permute-start | bytes 196616 | tf_op jit(solution)/shard_map/ppermute | solution.py:269
  90.6 7.2 %collective-permute-done.18.r4 = f32[128,128]{1,0:T(8,128)S(1)} collective-permute-done((f32[128,128]{1,0:T(8,128)S(1)}, f32[128,128]{1,0:T(8,128)S(1)}, u32[]{:S(2)}, u32[]{:S(2)}) %collective-permute-start.18) | collective-permute-done | bytes 65568 | tf_op jit(solution)/shard_map/ppermute | solution.py:269
  97.8 3.3 %collective-permute-done.19.r3 = f32[256,128]{1,0:T(8,128)S(1)} collective-permute-done((f32[256,128]{1,0:T(8,128)S(1)}, f32[256,128]{1,0:T(8,128)S(1)}, u32[]{:S(2)}, u32[]{:S(2)}) %collective-permute-start.19) | collective-permute-done | bytes 131104 | tf_op jit(solution)/shard_map/ppermute | solution.py:269
  101.1 1.8 %place.1 = f32[128,2048]{1,0:T(8,128)} custom-call(s32[68]{0:T(128)S(1)} %dynamic-slice_bitcast_fusion.table, f32[128,640]{1,0:T(8,128)S(1)} %get-tuple-element.19.own0, f32[128,512]{1,0:T(8,128)S(1)} %get-tuple-element.20.own1, f32[128,128]{1,0:T(8,128)S(1)} %collective-permute-done.18.r4, f32[256,128]{1,0:T(8,128)S(1)} %collective-permute-done.19.r3, ...), custom_call_target="tpu_custom_call" | custom-call | tf_op jit(solution)/shard_map/place/pallas_call | solution.py:245
  (48 shorter events, 28.4 us)
Async XLA Ops:
  1.5 2.8 %copy-start = (f32[768,2048]{1,0:T(8,128)S(1)}, f32[768,2048]{1,0:T(8,128)}, u32[]{:S(2)}) copy-start(f32[768,2048]{1,0:T(8,128)} %x_hbm.1) | copy-start | bytes 18874372
  4.3 0.7 copy-start.1
  14.9 2.5 %collective-permute-start.3 = (f32[128,640]{1,0:T(8,128)S(1)}, f32[128,640]{1,0:T(8,128)S(1)}, u32[]{:S(2)}, u32[]{:S(2)}) collective-permute-start(f32[128,640]{1,0:T(8,128)S(1)} %strip_1B_0.1), channel_id=1, source_target_pairs={{0,1},{1,0},{4,5},{5,4},{8,9},{9,8},{12,13},{13,12},{14,15},{15,14... | collective-permute-start | bytes 983048 | tf_op jit(solution)/shard_map/ppermute | solution.py:269
  17.3 9.7 %collective-permute-start.2 = (f32[256,640]{1,0:T(8,128)S(1)}, f32[256,640]{1,0:T(8,128)S(1)}, u32[]{:S(2)}, u32[]{:S(2)}) collective-permute-start(f32[256,640]{1,0:T(8,128)S(1)} %strip_2B_0.1), channel_id=1, source_target_pairs={{0,1},{1,0},{4,5},{5,4},{8,9},{9,8},{12,13},{13,12},{14,15},{15,14... | collective-permute-start | bytes 1966088 | tf_op jit(solution)/shard_map/ppermute | solution.py:269
  18.8 8.3 %collective-permute-start.4 = (f32[128,640]{1,0:T(8,128)S(1)}, f32[128,640]{1,0:T(8,128)S(1)}, u32[]{:S(2)}, u32[]{:S(2)}) collective-permute-start(f32[128,640]{1,0:T(8,128)S(1)} %strip_1A_0.1), channel_id=1, source_target_pairs={{0,4},{1,3},{4,8},{5,1},{8,12},{9,5},{12,14},{13,9},{14,10},{15,13... | collective-permute-start | bytes 983048 | tf_op jit(solution)/shard_map/ppermute | solution.py:269
  23.0 7.9 %collective-permute-start.12 = (f32[128,512]{1,0:T(8,128)S(1)}, f32[128,512]{1,0:T(8,128)S(1)}, u32[]{:S(2)}, u32[]{:S(2)}) collective-permute-start(f32[128,512]{1,0:T(8,128)S(1)} %strip_1B_1.1), channel_id=1, source_target_pairs={{0,1},{1,0},{4,5},{5,4},{8,9},{9,8},{12,13},{13,12},{14,15},{15,14... | collective-permute-start | bytes 786440 | tf_op jit(solution)/shard_map/ppermute | solution.py:269
  24.5 17.9 %collective-permute-start.11 = (f32[256,512]{1,0:T(8,128)S(1)}, f32[256,512]{1,0:T(8,128)S(1)}, u32[]{:S(2)}, u32[]{:S(2)}) collective-permute-start(f32[256,512]{1,0:T(8,128)S(1)} %strip_2B_1.1), channel_id=1, source_target_pairs={{0,1},{1,0},{4,5},{5,4},{8,9},{9,8},{12,13},{13,12},{14,15},{15,14... | collective-permute-start | bytes 1572872 | tf_op jit(solution)/shard_map/ppermute | solution.py:269
  27.0 21.0 %collective-permute-start.1 = (f32[256,640]{1,0:T(8,128)S(1)}, f32[256,640]{1,0:T(8,128)S(1)}, u32[]{:S(2)}, u32[]{:S(2)}) collective-permute-start(f32[256,640]{1,0:T(8,128)S(1)} %strip_3B_0.1), channel_id=1, source_target_pairs={{0,1},{1,0},{4,5},{5,4},{8,9},{9,8},{12,13},{13,12},{14,15},{15,14... | collective-permute-start | bytes 1966088 | tf_op jit(solution)/shard_map/ppermute | solution.py:269
  29.0 19.0 %collective-permute-start.5 = (f32[256,640]{1,0:T(8,128)S(1)}, f32[256,640]{1,0:T(8,128)S(1)}, u32[]{:S(2)}, u32[]{:S(2)}) collective-permute-start(f32[256,640]{1,0:T(8,128)S(1)} %strip_2A_0.1), channel_id=1, source_target_pairs={{0,4},{1,3},{4,8},{5,1},{8,12},{9,5},{12,14},{13,9},{14,10},{15,13... | collective-permute-start | bytes 1966088 | tf_op jit(solution)/shard_map/ppermute | solution.py:269
  32.1 10.3 %collective-permute-start.13 = (f32[128,512]{1,0:T(8,128)S(1)}, f32[128,512]{1,0:T(8,128)S(1)}, u32[]{:S(2)}, u32[]{:S(2)}) collective-permute-start(f32[128,512]{1,0:T(8,128)S(1)} %strip_1A_1.1), channel_id=1, source_target_pairs={{0,4},{1,3},{4,8},{5,1},{8,12},{9,5},{12,14},{13,9},{14,10},{15,13... | collective-permute-start | bytes 786440 | tf_op jit(solution)/shard_map/ppermute | solution.py:269
  35.1 17.9 %collective-permute-start.10 = (f32[256,512]{1,0:T(8,128)S(1)}, f32[256,512]{1,0:T(8,128)S(1)}, u32[]{:S(2)}, u32[]{:S(2)}) collective-permute-start(f32[256,512]{1,0:T(8,128)S(1)} %strip_3B_1.1), channel_id=1, source_target_pairs={{0,1},{1,0},{4,5},{5,4},{8,9},{9,8},{12,13},{13,12},{14,15},{15,14... | collective-permute-start | bytes 1572872 | tf_op jit(solution)/shard_map/ppermute | solution.py:269
  43.9 9.4 %collective-permute-start.14 = (f32[256,512]{1,0:T(8,128)S(1)}, f32[256,512]{1,0:T(8,128)S(1)}, u32[]{:S(2)}, u32[]{:S(2)}) collective-permute-start(f32[256,512]{1,0:T(8,128)S(1)} %strip_2A_1.1), channel_id=1, source_target_pairs={{0,4},{1,3},{4,8},{5,1},{8,12},{9,5},{12,14},{13,9},{14,10},{15,13... | collective-permute-start | bytes 1572872 | tf_op jit(solution)/shard_map/ppermute | solution.py:269
  47.9 8.7 %collective-permute-start = (f32[256,640]{1,0:T(8,128)S(1)}, f32[256,640]{1,0:T(8,128)S(1)}, u32[]{:S(2)}, u32[]{:S(2)}) collective-permute-start(f32[256,640]{1,0:T(8,128)S(1)} %strip_4B_0.1), channel_id=1, source_target_pairs={{0,1},{1,0},{4,5},{5,4},{8,9},{9,8},{12,13},{13,12},{14,15},{15,14... | collective-permute-start | bytes 1966088 | tf_op jit(solution)/shard_map/ppermute | solution.py:269
  49.9 10.6 %collective-permute-start.6 = (f32[256,640]{1,0:T(8,128)S(1)}, f32[256,640]{1,0:T(8,128)S(1)}, u32[]{:S(2)}, u32[]{:S(2)}) collective-permute-start(f32[256,640]{1,0:T(8,128)S(1)} %strip_3A_0.1), channel_id=1, source_target_pairs={{0,4},{1,3},{4,8},{5,1},{8,12},{9,5},{12,14},{13,9},{14,10},{15,13... | collective-permute-start | bytes 1966088 | tf_op jit(solution)/shard_map/ppermute | solution.py:269
  53.0 11.2 %collective-permute-start.9 = (f32[256,512]{1,0:T(8,128)S(1)}, f32[256,512]{1,0:T(8,128)S(1)}, u32[]{:S(2)}, u32[]{:S(2)}) collective-permute-start(f32[256,512]{1,0:T(8,128)S(1)} %strip_4B_1.1), channel_id=1, source_target_pairs={{0,1},{1,0},{4,5},{5,4},{8,9},{9,8},{12,13},{13,12},{14,15},{15,14... | collective-permute-start | bytes 1572872 | tf_op jit(solution)/shard_map/ppermute | solution.py:269
  54.7 11.5 %collective-permute-start.15 = (f32[256,512]{1,0:T(8,128)S(1)}, f32[256,512]{1,0:T(8,128)S(1)}, u32[]{:S(2)}, u32[]{:S(2)}) collective-permute-start(f32[256,512]{1,0:T(8,128)S(1)} %strip_3A_1.1), channel_id=1, source_target_pairs={{0,4},{1,3},{4,8},{5,1},{8,12},{9,5},{12,14},{13,9},{14,10},{15,13... | collective-permute-start | bytes 1572872 | tf_op jit(solution)/shard_map/ppermute | solution.py:269
  62.5 10.7 %collective-permute-start.7 = (f32[256,640]{1,0:T(8,128)S(1)}, f32[256,640]{1,0:T(8,128)S(1)}, u32[]{:S(2)}, u32[]{:S(2)}) collective-permute-start(f32[256,640]{1,0:T(8,128)S(1)} %strip_4A_0.1), channel_id=1, source_target_pairs={{0,4},{1,3},{4,8},{5,1},{8,12},{9,5},{12,14},{13,9},{14,10},{15,13... | collective-permute-start | bytes 1966088 | tf_op jit(solution)/shard_map/ppermute | solution.py:269
  67.6 11.2 %collective-permute-start.16 = (f32[256,512]{1,0:T(8,128)S(1)}, f32[256,512]{1,0:T(8,128)S(1)}, u32[]{:S(2)}, u32[]{:S(2)}) collective-permute-start(f32[256,512]{1,0:T(8,128)S(1)} %strip_4A_1.1), channel_id=1, source_target_pairs={{0,4},{1,3},{4,8},{5,1},{8,12},{9,5},{12,14},{13,9},{14,10},{15,13... | collective-permute-start | bytes 1572872 | tf_op jit(solution)/shard_map/ppermute | solution.py:269
  75.1 9.4 %collective-permute-start.8 = (f32[256,640]{1,0:T(8,128)S(1)}, f32[256,640]{1,0:T(8,128)S(1)}, u32[]{:S(2)}, u32[]{:S(2)}) collective-permute-start(f32[256,640]{1,0:T(8,128)S(1)} %strip_5_0.1.mine), channel_id=1, source_target_pairs={{0,1},{1,0},{4,5},{5,4},{8,9},{9,8},{12,13},{13,12},{14,15},{15,14... | collective-permute-start | bytes 1966088 | tf_op jit(solution)/shard_map/ppermute | solution.py:269
  80.2 2.0 %collective-permute-start.17 = (f32[256,512]{1,0:T(8,128)S(1)}, f32[256,512]{1,0:T(8,128)S(1)}, u32[]{:S(2)}, u32[]{:S(2)}) collective-permute-start(f32[256,512]{1,0:T(8,128)S(1)} %strip_5_1.1.mine), channel_id=1, source_target_pairs={{0,1},{1,0},{4,5},{5,4},{8,9},{9,8},{12,13},{13,12},{14,15},{15,14... | collective-permute-start | bytes 1572872 | tf_op jit(solution)/shard_map/ppermute | solution.py:269
  82.8 7.8 %collective-permute-start.21 = (f32[256,128]{1,0:T(8,128)S(1)}, f32[256,128]{1,0:T(8,128)S(1)}, u32[]{:S(2)}, u32[]{:S(2)}) collective-permute-start(f32[256,128]{1,0:T(8,128)S(1)} %get-tuple-element.24), channel_id=1, source_target_pairs={{0,4},{1,5},{4,8},{5,9},{8,12},{9,13},{12,14},{13,15},{14,10},{15,... | collective-permute-start | bytes 393224 | tf_op jit(solution)/shard_map/ppermute | solution.py:269
  85.1 16.0 %collective-permute-start.19 = (f32[256,128]{1,0:T(8,128)S(1)}, f32[256,128]{1,0:T(8,128)S(1)}, u32[]{:S(2)}, u32[]{:S(2)}) collective-permute-start(f32[256,128]{1,0:T(8,128)S(1)} %get-tuple-element.22), channel_id=1, source_target_pairs={{0,12},{1,13},{4,14},{5,15},{8,10},{9,11},{12,6},{13,7},{14,2},{15... | collective-permute-start | bytes 393224 | tf_op jit(solution)/shard_map/ppermute | solution.py:269
  88.8 12.3 %collective-permute-start.20 = (f32[256,128]{1,0:T(8,128)S(1)}, f32[256,128]{1,0:T(8,128)S(1)}, u32[]{:S(2)}, u32[]{:S(2)}) collective-permute-start(f32[256,128]{1,0:T(8,128)S(1)} %get-tuple-element.23), channel_id=1, source_target_pairs={{0,8},{1,9},{4,12},{5,13},{8,14},{9,15},{12,10},{13,11},{14,6},{15... | collective-permute-start | bytes 393224 | tf_op jit(solution)/shard_map/ppermute | solution.py:269
  88.8 9.0 %collective-permute-start.18 = (f32[128,128]{1,0:T(8,128)S(1)}, f32[128,128]{1,0:T(8,128)S(1)}, u32[]{:S(2)}, u32[]{:S(2)}) collective-permute-start(f32[128,128]{1,0:T(8,128)S(1)} %get-tuple-element.21), channel_id=1, source_target_pairs={{0,14},{1,15},{4,10},{5,11},{8,6},{9,7},{12,2},{13,3},{14,1},{15,0... | collective-permute-start | bytes 196616 | tf_op jit(solution)/shard_map/ppermute | solution.py:269

commit v2 on v0

v2 whole, which is shorter than its diff:
```python
import functools

import jax
import jax.numpy as jnp
import numpy as np
from jax import lax
from jax.experimental import pallas as pl
from jax.experimental.pallas import tpu as pltpu
from jax.sharding import PartitionSpec as P

F32 = jnp.float32
BF16 = jnp.bfloat16
MIB = 1 << 20
CHIPS = 8
SUB = 128
TWO = 2 * SUB


def prep_kernel(scale, block_hbm, mass_hbm, x_hbm, xh, xl, wh, wl, x, table, both, block_of, mass, sems, small):
    rows, order = x_hbm.shape
    nodes, _, classes = mass.shape
    first = [pltpu.make_async_copy(block_hbm, block_of, small.at[0]), pltpu.make_async_copy(mass_hbm, mass, small.at[1])]
    for copy in first:
        copy.start()
    per_element = rows // block_of.shape[0]
    bands, _, band = both.shape
    wide = order // PIECES
    copies = []
    for b in range(bands):
        for h in range(PIECES):
            at = (pl.ds(b * band, band), pl.ds(h * wide, wide))
            copy = pltpu.make_async_copy(x_hbm.at[at], x.at[at], sems.at[PIECES * b + h])
            copy.start()
            copies.append(copy)
    for copy in first:
        copy.wait()
    row = lax.broadcasted_iota(jnp.int32, (8, band), 0)
    column = lax.broadcasted_iota(jnp.int32, (8, band), 1)
    here = [[(row % nodes == i) & (column % nodes == j) for j in range(nodes)] for i in range(nodes)]
    for k in range(classes):
        tile = jnp.zeros((8, band), F32)
        for i in range(nodes):
            for j in range(nodes):
                tile = jnp.where(here[i][j], mass[i, j, k] * scale, tile)
        table[8 * k : 8 * k + 8, :] = tile
    for b in range(bands):
        for g in range(0, band // 8, 2):
            tiles = []
            for e in (g, g + 1):
                kind = block_of[(b * band + 8 * e) // per_element]
                tile = table[pl.ds(pl.multiple_of(kind * 8, 8), 8), :]
                tiles.append(jnp.where((row + 8 * e) // nodes == column // nodes, tile, 0.0))
            tile = jnp.concatenate(tiles, axis=0)
            high = tile.astype(BF16)
            both[b, 8 * g : 8 * g + 16, :] = high
            both[b, band + 8 * g : band + 8 * g + 16, :] = (tile - high.astype(F32)).astype(BF16)
    dot = functools.partial(jnp.dot, preferred_element_type=F32)
    for b in range(bands):
        for h in range(PIECES):
            copies[PIECES * b + h].wait()
            at = (pl.ds(b * band, band), pl.ds(h * wide, wide))
            value = x[at]
            high = value.astype(BF16)
            low = (value - high.astype(F32)).astype(BF16)
            xh[at] = high
            xl[at] = low
            weighted = dot(both[b], high)
            weighted = weighted[:band] + weighted[band:] + dot(both[b, :band], low)
            high = weighted.astype(BF16)
            wh[at] = high
            wl[at] = (weighted - high.astype(F32)).astype(BF16)


PIECES = 1


def prepare(snapshots, block_of, mass_table, scale):
    rows, order = snapshots.shape
    band = TWO
    bands = rows // band
    smem = pl.BlockSpec(memory_space=pltpu.SMEM)
    vmem = pl.BlockSpec(memory_space=pltpu.VMEM)
    return pl.pallas_call(
        functools.partial(prep_kernel, scale),
        out_shape=[pltpu.VMEM((rows, order), BF16)] * 4,
        in_specs=[pl.BlockSpec(memory_space=pl.ANY)] * 3,
        out_specs=[vmem] * 4,
        scratch_shapes=[
            pltpu.VMEM((rows, order), F32),
            pltpu.VMEM((8 * mass_table.shape[0], band), F32),
            pltpu.VMEM((bands, 2 * band, band), BF16),
            pltpu.SMEM(block_of.shape, jnp.int32),
            pltpu.SMEM(mass_table.shape[1:] + mass_table.shape[:1], F32),
            pltpu.SemaphoreType.DMA((PIECES * bands,)),
            pltpu.SemaphoreType.DMA((2,)),
        ],
        compiler_params=pltpu.CompilerParams(vmem_limit_bytes=32 * MIB),
        cost_estimate=pl.CostEstimate(
            flops=6 * rows * order * band, bytes_accessed=6 * rows * order, transcendentals=0
        ),
        name="weighting",
    )(*(pltpu.with_memory_space_constraint(x, pltpu.HBM) for x in (block_of, mass_table.transpose(1, 2, 0), snapshots)))


LHS, K0, K1, K2, K3, K4A, K4B = range(7)
FAR, NEAR = (K4A, K3, K2), (K1, K0)
FULL = FAR + NEAR
COST = 5000000000.0
COSTS = {'strip_4A_far': 0.02, 'strip_4A_near': 10, 'strip_5_far': 0.02, 'strip_5_near': 3, 'total_far': 0.1, 'total_near': 0.02, 'add_own': 0.02, 'place_far': 3}
CHAIN = 1
INSTANCES = {name: 7 * i for i, name in enumerate(("1A", "1B", "2A", "2B", "3A", "3B", "4A", "4B", "5"))}
CORE, R1, R2, R3, R4, FOUR = range(63, 69)
TABLE = 69


def ring_chip(p):
    p %= CHIPS
    return 2 * p if p < 4 else 2 * (CHIPS - 1 - p) + 1


def ring_device(p, core):
    return 2 * ring_chip(p) + core


def pair(q, k):
    return q + (((2, 1, -1), (-2, 3, -3))[q % 2][k - 1])


def fourth(q, r):
    return r if q % CHIPS < 4 else 1 - r


def position_table():
    table = np.zeros((2 * CHIPS, TABLE), np.int32)

    def strip(q, half=None):
        at = TWO * ring_chip(q)
        cols = [TWO * ring_chip(pair(q, k) if k else q) for k in range(4)]
        fours = [TWO * ring_chip(q + 4) + SUB * fourth(q, r) for r in range(2)]
        if half is None:
            return [at] + cols + fours
        return [at + SUB * half] + cols + [fours[half]] * 2

    for p in range(CHIPS):
        for c in range(2):
            sign = 1 - 2 * c
            row = strip(p + 4, c) + strip(p + 4, 1 - c)
            for step in (2, 3, 4):
                row += strip(p + sign * (5 - step)) + strip(p - sign * (5 - step))
            row += strip(p)
            row += [SUB * c] + [TWO * ring_chip(q) for k in (1, 2, 3) for q in range(CHIPS) if pair(q, k) % CHIPS == p]
            row += [TWO * ring_chip(p + 4) + SUB * (c if (p + 4) % CHIPS < 4 else 1 - c)]
            row += [strip(p, c)[K4A]]
            table[ring_device(p, c)] = row
    return table


def width_of(k):
    return SUB if k == K4A else TWO


def in_order(kernel, out_shape, operands, spaces, after, name, **kwargs):
    if after is not None:
        operands, spaces = operands + [after], spaces + [pl.ANY]
        inner, count = kernel, len(operands)
        kernel = lambda *refs: inner(*refs[: count - 1], *refs[count:])
    outs = pl.pallas_call(
        kernel,
        out_shape=out_shape,
        in_specs=[pl.BlockSpec(memory_space=s) for s in spaces],
        out_specs=[pl.BlockSpec(memory_space=pltpu.VMEM)] * len(out_shape),
        compiler_params=pltpu.CompilerParams(vmem_limit_bytes=20 * MIB),
        cost_estimate=pl.CostEstimate(flops=int(COST * COSTS.get(name, 1)), bytes_accessed=0, transcendentals=0),
        name=name,
        **kwargs,
    )(*operands)
    return list(outs)


def strip_kernel(base, height, group, names, table, xh, xl, wh, wl, *refs):
    ins, out = refs[:-1], refs[-1]

    def entry(i):
        return pl.multiple_of(table[base + i], SUB)

    def dot(a, b):
        return jnp.dot(a, b, preferred_element_type=F32)

    rows = pl.ds(entry(LHS), height)
    ah, al = xh[:, rows].T, xl[:, rows].T
    c = 0
    for k in group:
        w = width_of(k)
        pieces = [(0, height, entry(k))]
        if k == K4A:
            pieces = [(SUB * r, SUB, entry(K4A + r)) for r in range(height // SUB)]
        for r, n, at in pieces:
            bh, bl = wh[:, pl.ds(at, w)], wl[:, pl.ds(at, w)]
            lh, ll = ah[r : r + n], al[r : r + n]
            value = dot(lh, bh) + dot(lh, bl) + dot(ll, bh)
            for name, ref in zip(names, ins):
                if name == "same":
                    c0 = ref.shape[1] - out.shape[1] + c if group == NEAR else c
                    value = value + ref[r : r + n, c0 : c0 + w]
            out[r : r + n, c : c + w] = value
        c += w
    for name, ref in zip(names, ins):
        if name == "half":
            rows = pl.ds(pl.multiple_of(table[CORE], SUB), SUB)
            out[rows, :] = out[rows, :] + ref[...]


def strip(name, group, height, operands, table, after, same=(), half=()):
    names = ("same",) * len(same) + ("half",) * len(half)
    pinned = [pltpu.with_memory_space_constraint(x, pltpu.VMEM) for x in operands]
    return in_order(
        functools.partial(strip_kernel, INSTANCES[name], height, group, names),
        [jax.ShapeDtypeStruct((height, sum(map(width_of, group))), F32)],
        [pltpu.with_memory_space_constraint(table, pltpu.SMEM), *pinned, *same, *half],
        [pltpu.SMEM] + [pltpu.VMEM] * (4 + len(names)),
        after,
        name=f"strip_{name}" + ("" if group == FULL else "_far" if group == FAR else "_near"),
    )[0]


def sum_kernel(own, came, out):
    out[...] = own[:, own.shape[1] - out.shape[1] :] + came[...]


def add_own(own, came, after):
    return in_order(
        sum_kernel,
        [jax.ShapeDtypeStruct(came.shape, F32)],
        [own, came],
        [pltpu.VMEM] * 2,
        after,
        name="add_own",
    )[0]


def total_kernel(far, table, *refs):
    terms, own, sends = (refs[:4], refs[4], refs[5:]) if far else (refs[:2], refs[2], refs[3:])
    core = pl.multiple_of(table[CORE], SUB)

    def add(rows, at, n):
        values = [ref[rows, pl.ds(at, n)] for ref in terms]
        return (values[0] + values[1]) + (values[2] + values[3]) if far else values[0] + values[1]

    own[...] = add(pl.ds(core, SUB), 0, own.shape[1])
    if far:
        sends[0][...] = own[:, 0:SUB]
    at = (SUB, SUB + TWO) if far else (0,)
    for out, c0 in zip(sends[1:] if far else sends, at):
        out[...] = add(slice(None), pl.multiple_of(core + c0, SUB), SUB)


def total(far, table, after, *terms):
    blocks = [(SUB, terms[-1].shape[1])]
    blocks += [(SUB, SUB), (TWO, SUB), (TWO, SUB)] if far else [(TWO, SUB)]
    return in_order(
        functools.partial(total_kernel, far),
        [jax.ShapeDtypeStruct(b, F32) for b in blocks],
        [pltpu.with_memory_space_constraint(table, pltpu.SMEM), *terms],
        [pltpu.SMEM] + [pltpu.VMEM] * len(terms),
        after,
        name="total_far" if far else "total_near",
    )


def place_kernel(far, table, *refs):
    own, *got = refs[: 4 if far else 2]
    out, turned, sems = refs[-3:]
    base = INSTANCES["5"]
    copies = []

    def put(entry, source):
        columns = pl.ds(pl.multiple_of(table[entry], SUB), source.shape[1])
        copy = pltpu.make_async_copy(source, out.at[:, columns], sems.at[len(copies)])
        copy.start()
        copies.append(copy)

    if far:
        put(FOUR, own.at[:, 0:SUB])
    c = SUB if far else 0
    for k in (K3, K2) if far else (K1, K0):
        put(base + k, own.at[:, c : c + TWO])
        c += TWO
    c = 0
    for entry, ref in zip((R4, R3, R2) if far else (R1,), got):
        w = ref.shape[0]
        turned[:, c : c + w] = ref[...].T
        put(entry, turned.at[:, c : c + w])
        c += w
    for copy in copies:
        copy.wait()


def place(table, rest, own, *got, order, after):
    far = rest is None
    name = "place_far" if far else "place_near"
    operands = [pltpu.with_memory_space_constraint(table, pltpu.SMEM), own, *got]
    spaces = [pltpu.SMEM] + [pltpu.VMEM] * (1 + len(got))
    kernel, aliases = functools.partial(place_kernel, far), {}
    if not far:
        operands, spaces, aliases = operands + [rest], spaces + [pl.ANY], {len(operands): 0}
    if after is not None:
        operands, spaces = operands + [after], spaces + [pl.ANY]
    return pl.pallas_call(
        kernel,
        out_shape=jax.ShapeDtypeStruct((SUB, order), F32),
        in_specs=[pl.BlockSpec(memory_space=s) for s in spaces],
        out_specs=pl.BlockSpec(memory_space=pl.ANY),
        scratch_shapes=[
            pltpu.VMEM((SUB, sum(g.shape[0] for g in got)), F32),
            pltpu.SemaphoreType.DMA((6,)),
        ],
        input_output_aliases=aliases,
        compiler_params=pltpu.CompilerParams(vmem_limit_bytes=20 * MIB),
        cost_estimate=pl.CostEstimate(flops=int(COST * COSTS.get(name, 1)), bytes_accessed=0, transcendentals=0),
        name=name,
    )(*operands)


def ring_gram(snapshots, block_of, mass_table, axis):
    rows, order = snapshots.shape
    ring, swap, fours = [], [], []
    far = {1: [], 2: [], 3: []}
    for p in range(CHIPS):
        for c in range(2):
            here = ring_device(p, c)
            ring.append((here, ring_device(p + 1 - 2 * c, c)))
            swap.append((here, ring_device(p, 1 - c)))
            fours.append((here, ring_device(p + 4, fourth(p, c))))
            for k in far:
                far[k].append((here, ring_device(pair(p, k), c)))
    table = jnp.asarray(position_table())[lax.axis_index(axis)]
    operands = prepare(snapshots, block_of, mass_table, 1.0 / (rows * 2 * CHIPS))
    send = lambda x, pairs: lax.ppermute(x, axis, pairs)
    compute = lambda name, group, height, *rest, **adds: strip(
        name, group, height, operands, table, *rest, **adds
    )

    b = compute("1B", FULL, SUB, None)
    o = send(b, swap)
    last = compute("2B", FULL, TWO, b)
    o2 = send(last, swap)
    a_far = compute("1A", FAR, SUB, last, same=(o,))
    last = compute("1A", NEAR, SUB, a_far, same=(o,))
    r_far, r_near = send(a_far, ring), send(last, ring)
    o = o2
    for step in (2, 3, 4):
        if step < 4:
            last = b = compute(f"{step + 1}B", FULL, TWO, last)
        elif CHAIN == 3:
            last = b = compute("5", FAR, TWO, last)
        after_far = ((o,), (r_far,)) if step == 2 else ((o, r_far), ())
        last = a_far = compute(f"{step}A", FAR, TWO, last, *after_far)
        if step == 4 and CHAIN == 1:
            last = b = compute("5", FAR, TWO, last)
        after_near = ((o,), (r_near,)) if step == 2 else ((o, r_near), ())
        last = a_near = compute(f"{step}A", NEAR, TWO, last, *after_near)
        if step == 4 and CHAIN == 2:
            last = b = compute("5", FAR, TWO, last)
        r_far, r_near = send(a_far, ring), send(a_near, ring)
        o = send(b, swap)
    last = b_near = compute("5", NEAR, TWO, last)
    own_far, *sends = total(True, table, last, b, o, r_far, send(r_far, swap))
    got = [send(sends[0], fours), send(sends[1], far[3]), send(sends[2], far[2])]
    near = add_own(b_near, r_near, own_far)
    own_near, sent = total(False, table, None, near, send(near, swap))
    got_near = send(sent, far[1])
    out = place(table, None, own_far, *got, order=order, after=own_near)
    return place(table, out, own_near, got_near, order=order, after=None)


def scattered_gram(snapshots, block_of, mass_table, axis):
    rows, order = snapshots.shape
    xh, xl, wh, wl = prepare(snapshots, block_of, mass_table, 1.0 / (rows * lax.axis_size(axis)))

    def dot(a, b):
        return lax.dot_general(a, b, (((0,), (0,)), ((), ())), preferred_element_type=F32)

    return lax.psum_scatter(
        dot(xh, wh) + (dot(xh, wl) + dot(xl, wh)), axis, scatter_dimension=0, tiled=True
    )


def per_device(snapshots, block_of, mass_table):
    axis = "space"
    ring = lax.axis_size(axis) == 2 * CHIPS and snapshots.shape[1] == 2 * CHIPS * SUB
    form = ring_gram if ring else scattered_gram
    return form(snapshots, block_of, mass_table, axis)


def solution(mesh):
    return jax.shard_map(
        per_device,
        mesh=mesh,
        in_specs=(P(("groups", "space"), None), P(("groups", "space")), P()),
        out_specs=P(("groups", "space"), None),
        check_vma=False,
    )
```

time: 275 us -> 83.4 us (0.30)
  the two profiles are of different devices: /device:TPU:0 before, /device:TPU:19 now
where the time goes in v2:
time: 83.4 us; the launch traced here: 83.2 us
  Pallas kernels  33.1 us (40%)
  waiting for transfers between devices  29.8 us (36%)
  starting transfers between devices  19.3 us (23%)
    ppermute x19, waiting for transfers between devices, ring_gram(): send = lambda x, pairs: lax.ppermute(x, axis, pairs)  29.8 us
    pallas_call x17, Pallas kernels, in_order(): pl.pallas_call(kernel, out_shape=out_shape, in_specs=[pl.BlockSpec(memory...  25.5 us
    ppermute x19, starting transfers between devices, ring_gram(): send = lambda x, pairs: lax.ppermute(x, axis, pairs)  19.3 us
    pallas_call x1, Pallas kernels, prepare(): pl.pallas_call(functools.partial(prep_kernel, scale), out_shape=[pltpu.VM...  4.8 us
    pallas_call x2, Pallas kernels, place(): pl.pallas_call(kernel, out_shape=jax.ShapeDtypeStruct((SUB, order), F32),...  2.78 us
  transfers between devices with their start and end apart: 19, of which 7 were waited for; matrix products, arithmetic and copies ran while one was open for 0% of the time, Pallas kernels for 30%

profile of v2, /device:TPU:19, one launch (start us, length us, event | category | flops | bytes accessed | tf_op | source)
XLA Modules:
  0.0 83.2 jit_solution(12631519010071225736)
XLA Ops:
  0.7 4.8 %weighting.1 = (bf16[768,2048]{1,0:T(8,128)(2,1)S(1)}, bf16[768,2048]{1,0:T(8,128)(2,1)S(1)}, bf16[768,2048]{1,0:T(8,128)(2,1)S(1)}, bf16[768,2048]{1,0:T(8,128)(2,1)S(1)}) custom-call(s32[16]{0:T(128)} %block_hbm.1, f32[4,4,8]{2,1,0:T(4,128)} %bitcast.3, f32[768,2048]{1,0:T(8,128)} %x_hbm.1), custom_call_target="tpu_custom_call" | custom-call | flops 2415919104 | bytes 9437184 | tf_op jit(solution)/shard_map/weighting/pallas_call | solution.py:83
  5.5 1.6 %strip_1B.1.refs_5_ = f32[128,1152]{1,0:T(8,128)S(1)} custom-call(s32[69]{0:T(128)S(1)} %dynamic-slice_bitcast_fusion.table.refs_0_, bf16[768,2048]{1,0:T(8,128)(2,1)S(1)} %get-tuple-element.15.xh.refs_1_, bf16[768,2048]{1,0:T(8,128)(2,1)S(1)} %get-tuple-element.16.xl.refs_2_, bf16[768,2048]{1,0:T(8,128)(2,1)S(1)} %get-tuple-element.17.wh.refs_3_, ...), custom_call_target="tpu_custom_call" | custom-call | flops 5000000000 | tf_op jit(solution)/shard_map/strip_1B/pallas_call | solution.py:167
  7.9 2.4 %strip_2B.1.refs_6_ = f32[256,1152]{1,0:T(8,128)S(1)} custom-call(s32[69]{0:T(128)S(1)} %dynamic-slice_bitcast_fusion.table.refs_0_, bf16[768,2048]{1,0:T(8,128)(2,1)S(1)} %get-tuple-element.15.xh.refs_1_, bf16[768,2048]{1,0:T(8,128)(2,1)S(1)} %get-tuple-element.16.xl.refs_2_, bf16[768,2048]{1,0:T(8,128)(2,1)S(1)} %get-tuple-element.17.wh.refs_3_, ...), custom_call_target="tpu_custom_call" | custom-call | flops 5000000000 | tf_op jit(solution)/shard_map/strip_2B/pallas_call | solution.py:167
  13.3 2.4 %strip_3B.1.refs_7_ = f32[256,1152]{1,0:T(8,128)S(1)} custom-call(s32[69]{0:T(128)S(1)} %dynamic-slice_bitcast_fusion.table.refs_0_, bf16[768,2048]{1,0:T(8,128)(2,1)S(1)} %get-tuple-element.15.xh.refs_1_, bf16[768,2048]{1,0:T(8,128)(2,1)S(1)} %get-tuple-element.16.xl.refs_2_, bf16[768,2048]{1,0:T(8,128)(2,1)S(1)} %get-tuple-element.17.wh.refs_3_, ...), custom_call_target="tpu_custom_call" | custom-call | flops 5000000000 | tf_op jit(solution)/shard_map/strip_3B/pallas_call | solution.py:167
  15.8 3.3 %collective-permute-start.5 = (f32[256,1152]{1,0:T(8,128)S(1)}, f32[256,1152]{1,0:T(8,128)S(1)}, u32[]{:S(2)}, u32[]{:S(2)}) collective-permute-start(f32[256,1152]{1,0:T(8,128)S(1)} %strip_3B.1.refs_7_), channel_id=1, source_target_pairs={{0,1},{1,0},{4,5},{5,4},{8,9},{9,8},{12,13},{13,12},{14,15},{15,14... | collective-permute-start | bytes 3538952 | tf_op jit(solution)/shard_map/ppermute | solution.py:338
  19.1 1.8 %strip_2A_far.1.refs_7_ = f32[256,640]{1,0:T(8,128)S(1)} custom-call(s32[69]{0:T(128)S(1)} %dynamic-slice_bitcast_fusion.table.refs_0_, bf16[768,2048]{1,0:T(8,128)(2,1)S(1)} %get-tuple-element.15.xh.refs_1_, bf16[768,2048]{1,0:T(8,128)(2,1)S(1)} %get-tuple-element.16.xl.refs_2_, bf16[768,2048]{1,0:T(8,128)(2,1)S(1)} %get-tuple-element.17.wh.refs_3_, ...), custom_call_target="tpu_custom_call" | custom-call | flops 5000000000 | tf_op jit(solution)/shard_map/strip_2A_far/pallas_call | solution.py:167
  21.2 1.4 %strip_2A_near.1.refs_5_ = f32[256,512]{1,0:T(8,128)S(1)} custom-call(s32[69]{0:T(128)S(1)} %dynamic-slice_bitcast_fusion.table.refs_0_, bf16[768,2048]{1,0:T(8,128)(2,1)S(1)} %get-tuple-element.15.xh.refs_1_, bf16[768,2048]{1,0:T(8,128)(2,1)S(1)} %get-tuple-element.16.xl.refs_2_, bf16[768,2048]{1,0:T(8,128)(2,1)S(1)} %get-tuple-element.17.wh.refs_3_, ...), custom_call_target="tpu_custom_call" | custom-call | flops 5000000000 | tf_op jit(solution)/shard_map/strip_2A_near/pallas_call | solution.py:167
  23.0 2.4 %strip_4B.1.refs_7_ = f32[256,1152]{1,0:T(8,128)S(1)} custom-call(s32[69]{0:T(128)S(1)} %dynamic-slice_bitcast_fusion.table.refs_0_, bf16[768,2048]{1,0:T(8,128)(2,1)S(1)} %get-tuple-element.15.xh.refs_1_, bf16[768,2048]{1,0:T(8,128)(2,1)S(1)} %get-tuple-element.16.xl.refs_2_, bf16[768,2048]{1,0:T(8,128)(2,1)S(1)} %get-tuple-element.17.wh.refs_3_, ...), custom_call_target="tpu_custom_call" | custom-call | flops 5000000000 | tf_op jit(solution)/shard_map/strip_4B/pallas_call | solution.py:167
  25.5 3.0 %collective-permute-start.4 = (f32[256,1152]{1,0:T(8,128)S(1)}, f32[256,1152]{1,0:T(8,128)S(1)}, u32[]{:S(2)}, u32[]{:S(2)}) collective-permute-start(f32[256,1152]{1,0:T(8,128)S(1)} %strip_4B.1.refs_7_), channel_id=1, source_target_pairs={{0,1},{1,0},{4,5},{5,4},{8,9},{9,8},{12,13},{13,12},{14,15},{15,14... | collective-permute-start | bytes 3538952 | tf_op jit(solution)/shard_map/ppermute | solution.py:338
  28.4 2.3 %collective-permute-done.7.refs_6_ = f32[256,640]{1,0:T(8,128)S(1)} collective-permute-done((f32[256,640]{1,0:T(8,128)S(1)}, f32[256,640]{1,0:T(8,128)S(1)}, u32[]{:S(2)}, u32[]{:S(2)}) %collective-permute-start.7) | collective-permute-done | bytes 655392 | tf_op jit(solution)/shard_map/ppermute | solution.py:338
  30.7 1.8 %strip_3A_far.1.refs_7_ = f32[256,640]{1,0:T(8,128)S(1)} custom-call(s32[69]{0:T(128)S(1)} %dynamic-slice_bitcast_fusion.table.refs_0_, bf16[768,2048]{1,0:T(8,128)(2,1)S(1)} %get-tuple-element.15.xh.refs_1_, bf16[768,2048]{1,0:T(8,128)(2,1)S(1)} %get-tuple-element.16.xl.refs_2_, bf16[768,2048]{1,0:T(8,128)(2,1)S(1)} %get-tuple-element.17.wh.refs_3_, ...), custom_call_target="tpu_custom_call" | custom-call | flops 5000000000 | tf_op jit(solution)/shard_map/strip_3A_far/pallas_call | solution.py:167
  32.8 3.5 %collective-permute-done.6.refs_6_ = f32[256,512]{1,0:T(8,128)S(1)} collective-permute-done((f32[256,512]{1,0:T(8,128)S(1)}, f32[256,512]{1,0:T(8,128)S(1)}, u32[]{:S(2)}, u32[]{:S(2)}) %collective-permute-start.6) | collective-permute-done | bytes 524320 | tf_op jit(solution)/shard_map/ppermute | solution.py:338
  36.3 1.4 %strip_3A_near.1.refs_7_ = f32[256,512]{1,0:T(8,128)S(1)} custom-call(s32[69]{0:T(128)S(1)} %dynamic-slice_bitcast_fusion.table.refs_0_, bf16[768,2048]{1,0:T(8,128)(2,1)S(1)} %get-tuple-element.15.xh.refs_1_, bf16[768,2048]{1,0:T(8,128)(2,1)S(1)} %get-tuple-element.16.xl.refs_2_, bf16[768,2048]{1,0:T(8,128)(2,1)S(1)} %get-tuple-element.17.wh.refs_3_, ...), custom_call_target="tpu_custom_call" | custom-call | flops 5000000000 | tf_op jit(solution)/shard_map/strip_3A_near/pallas_call | solution.py:167
  38.0 5.4 %collective-permute-done.9.refs_6_ = f32[256,640]{1,0:T(8,128)S(1)} collective-permute-done((f32[256,640]{1,0:T(8,128)S(1)}, f32[256,640]{1,0:T(8,128)S(1)}, u32[]{:S(2)}, u32[]{:S(2)}) %collective-permute-start.9) | collective-permute-done | bytes 655392 | tf_op jit(solution)/shard_map/ppermute | solution.py:338
  43.3 1.8 %strip_4A_far.1.refs_5_ = f32[256,640]{1,0:T(8,128)S(1)} custom-call(s32[69]{0:T(128)S(1)} %dynamic-slice_bitcast_fusion.table.refs_0_, bf16[768,2048]{1,0:T(8,128)(2,1)S(1)} %get-tuple-element.15.xh.refs_1_, bf16[768,2048]{1,0:T(8,128)(2,1)S(1)} %get-tuple-element.16.xl.refs_2_, bf16[768,2048]{1,0:T(8,128)(2,1)S(1)} %get-tuple-element.17.wh.refs_3_, ...), custom_call_target="tpu_custom_call" | custom-call | flops 100000000 | tf_op jit(solution)/shard_map/strip_4A_far/pallas_call | solution.py:167
  45.4 1.8 %strip_5_far.1.refs_7_.refs_1_ = f32[256,640]{1,0:T(8,128)S(1)} custom-call(s32[69]{0:T(128)S(1)} %dynamic-slice_bitcast_fusion.table.refs_0_, bf16[768,2048]{1,0:T(8,128)(2,1)S(1)} %get-tuple-element.15.xh.refs_1_, bf16[768,2048]{1,0:T(8,128)(2,1)S(1)} %get-tuple-element.16.xl.refs_2_, bf16[768,2048]{1,0:T(8,128)(2,1)S(1)} %get-tuple-element.17.wh.refs_3_, ...), custom_call_target="tpu_custom_call" | custom-call | flops 100000000 | tf_op jit(solution)/shard_map/strip_5_far/pallas_call | solution.py:167
  47.3 2.5 %collective-permute-start.11 = (f32[256,640]{1,0:T(8,128)S(1)}, f32[256,640]{1,0:T(8,128)S(1)}, u32[]{:S(2)}, u32[]{:S(2)}) collective-permute-start(f32[256,640]{1,0:T(8,128)S(1)} %strip_5_far.1.refs_7_.refs_1_), channel_id=1, source_target_pairs={{0,1},{1,0},{4,5},{5,4},{8,9},{9,8},{12,13},{13,12},{14,15},{15,14... | collective-permute-start | bytes 1966088 | tf_op jit(solution)/shard_map/ppermute | solution.py:338
  49.8 1.4 %strip_4A_near.1.refs_5_ = f32[256,512]{1,0:T(8,128)S(1)} custom-call(s32[69]{0:T(128)S(1)} %dynamic-slice_bitcast_fusion.table.refs_0_, bf16[768,2048]{1,0:T(8,128)(2,1)S(1)} %get-tuple-element.15.xh.refs_1_, bf16[768,2048]{1,0:T(8,128)(2,1)S(1)} %get-tuple-element.16.xl.refs_2_, bf16[768,2048]{1,0:T(8,128)(2,1)S(1)} %get-tuple-element.17.wh.refs_3_, ...), custom_call_target="tpu_custom_call" | custom-call | flops 49999998976 | tf_op jit(solution)/shard_map/strip_4A_near/pallas_call | solution.py:167
  51.4 4.6 %collective-permute-done.12.refs_3_ = f32[256,640]{1,0:T(8,128)S(1)} collective-permute-done((f32[256,640]{1,0:T(8,128)S(1)}, f32[256,640]{1,0:T(8,128)S(1)}, u32[]{:S(2)}, u32[]{:S(2)}) %collective-permute-start.12) | collective-permute-done | bytes 655392 | tf_op jit(solution)/shard_map/ppermute | solution.py:338
  57.1 1.4 %strip_5_near.1.refs_5_.refs_0_ = f32[256,512]{1,0:T(8,128)S(1)} custom-call(s32[69]{0:T(128)S(1)} %dynamic-slice_bitcast_fusion.table.refs_0_, bf16[768,2048]{1,0:T(8,128)(2,1)S(1)} %get-tuple-element.15.xh.refs_1_, bf16[768,2048]{1,0:T(8,128)(2,1)S(1)} %get-tuple-element.16.xl.refs_2_, bf16[768,2048]{1,0:T(8,128)(2,1)S(1)} %get-tuple-element.17.wh.refs_3_, ...), custom_call_target="tpu_custom_call" | custom-call | flops 15000000512 | tf_op jit(solution)/shard_map/strip_5_near/pallas_call | solution.py:167
  59.5 2.1 %collective-permute-done.10.refs_1_ = f32[256,512]{1,0:T(8,128)S(1)} collective-permute-done((f32[256,512]{1,0:T(8,128)S(1)}, f32[256,512]{1,0:T(8,128)S(1)}, u32[]{:S(2)}, u32[]{:S(2)}) %collective-permute-start.10) | collective-permute-done | bytes 524320 | tf_op jit(solution)/shard_map/ppermute | solution.py:338
  64.1 3.3 %collective-permute-start.16 = (f32[128,128]{1,0:T(8,128)S(1)}, f32[128,128]{1,0:T(8,128)S(1)}, u32[]{:S(2)}, u32[]{:S(2)}) collective-permute-start(f32[128,128]{1,0:T(8,128)S(1)} %get-tuple-element.22), channel_id=1, source_target_pairs={{0,14},{1,15},{4,10},{5,11},{8,6},{9,7},{12,2},{13,3},{14,1},{15,0... | collective-permute-start | bytes 196616 | tf_op jit(solution)/shard_map/ppermute | solution.py:338
  68.7 11.5 %collective-permute-done.16.refs_1_ = f32[128,128]{1,0:T(8,128)S(1)} collective-permute-done((f32[128,128]{1,0:T(8,128)S(1)}, f32[128,128]{1,0:T(8,128)S(1)}, u32[]{:S(2)}, u32[]{:S(2)}) %collective-permute-start.16) | collective-permute-done | bytes 65568 | tf_op jit(solution)/shard_map/ppermute | solution.py:338
  80.2 1.4 %place_far.1.refs_2_ = f32[128,2048]{1,0:T(8,128)} custom-call(s32[69]{0:T(128)S(1)} %dynamic-slice_bitcast_fusion.table.refs_0_, f32[128,640]{1,0:T(8,128)S(1)} %get-tuple-element.19.refs_2_.refs_0_, f32[128,128]{1,0:T(8,128)S(1)} %collective-permute-done.16.refs_1_, f32[256,128]{1,0:T(8,128)S(1)} %collective-permute-done.17.refs_2_, ...), custom_call_target="tpu_custom_call" | custom-call | flops 15000000512 | tf_op jit(solution)/shard_map/place_far/pallas_call | solution.py:308
  (35 shorter events, 13.4 us)
Async XLA Ops:
  7.1 3.3 %collective-permute-start.1 = (f32[128,1152]{1,0:T(8,128)S(1)}, f32[128,1152]{1,0:T(8,128)S(1)}, u32[]{:S(2)}, u32[]{:S(2)}) collective-permute-start(f32[128,1152]{1,0:T(8,128)S(1)} %strip_1B.1.refs_5_), channel_id=1, source_target_pairs={{0,1},{1,0},{4,5},{5,4},{8,9},{9,8},{12,13},{13,12},{14,15},{15,14... | collective-permute-start | bytes 1769480 | tf_op jit(solution)/shard_map/ppermute | solution.py:338
  10.3 8.8 %collective-permute-start = (f32[256,1152]{1,0:T(8,128)S(1)}, f32[256,1152]{1,0:T(8,128)S(1)}, u32[]{:S(2)}, u32[]{:S(2)}) collective-permute-start(f32[256,1152]{1,0:T(8,128)S(1)} %strip_2B.1.refs_6_), channel_id=1, source_target_pairs={{0,1},{1,0},{4,5},{5,4},{8,9},{9,8},{12,13},{13,12},{14,15},{15,14... | collective-permute-start | bytes 3538952 | tf_op jit(solution)/shard_map/ppermute | solution.py:338
  11.7 7.4 %collective-permute-start.3 = (f32[128,640]{1,0:T(8,128)S(1)}, f32[128,640]{1,0:T(8,128)S(1)}, u32[]{:S(2)}, u32[]{:S(2)}) collective-permute-start(f32[128,640]{1,0:T(8,128)S(1)} %strip_1A_far.1.refs_6_), channel_id=1, source_target_pairs={{0,4},{1,3},{4,8},{5,1},{8,12},{9,5},{12,14},{13,9},{14,10},{15,13... | collective-permute-start | bytes 983048 | tf_op jit(solution)/shard_map/ppermute | solution.py:338
  13.1 8.1 %collective-permute-start.2 = (f32[128,512]{1,0:T(8,128)S(1)}, f32[128,512]{1,0:T(8,128)S(1)}, u32[]{:S(2)}, u32[]{:S(2)}) collective-permute-start(f32[128,512]{1,0:T(8,128)S(1)} %strip_1A_near.1.refs_5_), channel_id=1, source_target_pairs={{0,4},{1,3},{4,8},{5,1},{8,12},{9,5},{12,14},{13,9},{14,10},{15,13... | collective-permute-start | bytes 786440 | tf_op jit(solution)/shard_map/ppermute | solution.py:338
  15.8 12.7 %collective-permute-start.5 = (f32[256,1152]{1,0:T(8,128)S(1)}, f32[256,1152]{1,0:T(8,128)S(1)}, u32[]{:S(2)}, u32[]{:S(2)}) collective-permute-start(f32[256,1152]{1,0:T(8,128)S(1)} %strip_3B.1.refs_7_), channel_id=1, source_target_pairs={{0,1},{1,0},{4,5},{5,4},{8,9},{9,8},{12,13},{13,12},{14,15},{15,14... | collective-permute-start | bytes 3538952 | tf_op jit(solution)/shard_map/ppermute | solution.py:338
  20.9 9.8 %collective-permute-start.7 = (f32[256,640]{1,0:T(8,128)S(1)}, f32[256,640]{1,0:T(8,128)S(1)}, u32[]{:S(2)}, u32[]{:S(2)}) collective-permute-start(f32[256,640]{1,0:T(8,128)S(1)} %strip_2A_far.1.refs_7_), channel_id=1, source_target_pairs={{0,4},{1,3},{4,8},{5,1},{8,12},{9,5},{12,14},{13,9},{14,10},{15,13... | collective-permute-start | bytes 1966088 | tf_op jit(solution)/shard_map/ppermute | solution.py:338
  22.6 13.7 %collective-permute-start.6 = (f32[256,512]{1,0:T(8,128)S(1)}, f32[256,512]{1,0:T(8,128)S(1)}, u32[]{:S(2)}, u32[]{:S(2)}) collective-permute-start(f32[256,512]{1,0:T(8,128)S(1)} %strip_2A_near.1.refs_5_), channel_id=1, source_target_pairs={{0,4},{1,3},{4,8},{5,1},{8,12},{9,5},{12,14},{13,9},{14,10},{15,13... | collective-permute-start | bytes 1572872 | tf_op jit(solution)/shard_map/ppermute | solution.py:338
  25.5 12.5 %collective-permute-start.4 = (f32[256,1152]{1,0:T(8,128)S(1)}, f32[256,1152]{1,0:T(8,128)S(1)}, u32[]{:S(2)}, u32[]{:S(2)}) collective-permute-start(f32[256,1152]{1,0:T(8,128)S(1)} %strip_4B.1.refs_7_), channel_id=1, source_target_pairs={{0,1},{1,0},{4,5},{5,4},{8,9},{9,8},{12,13},{13,12},{14,15},{15,14... | collective-permute-start | bytes 3538952 | tf_op jit(solution)/shard_map/ppermute | solution.py:338
  32.5 10.8 %collective-permute-start.9 = (f32[256,640]{1,0:T(8,128)S(1)}, f32[256,640]{1,0:T(8,128)S(1)}, u32[]{:S(2)}, u32[]{:S(2)}) collective-permute-start(f32[256,640]{1,0:T(8,128)S(1)} %strip_3A_far.1.refs_7_), channel_id=1, source_target_pairs={{0,4},{1,3},{4,8},{5,1},{8,12},{9,5},{12,14},{13,9},{14,10},{15,13... | collective-permute-start | bytes 1966088 | tf_op jit(solution)/shard_map/ppermute | solution.py:338
  37.7 12.1 %collective-permute-start.8 = (f32[256,512]{1,0:T(8,128)S(1)}, f32[256,512]{1,0:T(8,128)S(1)}, u32[]{:S(2)}, u32[]{:S(2)}) collective-permute-start(f32[256,512]{1,0:T(8,128)S(1)} %strip_3A_near.1.refs_7_), channel_id=1, source_target_pairs={{0,4},{1,3},{4,8},{5,1},{8,12},{9,5},{12,14},{13,9},{14,10},{15,13... | collective-permute-start | bytes 1572872 | tf_op jit(solution)/shard_map/ppermute | solution.py:338
  45.2 10.8 %collective-permute-start.12 = (f32[256,640]{1,0:T(8,128)S(1)}, f32[256,640]{1,0:T(8,128)S(1)}, u32[]{:S(2)}, u32[]{:S(2)}) collective-permute-start(f32[256,640]{1,0:T(8,128)S(1)} %strip_4A_far.1.refs_5_), channel_id=1, source_target_pairs={{0,4},{1,3},{4,8},{5,1},{8,12},{9,5},{12,14},{13,9},{14,10},{15,13... | collective-permute-start | bytes 1966088 | tf_op jit(solution)/shard_map/ppermute | solution.py:338
  47.3 11.2 %collective-permute-start.11 = (f32[256,640]{1,0:T(8,128)S(1)}, f32[256,640]{1,0:T(8,128)S(1)}, u32[]{:S(2)}, u32[]{:S(2)}) collective-permute-start(f32[256,640]{1,0:T(8,128)S(1)} %strip_5_far.1.refs_7_.refs_1_), channel_id=1, source_target_pairs={{0,1},{1,0},{4,5},{5,4},{8,9},{9,8},{12,13},{13,12},{14,15},{15,14... | collective-permute-start | bytes 1966088 | tf_op jit(solution)/shard_map/ppermute | solution.py:338
  51.2 10.4 %collective-permute-start.10 = (f32[256,512]{1,0:T(8,128)S(1)}, f32[256,512]{1,0:T(8,128)S(1)}, u32[]{:S(2)}, u32[]{:S(2)}) collective-permute-start(f32[256,512]{1,0:T(8,128)S(1)} %strip_4A_near.1.refs_5_), channel_id=1, source_target_pairs={{0,4},{1,3},{4,8},{5,1},{8,12},{9,5},{12,14},{13,9},{14,10},{15,13... | collective-permute-start | bytes 1572872 | tf_op jit(solution)/shard_map/ppermute | solution.py:338
  56.0 2.8 %collective-permute-start.13 = (f32[256,640]{1,0:T(8,128)S(1)}, f32[256,640]{1,0:T(8,128)S(1)}, u32[]{:S(2)}, u32[]{:S(2)}) collective-permute-start(f32[256,640]{1,0:T(8,128)S(1)} %collective-permute-done.12.refs_3_), channel_id=1, source_target_pairs={{0,1},{1,0},{4,5},{5,4},{8,9},{9,8},{12,13},{13,12},{14,15},{15,14... | collective-permute-start | bytes 1966088 | tf_op jit(solution)/shard_map/ppermute | solution.py:338
  61.7 5.8 %collective-permute-start.14 = (f32[256,512]{1,0:T(8,128)S(1)}, f32[256,512]{1,0:T(8,128)S(1)}, u32[]{:S(2)}, u32[]{:S(2)}) collective-permute-start(f32[256,512]{1,0:T(8,128)S(1)} %add_own.1.refs_0_), channel_id=1, source_target_pairs={{0,1},{1,0},{4,5},{5,4},{8,9},{9,8},{12,13},{13,12},{14,15},{15,14... | collective-permute-start | bytes 1572872 | tf_op jit(solution)/shard_map/ppermute | solution.py:338
  62.8 17.4 %collective-permute-start.17 = (f32[256,128]{1,0:T(8,128)S(1)}, f32[256,128]{1,0:T(8,128)S(1)}, u32[]{:S(2)}, u32[]{:S(2)}) collective-permute-start(f32[256,128]{1,0:T(8,128)S(1)} %get-tuple-element.23), channel_id=1, source_target_pairs={{0,2},{1,3},{4,6},{5,7},{8,4},{9,5},{12,0},{13,1},{14,12},{15,13},... | collective-permute-start | bytes 393224 | tf_op jit(solution)/shard_map/ppermute | solution.py:338
  63.0 17.3 %collective-permute-start.18 = (f32[256,128]{1,0:T(8,128)S(1)}, f32[256,128]{1,0:T(8,128)S(1)}, u32[]{:S(2)}, u32[]{:S(2)}) collective-permute-start(f32[256,128]{1,0:T(8,128)S(1)} %get-tuple-element.24), channel_id=1, source_target_pairs={{0,4},{1,5},{4,14},{5,15},{8,12},{9,13},{12,6},{13,7},{14,10},{15,... | collective-permute-start | bytes 393224 | tf_op jit(solution)/shard_map/ppermute | solution.py:338
  64.1 16.1 %collective-permute-start.16 = (f32[128,128]{1,0:T(8,128)S(1)}, f32[128,128]{1,0:T(8,128)S(1)}, u32[]{:S(2)}, u32[]{:S(2)}) collective-permute-start(f32[128,128]{1,0:T(8,128)S(1)} %get-tuple-element.22), channel_id=1, source_target_pairs={{0,14},{1,15},{4,10},{5,11},{8,6},{9,7},{12,2},{13,3},{14,1},{15,0... | collective-permute-start | bytes 196616 | tf_op jit(solution)/shard_map/ppermute | solution.py:338
  68.1 13.6 %collective-permute-start.15 = (f32[256,128]{1,0:T(8,128)S(1)}, f32[256,128]{1,0:T(8,128)S(1)}, u32[]{:S(2)}, u32[]{:S(2)}) collective-permute-start(f32[256,128]{1,0:T(8,128)S(1)} %get-tuple-element.21), channel_id=1, source_target_pairs={{0,8},{1,9},{4,2},{5,3},{8,14},{9,15},{12,4},{13,5},{14,6},{15,7},... | collective-permute-start | bytes 393224 | tf_op jit(solution)/shard_map/ppermute | solution.py:338

commit v3 on v2

--- a/solution.py
+++ b/solution.py
@@ -122,8 +122,11 @@
     return 2 * ring_chip(p) + core
 
 
+PAIRS = ((7, 3, 0, 2, 5, 6, 4, 1), (1, 2, 5, 6, 3, 7, 0, 4), (5, 6, 4, 0, 1, 3, 7, 2))
+
+
 def pair(q, k):
-    return q + (((2, 1, -1), (-2, 3, -3))[q % 2][k - 1])
+    return PAIRS[k - 1][q % CHIPS]
 
 
 def fourth(q, r):
@@ -267,10 +270,11 @@
     )
 
 
-def place_kernel(far, table, *refs):
-    own, *got = refs[: 4 if far else 2]
-    out, turned, sems = refs[-3:]
-    base = INSTANCES["5"]
+SENT = {K4A: 4, K3: 3, K2: 2, K1: 1}
+
+
+def place_kernel(table, far, near, *refs):
+    got, (out, turned, sems) = refs[: len(SENT)], refs[len(SENT) :]
     copies = []
 
     def put(entry, source):
@@ -279,46 +283,36 @@
         copy.start()
         copies.append(copy)
 
-    if far:
-        put(FOUR, own.at[:, 0:SUB])
-    c = SUB if far else 0
-    for k in (K3, K2) if far else (K1, K0):
-        put(base + k, own.at[:, c : c + TWO])
-        c += TWO
+    for group, own in ((FAR, far), (NEAR, near)):
+        c = 0
+        for k in group:
+            put(FOUR if k == K4A else INSTANCES["5"] + k, own.at[:, c : c + width_of(k)])
+            c += width_of(k)
     c = 0
-    for entry, ref in zip((R4, R3, R2) if far else (R1,), got):
+    for k, ref in zip(SENT, got):
         w = ref.shape[0]
         turned[:, c : c + w] = ref[...].T
-        put(entry, turned.at[:, c : c + w])
+        put(R1 + SENT[k] - 1, turned.at[:, c : c + w])
         c += w
     for copy in copies:
         copy.wait()
 
 
-def place(table, rest, own, *got, order, after):
-    far = rest is None
-    name = "place_far" if far else "place_near"
-    operands = [pltpu.with_memory_space_constraint(table, pltpu.SMEM), own, *got]
-    spaces = [pltpu.SMEM] + [pltpu.VMEM] * (1 + len(got))
-    kernel, aliases = functools.partial(place_kernel, far), {}
-    if not far:
-        operands, spaces, aliases = operands + [rest], spaces + [pl.ANY], {len(operands): 0}
-    if after is not None:
-        operands, spaces = operands + [after], spaces + [pl.ANY]
+def place(table, far, near, *got, order):
     return pl.pallas_call(
-        kernel,
+        place_kernel,
         out_shape=jax.ShapeDtypeStruct((SUB, order), F32),
-        in_specs=[pl.BlockSpec(memory_space=s) for s in spaces],
+        in_specs=[pl.BlockSpec(memory_space=pltpu.SMEM)]
+        + [pl.BlockSpec(memory_space=pltpu.VMEM)] * (2 + len(got)),
         out_specs=pl.BlockSpec(memory_space=pl.ANY),
         scratch_shapes=[
             pltpu.VMEM((SUB, sum(g.shape[0] for g in got)), F32),
-            pltpu.SemaphoreType.DMA((6,)),
+            pltpu.SemaphoreType.DMA((9,)),
         ],
-        input_output_aliases=aliases,
         compiler_params=pltpu.CompilerParams(vmem_limit_bytes=20 * MIB),
-        cost_estimate=pl.CostEstimate(flops=int(COST * COSTS.get(name, 1)), bytes_accessed=0, transcendentals=0),
-        name=name,
-    )(*operands)
+        cost_estimate=pl.CostEstimate(flops=int(COST), bytes_accessed=0, transcendentals=0),
+        name="place",
+    )(pltpu.with_memory_space_constraint(table, pltpu.SMEM), far, near, *got)
 
 
 def ring_gram(snapshots, block_of, mass_table, axis):
@@ -369,8 +363,7 @@
     near = add_own(b_near, r_near, own_far)
     own_near, sent = total(False, table, None, near, send(near, swap))
     got_near = send(sent, far[1])
-    out = place(table, None, own_far, *got, order=order, after=own_near)
-    return place(table, out, own_near, got_near, order=order, after=None)
+    return place(table, own_far, own_near, *got, got_near, order=order)
 
 
 def scattered_gram(snapshots, block_of, mass_table, axis):

time: 83.4 us -> 80.5 us (0.965)
  the two profiles are of different devices: /device:TPU:19 before, /device:TPU:0 now
where the time goes in v3:
time: 80.5 us; the launch traced here: 79.6 us
  Pallas kernels  31.9 us (40%)
  starting transfers between devices  24.4 us (30%)
  waiting for transfers between devices  22.2 us (28%)
    pallas_call x17, Pallas kernels, in_order(): pl.pallas_call(kernel, out_shape=out_shape, in_specs=[pl.BlockSpec(memory...  25.5 us
    ppermute x19, starting transfers between devices, ring_gram(): send = lambda x, pairs: lax.ppermute(x, axis, pairs)  24.4 us
    ppermute x19, waiting for transfers between devices, ring_gram(): send = lambda x, pairs: lax.ppermute(x, axis, pairs)  22.2 us
    pallas_call x1, Pallas kernels, prepare(): pl.pallas_call(functools.partial(prep_kernel, scale), out_shape=[pltpu.VM...  4.81 us
  transfers between devices with their start and end apart: 19, of which 9 were waited for; matrix products, arithmetic and copies ran while one was open for 0% of the time, Pallas kernels for 30%

profile of v3, /device:TPU:0, one launch (start us, length us, event | category | flops | bytes accessed | tf_op | source)
XLA Modules:
  0.0 79.6 jit_solution(13936673689090401025)
XLA Ops:
  0.7 4.8 %weighting.1 = (bf16[768,2048]{1,0:T(8,128)(2,1)S(1)}, bf16[768,2048]{1,0:T(8,128)(2,1)S(1)}, bf16[768,2048]{1,0:T(8,128)(2,1)S(1)}, bf16[768,2048]{1,0:T(8,128)(2,1)S(1)}) custom-call(s32[16]{0:T(128)} %block_hbm.1, f32[4,4,8]{2,1,0:T(4,128)} %bitcast.3, f32[768,2048]{1,0:T(8,128)} %x_hbm.1), custom_call_target="tpu_custom_call" | custom-call | flops 2415919104 | bytes 9437184 | tf_op jit(solution)/shard_map/weighting/pallas_call | solution.py:83
  7.6 2.4 %strip_2B.1.refs_6_ = f32[256,1152]{1,0:T(8,128)S(1)} custom-call(s32[69]{0:T(128)S(1)} %dynamic-slice_bitcast_fusion.table.refs_0_, bf16[768,2048]{1,0:T(8,128)(2,1)S(1)} %get-tuple-element.15.xh.refs_1_, bf16[768,2048]{1,0:T(8,128)(2,1)S(1)} %get-tuple-element.16.xl.refs_2_, bf16[768,2048]{1,0:T(8,128)(2,1)S(1)} %get-tuple-element.17.wh.refs_3_, ...), custom_call_target="tpu_custom_call" | custom-call | flops 5000000000 | tf_op jit(solution)/shard_map/strip_2B/pallas_call | solution.py:170
  11.5 3.0 %collective-permute-start.3 = (f32[128,640]{1,0:T(8,128)S(1)}, f32[128,640]{1,0:T(8,128)S(1)}, u32[]{:S(2)}, u32[]{:S(2)}) collective-permute-start(f32[128,640]{1,0:T(8,128)S(1)} %strip_1A_far.1.refs_6_), channel_id=1, source_target_pairs={{0,4},{1,3},{4,8},{5,1},{8,12},{9,5},{12,14},{13,9},{14,10},{15,13... | collective-permute-start | bytes 983048 | tf_op jit(solution)/shard_map/ppermute | solution.py:332
  17.4 2.4 %strip_3B.1.refs_7_ = f32[256,1152]{1,0:T(8,128)S(1)} custom-call(s32[69]{0:T(128)S(1)} %dynamic-slice_bitcast_fusion.table.refs_0_, bf16[768,2048]{1,0:T(8,128)(2,1)S(1)} %get-tuple-element.15.xh.refs_1_, bf16[768,2048]{1,0:T(8,128)(2,1)S(1)} %get-tuple-element.16.xl.refs_2_, bf16[768,2048]{1,0:T(8,128)(2,1)S(1)} %get-tuple-element.17.wh.refs_3_, ...), custom_call_target="tpu_custom_call" | custom-call | flops 5000000000 | tf_op jit(solution)/shard_map/strip_3B/pallas_call | solution.py:170
  19.9 1.9 %strip_2A_far.1.refs_7_ = f32[256,640]{1,0:T(8,128)S(1)} custom-call(s32[69]{0:T(128)S(1)} %dynamic-slice_bitcast_fusion.table.refs_0_, bf16[768,2048]{1,0:T(8,128)(2,1)S(1)} %get-tuple-element.15.xh.refs_1_, bf16[768,2048]{1,0:T(8,128)(2,1)S(1)} %get-tuple-element.16.xl.refs_2_, bf16[768,2048]{1,0:T(8,128)(2,1)S(1)} %get-tuple-element.17.wh.refs_3_, ...), custom_call_target="tpu_custom_call" | custom-call | flops 5000000000 | tf_op jit(solution)/shard_map/strip_2A_far/pallas_call | solution.py:170
  21.8 1.8 %collective-permute-start.6 = (f32[256,640]{1,0:T(8,128)S(1)}, f32[256,640]{1,0:T(8,128)S(1)}, u32[]{:S(2)}, u32[]{:S(2)}) collective-permute-start(f32[256,640]{1,0:T(8,128)S(1)} %strip_2A_far.1.refs_7_), channel_id=1, source_target_pairs={{0,4},{1,3},{4,8},{5,1},{8,12},{9,5},{12,14},{13,9},{14,10},{15,13... | collective-permute-start | bytes 1966088 | tf_op jit(solution)/shard_map/ppermute | solution.py:332
  24.9 1.8 %collective-permute-start.8 = (f32[256,512]{1,0:T(8,128)S(1)}, f32[256,512]{1,0:T(8,128)S(1)}, u32[]{:S(2)}, u32[]{:S(2)}) collective-permute-start(f32[256,512]{1,0:T(8,128)S(1)} %strip_2A_near.1.refs_5_), channel_id=1, source_target_pairs={{0,4},{1,3},{4,8},{5,1},{8,12},{9,5},{12,14},{13,9},{14,10},{15,13... | collective-permute-start | bytes 1572872 | tf_op jit(solution)/shard_map/ppermute | solution.py:332
  26.8 2.4 %strip_4B.1.refs_7_ = f32[256,1152]{1,0:T(8,128)S(1)} custom-call(s32[69]{0:T(128)S(1)} %dynamic-slice_bitcast_fusion.table.refs_0_, bf16[768,2048]{1,0:T(8,128)(2,1)S(1)} %get-tuple-element.15.xh.refs_1_, bf16[768,2048]{1,0:T(8,128)(2,1)S(1)} %get-tuple-element.16.xl.refs_2_, bf16[768,2048]{1,0:T(8,128)(2,1)S(1)} %get-tuple-element.17.wh.refs_3_, ...), custom_call_target="tpu_custom_call" | custom-call | flops 5000000000 | tf_op jit(solution)/shard_map/strip_4B/pallas_call | solution.py:170
  29.3 3.1 %collective-permute-done.6.refs_6_ = f32[256,640]{1,0:T(8,128)S(1)} collective-permute-done((f32[256,640]{1,0:T(8,128)S(1)}, f32[256,640]{1,0:T(8,128)S(1)}, u32[]{:S(2)}, u32[]{:S(2)}) %collective-permute-start.6) | collective-permute-done | bytes 655392 | tf_op jit(solution)/shard_map/ppermute | solution.py:332
  32.4 1.8 %strip_3A_far.1.refs_7_ = f32[256,640]{1,0:T(8,128)S(1)} custom-call(s32[69]{0:T(128)S(1)} %dynamic-slice_bitcast_fusion.table.refs_0_, bf16[768,2048]{1,0:T(8,128)(2,1)S(1)} %get-tuple-element.15.xh.refs_1_, bf16[768,2048]{1,0:T(8,128)(2,1)S(1)} %get-tuple-element.16.xl.refs_2_, bf16[768,2048]{1,0:T(8,128)(2,1)S(1)} %get-tuple-element.17.wh.refs_3_, ...), custom_call_target="tpu_custom_call" | custom-call | flops 5000000000 | tf_op jit(solution)/shard_map/strip_3A_far/pallas_call | solution.py:170
  34.2 1.8 %collective-permute-start.7 = (f32[256,640]{1,0:T(8,128)S(1)}, f32[256,640]{1,0:T(8,128)S(1)}, u32[]{:S(2)}, u32[]{:S(2)}) collective-permute-start(f32[256,640]{1,0:T(8,128)S(1)} %strip_3A_far.1.refs_7_), channel_id=1, source_target_pairs={{0,4},{1,3},{4,8},{5,1},{8,12},{9,5},{12,14},{13,9},{14,10},{15,13... | collective-permute-start | bytes 1966088 | tf_op jit(solution)/shard_map/ppermute | solution.py:332
  36.0 2.0 %collective-permute-done.8.refs_6_ = f32[256,512]{1,0:T(8,128)S(1)} collective-permute-done((f32[256,512]{1,0:T(8,128)S(1)}, f32[256,512]{1,0:T(8,128)S(1)}, u32[]{:S(2)}, u32[]{:S(2)}) %collective-permute-start.8) | collective-permute-done | bytes 524320 | tf_op jit(solution)/shard_map/ppermute | solution.py:332
  39.4 1.8 %collective-permute-start.12 = (f32[256,512]{1,0:T(8,128)S(1)}, f32[256,512]{1,0:T(8,128)S(1)}, u32[]{:S(2)}, u32[]{:S(2)}) collective-permute-start(f32[256,512]{1,0:T(8,128)S(1)} %strip_3A_near.1.refs_7_), channel_id=1, source_target_pairs={{0,4},{1,3},{4,8},{5,1},{8,12},{9,5},{12,14},{13,9},{14,10},{15,13... | collective-permute-start | bytes 1572872 | tf_op jit(solution)/shard_map/ppermute | solution.py:332
  41.2 3.9 %collective-permute-done.7.refs_6_ = f32[256,640]{1,0:T(8,128)S(1)} collective-permute-done((f32[256,640]{1,0:T(8,128)S(1)}, f32[256,640]{1,0:T(8,128)S(1)}, u32[]{:S(2)}, u32[]{:S(2)}) %collective-permute-start.7) | collective-permute-done | bytes 655392 | tf_op jit(solution)/shard_map/ppermute | solution.py:332
  45.0 1.8 %strip_4A_far.1.refs_5_ = f32[256,640]{1,0:T(8,128)S(1)} custom-call(s32[69]{0:T(128)S(1)} %dynamic-slice_bitcast_fusion.table.refs_0_, bf16[768,2048]{1,0:T(8,128)(2,1)S(1)} %get-tuple-element.15.xh.refs_1_, bf16[768,2048]{1,0:T(8,128)(2,1)S(1)} %get-tuple-element.16.xl.refs_2_, bf16[768,2048]{1,0:T(8,128)(2,1)S(1)} %get-tuple-element.17.wh.refs_3_, ...), custom_call_target="tpu_custom_call" | custom-call | flops 100000000 | tf_op jit(solution)/shard_map/strip_4A_far/pallas_call | solution.py:170
  46.9 1.8 %collective-permute-start.10 = (f32[256,640]{1,0:T(8,128)S(1)}, f32[256,640]{1,0:T(8,128)S(1)}, u32[]{:S(2)}, u32[]{:S(2)}) collective-permute-start(f32[256,640]{1,0:T(8,128)S(1)} %strip_4A_far.1.refs_5_), channel_id=1, source_target_pairs={{0,4},{1,3},{4,8},{5,1},{8,12},{9,5},{12,14},{13,9},{14,10},{15,13... | collective-permute-start | bytes 1966088 | tf_op jit(solution)/shard_map/ppermute | solution.py:332
  48.6 1.8 %strip_5_far.1.refs_7_.refs_1_ = f32[256,640]{1,0:T(8,128)S(1)} custom-call(s32[69]{0:T(128)S(1)} %dynamic-slice_bitcast_fusion.table.refs_0_, bf16[768,2048]{1,0:T(8,128)(2,1)S(1)} %get-tuple-element.15.xh.refs_1_, bf16[768,2048]{1,0:T(8,128)(2,1)S(1)} %get-tuple-element.16.xl.refs_2_, bf16[768,2048]{1,0:T(8,128)(2,1)S(1)} %get-tuple-element.17.wh.refs_3_, ...), custom_call_target="tpu_custom_call" | custom-call | flops 100000000 | tf_op jit(solution)/shard_map/strip_5_far/pallas_call | solution.py:170
  52.0 1.8 %collective-permute-start.13 = (f32[256,512]{1,0:T(8,128)S(1)}, f32[256,512]{1,0:T(8,128)S(1)}, u32[]{:S(2)}, u32[]{:S(2)}) collective-permute-start(f32[256,512]{1,0:T(8,128)S(1)} %strip_4A_near.1.refs_5_), channel_id=1, source_target_pairs={{0,4},{1,3},{4,8},{5,1},{8,12},{9,5},{12,14},{13,9},{14,10},{15,13... | collective-permute-start | bytes 1572872 | tf_op jit(solution)/shard_map/ppermute | solution.py:332
  53.8 3.9 %collective-permute-done.10.refs_3_ = f32[256,640]{1,0:T(8,128)S(1)} collective-permute-done((f32[256,640]{1,0:T(8,128)S(1)}, f32[256,640]{1,0:T(8,128)S(1)}, u32[]{:S(2)}, u32[]{:S(2)}) %collective-permute-start.10) | collective-permute-done | bytes 655392 | tf_op jit(solution)/shard_map/ppermute | solution.py:332
  60.5 2.8 %collective-permute-done.13.refs_1_ = f32[256,512]{1,0:T(8,128)S(1)} collective-permute-done((f32[256,512]{1,0:T(8,128)S(1)}, f32[256,512]{1,0:T(8,128)S(1)}, u32[]{:S(2)}, u32[]{:S(2)}) %collective-permute-start.13) | collective-permute-done | bytes 524320 | tf_op jit(solution)/shard_map/ppermute | solution.py:332
  63.4 3.7 %collective-permute-start.16 = (f32[256,128]{1,0:T(8,128)S(1)}, f32[256,128]{1,0:T(8,128)S(1)}, u32[]{:S(2)}, u32[]{:S(2)}) collective-permute-start(f32[256,128]{1,0:T(8,128)S(1)} %get-tuple-element.22), channel_id=1, source_target_pairs={{0,10},{1,11},{4,6},{5,7},{8,14},{9,15},{12,0},{13,1},{14,4},{15,5... | collective-permute-start | bytes 393224 | tf_op jit(solution)/shard_map/ppermute | solution.py:332
  67.8 1.9 %collective-permute-start.18 = (f32[256,128]{1,0:T(8,128)S(1)}, f32[256,128]{1,0:T(8,128)S(1)}, u32[]{:S(2)}, u32[]{:S(2)}) collective-permute-start(f32[256,128]{1,0:T(8,128)S(1)} %get-tuple-element.24), channel_id=1, source_target_pairs={{0,2},{1,3},{4,12},{5,13},{8,0},{9,1},{12,8},{13,9},{14,10},{15,11... | collective-permute-start | bytes 393224 | tf_op jit(solution)/shard_map/ppermute | solution.py:332
  69.7 2.5 %collective-permute-start.15 = (f32[128,128]{1,0:T(8,128)S(1)}, f32[128,128]{1,0:T(8,128)S(1)}, u32[]{:S(2)}, u32[]{:S(2)}) collective-permute-start(f32[128,128]{1,0:T(8,128)S(1)} %get-tuple-element.21), channel_id=1, source_target_pairs={{0,14},{1,15},{4,10},{5,11},{8,6},{9,7},{12,2},{13,3},{14,1},{15,0... | collective-permute-start | bytes 196616 | tf_op jit(solution)/shard_map/ppermute | solution.py:332
  72.2 4.8 %collective-permute-done.15.refs_0_ = f32[128,128]{1,0:T(8,128)S(1)} collective-permute-done((f32[128,128]{1,0:T(8,128)S(1)}, f32[128,128]{1,0:T(8,128)S(1)}, u32[]{:S(2)}, u32[]{:S(2)}) %collective-permute-start.15) | collective-permute-done | bytes 65568 | tf_op jit(solution)/shard_map/ppermute | solution.py:332
  (34 shorter events, 17.5 us)
Async XLA Ops:
  7.1 3.1 %collective-permute-start.1 = (f32[128,1152]{1,0:T(8,128)S(1)}, f32[128,1152]{1,0:T(8,128)S(1)}, u32[]{:S(2)}, u32[]{:S(2)}) collective-permute-start(f32[128,1152]{1,0:T(8,128)S(1)} %strip_1B.1.refs_5_), channel_id=1, source_target_pairs={{0,1},{1,0},{4,5},{5,4},{8,9},{9,8},{12,13},{13,12},{14,15},{15,14... | collective-permute-start | bytes 1769480 | tf_op jit(solution)/shard_map/ppermute | solution.py:332
  10.1 9.8 %collective-permute-start = (f32[256,1152]{1,0:T(8,128)S(1)}, f32[256,1152]{1,0:T(8,128)S(1)}, u32[]{:S(2)}, u32[]{:S(2)}) collective-permute-start(f32[256,1152]{1,0:T(8,128)S(1)} %strip_2B.1.refs_6_), channel_id=1, source_target_pairs={{0,1},{1,0},{4,5},{5,4},{8,9},{9,8},{12,13},{13,12},{14,15},{15,14... | collective-permute-start | bytes 3538952 | tf_op jit(solution)/shard_map/ppermute | solution.py:332
  11.5 8.4 %collective-permute-start.3 = (f32[128,640]{1,0:T(8,128)S(1)}, f32[128,640]{1,0:T(8,128)S(1)}, u32[]{:S(2)}, u32[]{:S(2)}) collective-permute-start(f32[128,640]{1,0:T(8,128)S(1)} %strip_1A_far.1.refs_6_), channel_id=1, source_target_pairs={{0,4},{1,3},{4,8},{5,1},{8,12},{9,5},{12,14},{13,9},{14,10},{15,13... | collective-permute-start | bytes 983048 | tf_op jit(solution)/shard_map/ppermute | solution.py:332
  15.7 7.8 %collective-permute-start.2 = (f32[128,512]{1,0:T(8,128)S(1)}, f32[128,512]{1,0:T(8,128)S(1)}, u32[]{:S(2)}, u32[]{:S(2)}) collective-permute-start(f32[128,512]{1,0:T(8,128)S(1)} %strip_1A_near.1.refs_5_), channel_id=1, source_target_pairs={{0,4},{1,3},{4,8},{5,1},{8,12},{9,5},{12,14},{13,9},{14,10},{15,13... | collective-permute-start | bytes 786440 | tf_op jit(solution)/shard_map/ppermute | solution.py:332
  19.8 9.5 %collective-permute-start.5 = (f32[256,1152]{1,0:T(8,128)S(1)}, f32[256,1152]{1,0:T(8,128)S(1)}, u32[]{:S(2)}, u32[]{:S(2)}) collective-permute-start(f32[256,1152]{1,0:T(8,128)S(1)} %strip_3B.1.refs_7_), channel_id=1, source_target_pairs={{0,1},{1,0},{4,5},{5,4},{8,9},{9,8},{12,13},{13,12},{14,15},{15,14... | collective-permute-start | bytes 3538952 | tf_op jit(solution)/shard_map/ppermute | solution.py:332
  21.8 10.6 %collective-permute-start.6 = (f32[256,640]{1,0:T(8,128)S(1)}, f32[256,640]{1,0:T(8,128)S(1)}, u32[]{:S(2)}, u32[]{:S(2)}) collective-permute-start(f32[256,640]{1,0:T(8,128)S(1)} %strip_2A_far.1.refs_7_), channel_id=1, source_target_pairs={{0,4},{1,3},{4,8},{5,1},{8,12},{9,5},{12,14},{13,9},{14,10},{15,13... | collective-permute-start | bytes 1966088 | tf_op jit(solution)/shard_map/ppermute | solution.py:332
  24.9 13.1 %collective-permute-start.8 = (f32[256,512]{1,0:T(8,128)S(1)}, f32[256,512]{1,0:T(8,128)S(1)}, u32[]{:S(2)}, u32[]{:S(2)}) collective-permute-start(f32[256,512]{1,0:T(8,128)S(1)} %strip_2A_near.1.refs_5_), channel_id=1, source_target_pairs={{0,4},{1,3},{4,8},{5,1},{8,12},{9,5},{12,14},{13,9},{14,10},{15,13... | collective-permute-start | bytes 1572872 | tf_op jit(solution)/shard_map/ppermute | solution.py:332
  29.2 12.0 %collective-permute-start.4 = (f32[256,1152]{1,0:T(8,128)S(1)}, f32[256,1152]{1,0:T(8,128)S(1)}, u32[]{:S(2)}, u32[]{:S(2)}) collective-permute-start(f32[256,1152]{1,0:T(8,128)S(1)} %strip_4B.1.refs_7_), channel_id=1, source_target_pairs={{0,1},{1,0},{4,5},{5,4},{8,9},{9,8},{12,13},{13,12},{14,15},{15,14... | collective-permute-start | bytes 3538952 | tf_op jit(solution)/shard_map/ppermute | solution.py:332
  34.2 10.8 %collective-permute-start.7 = (f32[256,640]{1,0:T(8,128)S(1)}, f32[256,640]{1,0:T(8,128)S(1)}, u32[]{:S(2)}, u32[]{:S(2)}) collective-permute-start(f32[256,640]{1,0:T(8,128)S(1)} %strip_3A_far.1.refs_7_), channel_id=1, source_target_pairs={{0,4},{1,3},{4,8},{5,1},{8,12},{9,5},{12,14},{13,9},{14,10},{15,13... | collective-permute-start | bytes 1966088 | tf_op jit(solution)/shard_map/ppermute | solution.py:332
  39.4 11.3 %collective-permute-start.12 = (f32[256,512]{1,0:T(8,128)S(1)}, f32[256,512]{1,0:T(8,128)S(1)}, u32[]{:S(2)}, u32[]{:S(2)}) collective-permute-start(f32[256,512]{1,0:T(8,128)S(1)} %strip_3A_near.1.refs_7_), channel_id=1, source_target_pairs={{0,4},{1,3},{4,8},{5,1},{8,12},{9,5},{12,14},{13,9},{14,10},{15,13... | collective-permute-start | bytes 1572872 | tf_op jit(solution)/shard_map/ppermute | solution.py:332
  46.9 10.8 %collective-permute-start.10 = (f32[256,640]{1,0:T(8,128)S(1)}, f32[256,640]{1,0:T(8,128)S(1)}, u32[]{:S(2)}, u32[]{:S(2)}) collective-permute-start(f32[256,640]{1,0:T(8,128)S(1)} %strip_4A_far.1.refs_5_), channel_id=1, source_target_pairs={{0,4},{1,3},{4,8},{5,1},{8,12},{9,5},{12,14},{13,9},{14,10},{15,13... | collective-permute-start | bytes 1966088 | tf_op jit(solution)/shard_map/ppermute | solution.py:332
  50.5 8.6 %collective-permute-start.9 = (f32[256,640]{1,0:T(8,128)S(1)}, f32[256,640]{1,0:T(8,128)S(1)}, u32[]{:S(2)}, u32[]{:S(2)}) collective-permute-start(f32[256,640]{1,0:T(8,128)S(1)} %strip_5_far.1.refs_7_.refs_1_), channel_id=1, source_target_pairs={{0,1},{1,0},{4,5},{5,4},{8,9},{9,8},{12,13},{13,12},{14,15},{15,14... | collective-permute-start | bytes 1966088 | tf_op jit(solution)/shard_map/ppermute | solution.py:332
  52.0 11.3 %collective-permute-start.13 = (f32[256,512]{1,0:T(8,128)S(1)}, f32[256,512]{1,0:T(8,128)S(1)}, u32[]{:S(2)}, u32[]{:S(2)}) collective-permute-start(f32[256,512]{1,0:T(8,128)S(1)} %strip_4A_near.1.refs_5_), channel_id=1, source_target_pairs={{0,4},{1,3},{4,8},{5,1},{8,12},{9,5},{12,14},{13,9},{14,10},{15,13... | collective-permute-start | bytes 1572872 | tf_op jit(solution)/shard_map/ppermute | solution.py:332
  57.7 2.1 %collective-permute-start.11 = (f32[256,640]{1,0:T(8,128)S(1)}, f32[256,640]{1,0:T(8,128)S(1)}, u32[]{:S(2)}, u32[]{:S(2)}) collective-permute-start(f32[256,640]{1,0:T(8,128)S(1)} %collective-permute-done.10.refs_3_), channel_id=1, source_target_pairs={{0,1},{1,0},{4,5},{5,4},{8,9},{9,8},{12,13},{13,12},{14,15},{15,14... | collective-permute-start | bytes 1966088 | tf_op jit(solution)/shard_map/ppermute | solution.py:332
  63.4 3.8 %collective-permute-start.14 = (f32[256,512]{1,0:T(8,128)S(1)}, f32[256,512]{1,0:T(8,128)S(1)}, u32[]{:S(2)}, u32[]{:S(2)}) collective-permute-start(f32[256,512]{1,0:T(8,128)S(1)} %add_own.1.refs_0_), channel_id=1, source_target_pairs={{0,1},{1,0},{4,5},{5,4},{8,9},{9,8},{12,13},{13,12},{14,15},{15,14... | collective-permute-start | bytes 1572872 | tf_op jit(solution)/shard_map/ppermute | solution.py:332
  63.4 13.5 %collective-permute-start.16 = (f32[256,128]{1,0:T(8,128)S(1)}, f32[256,128]{1,0:T(8,128)S(1)}, u32[]{:S(2)}, u32[]{:S(2)}) collective-permute-start(f32[256,128]{1,0:T(8,128)S(1)} %get-tuple-element.22), channel_id=1, source_target_pairs={{0,10},{1,11},{4,6},{5,7},{8,14},{9,15},{12,0},{13,1},{14,4},{15,5... | collective-permute-start | bytes 393224 | tf_op jit(solution)/shard_map/ppermute | solution.py:332
  67.2 10.7 %collective-permute-start.17 = (f32[256,128]{1,0:T(8,128)S(1)}, f32[256,128]{1,0:T(8,128)S(1)}, u32[]{:S(2)}, u32[]{:S(2)}) collective-permute-start(f32[256,128]{1,0:T(8,128)S(1)} %get-tuple-element.23), channel_id=1, source_target_pairs={{0,4},{1,5},{4,8},{5,9},{8,10},{9,11},{12,6},{13,7},{14,12},{15,13... | collective-permute-start | bytes 393224 | tf_op jit(solution)/shard_map/ppermute | solution.py:332
  67.8 10.1 %collective-permute-start.18 = (f32[256,128]{1,0:T(8,128)S(1)}, f32[256,128]{1,0:T(8,128)S(1)}, u32[]{:S(2)}, u32[]{:S(2)}) collective-permute-start(f32[256,128]{1,0:T(8,128)S(1)} %get-tuple-element.24), channel_id=1, source_target_pairs={{0,2},{1,3},{4,12},{5,13},{8,0},{9,1},{12,8},{13,9},{14,10},{15,11... | collective-permute-start | bytes 393224 | tf_op jit(solution)/shard_map/ppermute | solution.py:332
  69.7 7.3 %collective-permute-start.15 = (f32[128,128]{1,0:T(8,128)S(1)}, f32[128,128]{1,0:T(8,128)S(1)}, u32[]{:S(2)}, u32[]{:S(2)}) collective-permute-start(f32[128,128]{1,0:T(8,128)S(1)} %get-tuple-element.21), channel_id=1, source_target_pairs={{0,14},{1,15},{4,10},{5,11},{8,6},{9,7},{12,2},{13,3},{14,1},{15,0... | collective-permute-start | bytes 196616 | tf_op jit(solution)/shard_map/ppermute | solution.py:332

commit v4 on v3

--- a/solution.py
+++ b/solution.py
@@ -106,8 +106,7 @@
 FAR, NEAR = (K4A, K3, K2), (K1, K0)
 FULL = FAR + NEAR
 COST = 5000000000.0
-COSTS = {'strip_4A_far': 0.02, 'strip_4A_near': 10, 'strip_5_far': 0.02, 'strip_5_near': 3, 'total_far': 0.1, 'total_near': 0.02, 'add_own': 0.02, 'place_far': 3}
-CHAIN = 1
+COSTS = {"sum_4_far": 0.02, "sum_4_near": 10, "strip_5_far": 0.02, "strip_5_near": 3, "total_far": 0.1, "total_near": 0.02, "add_own": 0.02}
 INSTANCES = {name: 7 * i for i, name in enumerate(("1A", "1B", "2A", "2B", "3A", "3B", "4A", "4B", "5"))}
 CORE, R1, R2, R3, R4, FOUR = range(63, 69)
 TABLE = 69
@@ -156,6 +155,14 @@
             row += [strip(p, c)[K4A]]
             table[ring_device(p, c)] = row
     return table
+
+
+PACKED = ((K1, 0, 0, TWO, 0), (K1, SUB, 0, TWO, TWO), (K0, 0, 0, TWO, 2 * TWO), (K0, SUB, SUB, SUB, 3 * TWO))
+PACKED_SHAPE = (SUB, 3 * TWO + SUB)
+
+
+def near_column(k, c):
+    return c if k == K1 else TWO + c
 
 
 def width_of(k):
@@ -180,8 +187,9 @@
     return list(outs)
 
 
-def strip_kernel(base, height, group, names, table, xh, xl, wh, wl, *refs):
+def strip_kernel(base, height, group, names, pack, table, xh, xl, wh, wl, *refs):
     ins, out = refs[:-1], refs[-1]
+    width = sum(map(width_of, group))
 
     def entry(i):
         return pl.multiple_of(table[base + i], SUB)
@@ -203,22 +211,36 @@
             value = dot(lh, bh) + dot(lh, bl) + dot(ll, bh)
             for name, ref in zip(names, ins):
                 if name == "same":
-                    c0 = ref.shape[1] - out.shape[1] + c if group == NEAR else c
+                    c0 = ref.shape[1] - width + c if group == NEAR else c
                     value = value + ref[r : r + n, c0 : c0 + w]
-            out[r : r + n, c : c + w] = value
+            if not pack:
+                out[r : r + n, c : c + w] = value
+        if pack:
+            for _, r, c0, n, at in (p for p in PACKED if p[0] == k):
+                out[:, at : at + n] = value[r : r + SUB, c0 : c0 + n]
         c += w
     for name, ref in zip(names, ins):
-        if name == "half":
+        if name == "half" and pack:
+            for mine in range(2):
+
+                @pl.when(table[CORE] == SUB * mine)
+                def _():
+                    for k, r, c0, n, at in PACKED:
+                        if r == SUB * mine:
+                            c = near_column(k, c0)
+                            out[:, at : at + n] = out[:, at : at + n] + ref[:, c : c + n]
+
+        elif name == "half":
             rows = pl.ds(pl.multiple_of(table[CORE], SUB), SUB)
             out[rows, :] = out[rows, :] + ref[...]
 
 
-def strip(name, group, height, operands, table, after, same=(), half=()):
+def strip(name, group, height, operands, table, after, same=(), half=(), pack=False):
     names = ("same",) * len(same) + ("half",) * len(half)
     pinned = [pltpu.with_memory_space_constraint(x, pltpu.VMEM) for x in operands]
     return in_order(
-        functools.partial(strip_kernel, INSTANCES[name], height, group, names),
-        [jax.ShapeDtypeStruct((height, sum(map(width_of, group))), F32)],
+        functools.partial(strip_kernel, INSTANCES[name], height, group, names, pack),
+        [jax.ShapeDtypeStruct(PACKED_SHAPE if pack else (height, sum(map(width_of, group))), F32)],
         [pltpu.with_memory_space_constraint(table, pltpu.SMEM), *pinned, *same, *half],
         [pltpu.SMEM] + [pltpu.VMEM] * (4 + len(names)),
         after,
@@ -226,47 +248,76 @@
     )[0]
 
 
-def sum_kernel(own, came, out):
-    out[...] = own[:, own.shape[1] - out.shape[1] :] + came[...]
-
-
-def add_own(own, came, after):
+def sum_kernel(group, *refs):
+    *olds, came, out = refs
+    if group == FAR:
+        value = came[...]
+        for ref in olds:
+            value = value + ref[:, : out.shape[1]]
+        out[...] = value
+        return
+    for k, r, c0, n, at in PACKED:
+        value = came[:, at : at + n]
+        for ref in olds:
+            c = ref.shape[1] - 2 * TWO + near_column(k, c0)
+            value = value + ref[r : r + SUB, c : c + n]
+        out[:, at : at + n] = value
+
+
+def add_up(name, group, after, came, *olds):
     return in_order(
-        sum_kernel,
+        functools.partial(sum_kernel, group),
         [jax.ShapeDtypeStruct(came.shape, F32)],
-        [own, came],
-        [pltpu.VMEM] * 2,
+        [*olds, came],
+        [pltpu.VMEM] * (1 + len(olds)),
         after,
-        name="add_own",
+        name=name,
     )[0]
 
 
-def total_kernel(far, table, *refs):
-    terms, own, sends = (refs[:4], refs[4], refs[5:]) if far else (refs[:2], refs[2], refs[3:])
+def total_far_kernel(table, a, b, c, d, own, four, *sends):
     core = pl.multiple_of(table[CORE], SUB)
 
-    def add(rows, at, n):
-        values = [ref[rows, pl.ds(at, n)] for ref in terms]
-        return (values[0] + values[1]) + (values[2] + values[3]) if far else values[0] + values[1]
-
-    own[...] = add(pl.ds(core, SUB), 0, own.shape[1])
-    if far:
-        sends[0][...] = own[:, 0:SUB]
-    at = (SUB, SUB + TWO) if far else (0,)
-    for out, c0 in zip(sends[1:] if far else sends, at):
-        out[...] = add(slice(None), pl.multiple_of(core + c0, SUB), SUB)
-
-
-def total(far, table, after, *terms):
-    blocks = [(SUB, terms[-1].shape[1])]
-    blocks += [(SUB, SUB), (TWO, SUB), (TWO, SUB)] if far else [(TWO, SUB)]
+    def add(rows, columns):
+        return (a[rows, columns] + b[rows, columns]) + (c[rows, columns] + d[rows, columns])
+
+    own[...] = add(pl.ds(core, SUB), slice(None))
+    four[...] = own[:, 0:SUB]
+    for out, at in zip(sends, (SUB, SUB + TWO)):
+        out[...] = add(slice(None), pl.ds(pl.multiple_of(core + at, SUB), SUB))
+
+
+def total_near_kernel(table, a, b, own, sent):
+    core = pl.multiple_of(table[CORE], SUB)
+
+    def add(at, n):
+        columns = pl.ds(at, n)
+        return a[:, columns] + b[:, columns]
+
+    own[:, 0:TWO] = add(pl.multiple_of(2 * core, SUB), TWO)
+    for r in range(2):
+        sent[SUB * r : SUB * r + SUB, :] = add(pl.multiple_of(TWO * r + core, SUB), SUB)
+
+    @pl.when(core == 0)
+    def _():
+        own[:, TWO:] = add(2 * TWO, TWO)
+
+    @pl.when(core != 0)
+    def _():
+        own[:, TWO : TWO + SUB] = add(2 * TWO + SUB, SUB).T
+        own[:, TWO + SUB :] = add(3 * TWO, SUB)
+
+
+def total(group, table, after, *terms):
+    blocks = [(SUB, sum(map(width_of, group)))]
+    blocks += [(SUB, SUB), (TWO, SUB), (TWO, SUB)] if group == FAR else [(TWO, SUB)]
     return in_order(
-        functools.partial(total_kernel, far),
+        total_far_kernel if group == FAR else total_near_kernel,
         [jax.ShapeDtypeStruct(b, F32) for b in blocks],
         [pltpu.with_memory_space_constraint(table, pltpu.SMEM), *terms],
         [pltpu.SMEM] + [pltpu.VMEM] * len(terms),
         after,
-        name="total_far" if far else "total_near",
+        name="total_far" if group == FAR else "total_near",
     )
 
 
@@ -345,23 +396,22 @@
     for step in (2, 3, 4):
         if step < 4:
             last = b = compute(f"{step + 1}B", FULL, TWO, last)
-        elif CHAIN == 3:
-            last = b = compute("5", FAR, TWO, last)
-        after_far = ((o,), (r_far,)) if step == 2 else ((o, r_far), ())
-        last = a_far = compute(f"{step}A", FAR, TWO, last, *after_far)
-        if step == 4 and CHAIN == 1:
-            last = b = compute("5", FAR, TWO, last)
-        after_near = ((o,), (r_near,)) if step == 2 else ((o, r_near), ())
-        last = a_near = compute(f"{step}A", NEAR, TWO, last, *after_near)
-        if step == 4 and CHAIN == 2:
-            last = b = compute("5", FAR, TWO, last)
+        if step == 2:
+            last = a_far = compute("2A", FAR, TWO, last, same=(o,), half=(r_far,))
+            last = a_near = compute("2A", NEAR, TWO, last, same=(o,), half=(r_near,), pack=True)
+        else:
+            last = mine = compute(f"{step}A", FULL, TWO, last)
+            last = a_far = add_up(f"sum_{step}_far", FAR, last, r_far, mine, o)
+            if step == 4:
+                last = b = compute("5", FAR, TWO, last)
+            last = a_near = add_up(f"sum_{step}_near", NEAR, last, r_near, mine, o)
         r_far, r_near = send(a_far, ring), send(a_near, ring)
         o = send(b, swap)
     last = b_near = compute("5", NEAR, TWO, last)
-    own_far, *sends = total(True, table, last, b, o, r_far, send(r_far, swap))
+    own_far, *sends = total(FAR, table, last, b, o, r_far, send(r_far, swap))
     got = [send(sends[0], fours), send(sends[1], far[3]), send(sends[2], far[2])]
-    near = add_own(b_near, r_near, own_far)
-    own_near, sent = total(False, table, None, near, send(near, swap))
+    near = add_up("add_own", NEAR, own_far, r_near, b_near)
+    own_near, sent = total(NEAR, table, None, near, send(near, swap))
     got_near = send(sent, far[1])
     return place(table, own_far, own_near, *got, got_near, order=order)
 

time: 80.5 us -> 78.4 us (0.974)
  Pallas kernels: 31.9 us -> 30.7 us
  waiting for transfers between devices: 22.2 us -> 21.3 us
    pallas_call x17 -> x19, Pallas kernels: 25.5 us -> 24.3 us  [in_order(): pl.pallas_call(kernel, out_shape=out_shape, in_specs=[pl.BlockSpec(memory...]
    ppermute x19, waiting for transfers between devices: 22.2 us -> 21.3 us  [ring_gram(): send = lambda x, pairs: lax.ppermute(x, axis, pairs)]
  transfers between devices with their start and end apart: 19 -> 19, of which waited for: 9 -> 9; matrix products, arithmetic and copies ran while one was open for 0% -> 0% of each run, Pallas kernels for 30% -> 29%
where the time goes in v4:
time: 78.4 us; the launch traced here: 77.5 us
  Pallas kernels  30.7 us (39%)
  starting transfers between devices  24.4 us (31%)
  waiting for transfers between devices  21.3 us (27%)
    ppermute x19, starting transfers between devices, ring_gram(): send = lambda x, pairs: lax.ppermute(x, axis, pairs)  24.4 us
    pallas_call x19, Pallas kernels, in_order(): pl.pallas_call(kernel, out_shape=out_shape, in_specs=[pl.BlockSpec(memory...  24.3 us
    ppermute x19, waiting for transfers between devices, ring_gram(): send = lambda x, pairs: lax.ppermute(x, axis, pairs)  21.3 us
    pallas_call x1, Pallas kernels, prepare(): pl.pallas_call(functools.partial(prep_kernel, scale), out_shape=[pltpu.VM...  4.81 us
    pallas_call x1, Pallas kernels, place(): pl.pallas_call(place_kernel, out_shape=jax.ShapeDtypeStruct((SUB, order),...  1.58 us
  transfers between devices with their start and end apart: 19, of which 9 were waited for; matrix products, arithmetic and copies ran while one was open for 0% of the time, Pallas kernels for 29%

profile of v4, /device:TPU:0, one launch (start us, length us, event | category | flops | bytes accessed | tf_op | source)
XLA Modules:
  0.0 77.5 jit_solution(15001057506393790964)
XLA Ops:
  0.7 4.8 %weighting.1 = (bf16[768,2048]{1,0:T(8,128)(2,1)S(1)}, bf16[768,2048]{1,0:T(8,128)(2,1)S(1)}, bf16[768,2048]{1,0:T(8,128)(2,1)S(1)}, bf16[768,2048]{1,0:T(8,128)(2,1)S(1)}) custom-call(s32[16]{0:T(128)} %block_hbm.1, f32[4,4,8]{2,1,0:T(4,128)} %bitcast.3, f32[768,2048]{1,0:T(8,128)} %x_hbm.1), custom_call_target="tpu_custom_call" | custom-call | flops 2415919104 | bytes 9437184 | tf_op jit(solution)/shard_map/weighting/pallas_call | solution.py:83
  7.6 2.4 %strip_2B.1.refs_6_ = f32[256,1152]{1,0:T(8,128)S(1)} custom-call(s32[69]{0:T(128)S(1)} %dynamic-slice_bitcast_fusion.table.refs_0_, bf16[768,2048]{1,0:T(8,128)(2,1)S(1)} %get-tuple-element.15.xh.refs_1_, bf16[768,2048]{1,0:T(8,128)(2,1)S(1)} %get-tuple-element.16.xl.refs_2_, bf16[768,2048]{1,0:T(8,128)(2,1)S(1)} %get-tuple-element.17.wh.refs_3_, ...), custom_call_target="tpu_custom_call" | custom-call | flops 5000000000 | tf_op jit(solution)/shard_map/strip_2B/pallas_call | solution.py:177
  11.5 3.0 %collective-permute-start.3 = (f32[128,640]{1,0:T(8,128)S(1)}, f32[128,640]{1,0:T(8,128)S(1)}, u32[]{:S(2)}, u32[]{:S(2)}) collective-permute-start(f32[128,640]{1,0:T(8,128)S(1)} %strip_1A_far.1.refs_6_), channel_id=1, source_target_pairs={{0,4},{1,3},{4,8},{5,1},{8,12},{9,5},{12,14},{13,9},{14,10},{15,13... | collective-permute-start | bytes 983048 | tf_op jit(solution)/shard_map/ppermute | solution.py:383
  15.7 1.6 %collective-permute-start.2 = (f32[128,512]{1,0:T(8,128)S(1)}, f32[128,512]{1,0:T(8,128)S(1)}, u32[]{:S(2)}, u32[]{:S(2)}) collective-permute-start(f32[128,512]{1,0:T(8,128)S(1)} %strip_1A_near.1.refs_5_), channel_id=1, source_target_pairs={{0,4},{1,3},{4,8},{5,1},{8,12},{9,5},{12,14},{13,9},{14,10},{15,13... | collective-permute-start | bytes 786440 | tf_op jit(solution)/shard_map/ppermute | solution.py:383
  17.4 2.4 %strip_3B.1.refs_7_ = f32[256,1152]{1,0:T(8,128)S(1)} custom-call(s32[69]{0:T(128)S(1)} %dynamic-slice_bitcast_fusion.table.refs_0_, bf16[768,2048]{1,0:T(8,128)(2,1)S(1)} %get-tuple-element.15.xh.refs_1_, bf16[768,2048]{1,0:T(8,128)(2,1)S(1)} %get-tuple-element.16.xl.refs_2_, bf16[768,2048]{1,0:T(8,128)(2,1)S(1)} %get-tuple-element.17.wh.refs_3_, ...), custom_call_target="tpu_custom_call" | custom-call | flops 5000000000 | tf_op jit(solution)/shard_map/strip_3B/pallas_call | solution.py:177
  19.9 1.9 %strip_2A_far.1.refs_7_ = f32[256,640]{1,0:T(8,128)S(1)} custom-call(s32[69]{0:T(128)S(1)} %dynamic-slice_bitcast_fusion.table.refs_0_, bf16[768,2048]{1,0:T(8,128)(2,1)S(1)} %get-tuple-element.15.xh.refs_1_, bf16[768,2048]{1,0:T(8,128)(2,1)S(1)} %get-tuple-element.16.xl.refs_2_, bf16[768,2048]{1,0:T(8,128)(2,1)S(1)} %get-tuple-element.17.wh.refs_3_, ...), custom_call_target="tpu_custom_call" | custom-call | flops 5000000000 | tf_op jit(solution)/shard_map/strip_2A_far/pallas_call | solution.py:177
  21.8 1.8 %collective-permute-start.6 = (f32[256,640]{1,0:T(8,128)S(1)}, f32[256,640]{1,0:T(8,128)S(1)}, u32[]{:S(2)}, u32[]{:S(2)}) collective-permute-start(f32[256,640]{1,0:T(8,128)S(1)} %strip_2A_far.1.refs_7_), channel_id=1, source_target_pairs={{0,4},{1,3},{4,8},{5,1},{8,12},{9,5},{12,14},{13,9},{14,10},{15,13... | collective-permute-start | bytes 1966088 | tf_op jit(solution)/shard_map/ppermute | solution.py:383
  25.0 1.8 %collective-permute-start.5 = (f32[128,896]{1,0:T(8,128)S(1)}, f32[128,896]{1,0:T(8,128)S(1)}, u32[]{:S(2)}, u32[]{:S(2)}) collective-permute-start(f32[128,896]{1,0:T(8,128)S(1)} %strip_2A_near.1.refs_5_), channel_id=1, source_target_pairs={{0,4},{1,3},{4,8},{5,1},{8,12},{9,5},{12,14},{13,9},{14,10},{15,13... | collective-permute-start | bytes 1376264 | tf_op jit(solution)/shard_map/ppermute | solution.py:383
  26.8 2.4 %strip_4B.1.refs_5_ = f32[256,1152]{1,0:T(8,128)S(1)} custom-call(s32[69]{0:T(128)S(1)} %dynamic-slice_bitcast_fusion.table.refs_0_, bf16[768,2048]{1,0:T(8,128)(2,1)S(1)} %get-tuple-element.15.xh.refs_1_, bf16[768,2048]{1,0:T(8,128)(2,1)S(1)} %get-tuple-element.16.xl.refs_2_, bf16[768,2048]{1,0:T(8,128)(2,1)S(1)} %get-tuple-element.17.wh.refs_3_, ...), custom_call_target="tpu_custom_call" | custom-call | flops 5000000000 | tf_op jit(solution)/shard_map/strip_4B/pallas_call | solution.py:177
  29.3 2.4 %strip_3A.1.refs_0_.refs_3_ = f32[256,1152]{1,0:T(8,128)S(1)} custom-call(s32[69]{0:T(128)S(1)} %dynamic-slice_bitcast_fusion.table.refs_0_, bf16[768,2048]{1,0:T(8,128)(2,1)S(1)} %get-tuple-element.15.xh.refs_1_, bf16[768,2048]{1,0:T(8,128)(2,1)S(1)} %get-tuple-element.16.xl.refs_2_, bf16[768,2048]{1,0:T(8,128)(2,1)S(1)} %get-tuple-element.17.wh.refs_3_, ...), custom_call_target="tpu_custom_call" | custom-call | flops 5000000000 | tf_op jit(solution)/shard_map/strip_3A/pallas_call | solution.py:177
  32.5 1.8 %collective-permute-start.8 = (f32[256,640]{1,0:T(8,128)S(1)}, f32[256,640]{1,0:T(8,128)S(1)}, u32[]{:S(2)}, u32[]{:S(2)}) collective-permute-start(f32[256,640]{1,0:T(8,128)S(1)} %sum_3_far.1.refs_3_), channel_id=1, source_target_pairs={{0,4},{1,3},{4,8},{5,1},{8,12},{9,5},{12,14},{13,9},{14,10},{15,13... | collective-permute-start | bytes 1966088 | tf_op jit(solution)/shard_map/ppermute | solution.py:383
  34.3 3.0 %collective-permute-done.5.refs_2_ = f32[128,896]{1,0:T(8,128)S(1)} collective-permute-done((f32[128,896]{1,0:T(8,128)S(1)}, f32[128,896]{1,0:T(8,128)S(1)}, u32[]{:S(2)}, u32[]{:S(2)}) %collective-permute-start.5) | collective-permute-done | bytes 458784 | tf_op jit(solution)/shard_map/ppermute | solution.py:383
  37.4 1.8 %collective-permute-start.12 = (f32[128,896]{1,0:T(8,128)S(1)}, f32[128,896]{1,0:T(8,128)S(1)}, u32[]{:S(2)}, u32[]{:S(2)}) collective-permute-start(f32[128,896]{1,0:T(8,128)S(1)} %sum_3_near.1.refs_5_), channel_id=1, source_target_pairs={{0,4},{1,3},{4,8},{5,1},{8,12},{9,5},{12,14},{13,9},{14,10},{15,13... | collective-permute-start | bytes 1376264 | tf_op jit(solution)/shard_map/ppermute | solution.py:383
  39.2 2.4 %strip_4A.1.refs_0_.refs_3_ = f32[256,1152]{1,0:T(8,128)S(1)} custom-call(s32[69]{0:T(128)S(1)} %dynamic-slice_bitcast_fusion.table.refs_0_, bf16[768,2048]{1,0:T(8,128)(2,1)S(1)} %get-tuple-element.15.xh.refs_1_, bf16[768,2048]{1,0:T(8,128)(2,1)S(1)} %get-tuple-element.16.xl.refs_2_, bf16[768,2048]{1,0:T(8,128)(2,1)S(1)} %get-tuple-element.17.wh.refs_3_, ...), custom_call_target="tpu_custom_call" | custom-call | flops 5000000000 | tf_op jit(solution)/shard_map/strip_4A/pallas_call | solution.py:177
  41.6 2.7 %collective-permute-done.8.refs_2_ = f32[256,640]{1,0:T(8,128)S(1)} collective-permute-done((f32[256,640]{1,0:T(8,128)S(1)}, f32[256,640]{1,0:T(8,128)S(1)}, u32[]{:S(2)}, u32[]{:S(2)}) %collective-permute-start.8) | collective-permute-done | bytes 655392 | tf_op jit(solution)/shard_map/ppermute | solution.py:383
  44.4 1.8 %collective-permute-start.10 = (f32[256,640]{1,0:T(8,128)S(1)}, f32[256,640]{1,0:T(8,128)S(1)}, u32[]{:S(2)}, u32[]{:S(2)}) collective-permute-start(f32[256,640]{1,0:T(8,128)S(1)} %sum_4_far.1.refs_5_), channel_id=1, source_target_pairs={{0,4},{1,3},{4,8},{5,1},{8,12},{9,5},{12,14},{13,9},{14,10},{15,13... | collective-permute-start | bytes 1966088 | tf_op jit(solution)/shard_map/ppermute | solution.py:383
  46.2 1.8 %strip_5_far.1.refs_3_.refs_1_ = f32[256,640]{1,0:T(8,128)S(1)} custom-call(s32[69]{0:T(128)S(1)} %dynamic-slice_bitcast_fusion.table.refs_0_, bf16[768,2048]{1,0:T(8,128)(2,1)S(1)} %get-tuple-element.15.xh.refs_1_, bf16[768,2048]{1,0:T(8,128)(2,1)S(1)} %get-tuple-element.16.xl.refs_2_, bf16[768,2048]{1,0:T(8,128)(2,1)S(1)} %get-tuple-element.17.wh.refs_3_, ...), custom_call_target="tpu_custom_call" | custom-call | flops 100000000 | tf_op jit(solution)/shard_map/strip_5_far/pallas_call | solution.py:177
  49.3 1.8 %collective-permute-start.13 = (f32[128,896]{1,0:T(8,128)S(1)}, f32[128,896]{1,0:T(8,128)S(1)}, u32[]{:S(2)}, u32[]{:S(2)}) collective-permute-start(f32[128,896]{1,0:T(8,128)S(1)} %sum_4_near.1.refs_5_), channel_id=1, source_target_pairs={{0,4},{1,3},{4,8},{5,1},{8,12},{9,5},{12,14},{13,9},{14,10},{15,13... | collective-permute-start | bytes 1376264 | tf_op jit(solution)/shard_map/ppermute | solution.py:383
  51.1 5.2 %collective-permute-done.10.refs_3_ = f32[256,640]{1,0:T(8,128)S(1)} collective-permute-done((f32[256,640]{1,0:T(8,128)S(1)}, f32[256,640]{1,0:T(8,128)S(1)}, u32[]{:S(2)}, u32[]{:S(2)}) %collective-permute-start.10) | collective-permute-done | bytes 655392 | tf_op jit(solution)/shard_map/ppermute | solution.py:383
  59.1 2.1 %collective-permute-done.13.refs_1_ = f32[128,896]{1,0:T(8,128)S(1)} collective-permute-done((f32[128,896]{1,0:T(8,128)S(1)}, f32[128,896]{1,0:T(8,128)S(1)}, u32[]{:S(2)}, u32[]{:S(2)}) %collective-permute-start.13) | collective-permute-done | bytes 458784 | tf_op jit(solution)/shard_map/ppermute | solution.py:383
  61.3 3.7 %collective-permute-start.16 = (f32[256,128]{1,0:T(8,128)S(1)}, f32[256,128]{1,0:T(8,128)S(1)}, u32[]{:S(2)}, u32[]{:S(2)}) collective-permute-start(f32[256,128]{1,0:T(8,128)S(1)} %get-tuple-element.22), channel_id=1, source_target_pairs={{0,10},{1,11},{4,6},{5,7},{8,14},{9,15},{12,0},{13,1},{14,4},{15,5... | collective-permute-start | bytes 393224 | tf_op jit(solution)/shard_map/ppermute | solution.py:383
  65.7 1.9 %collective-permute-start.18 = (f32[256,128]{1,0:T(8,128)S(1)}, f32[256,128]{1,0:T(8,128)S(1)}, u32[]{:S(2)}, u32[]{:S(2)}) collective-permute-start(f32[256,128]{1,0:T(8,128)S(1)} %get-tuple-element.24), channel_id=1, source_target_pairs={{0,2},{1,3},{4,12},{5,13},{8,0},{9,1},{12,8},{13,9},{14,10},{15,11... | collective-permute-start | bytes 393224 | tf_op jit(solution)/shard_map/ppermute | solution.py:383
  67.6 2.5 %collective-permute-start.15 = (f32[128,128]{1,0:T(8,128)S(1)}, f32[128,128]{1,0:T(8,128)S(1)}, u32[]{:S(2)}, u32[]{:S(2)}) collective-permute-start(f32[128,128]{1,0:T(8,128)S(1)} %get-tuple-element.21), channel_id=1, source_target_pairs={{0,14},{1,15},{4,10},{5,11},{8,6},{9,7},{12,2},{13,3},{14,1},{15,0... | collective-permute-start | bytes 196616 | tf_op jit(solution)/shard_map/ppermute | solution.py:383
  70.1 4.8 %collective-permute-done.15.refs_0_ = f32[128,128]{1,0:T(8,128)S(1)} collective-permute-done((f32[128,128]{1,0:T(8,128)S(1)}, f32[128,128]{1,0:T(8,128)S(1)}, u32[]{:S(2)}, u32[]{:S(2)}) %collective-permute-start.15) | collective-permute-done | bytes 65568 | tf_op jit(solution)/shard_map/ppermute | solution.py:383
  (36 shorter events, 15.2 us)
Async XLA Ops:
  7.1 3.1 %collective-permute-start.1 = (f32[128,1152]{1,0:T(8,128)S(1)}, f32[128,1152]{1,0:T(8,128)S(1)}, u32[]{:S(2)}, u32[]{:S(2)}) collective-permute-start(f32[128,1152]{1,0:T(8,128)S(1)} %strip_1B.1.refs_5_), channel_id=1, source_target_pairs={{0,1},{1,0},{4,5},{5,4},{8,9},{9,8},{12,13},{13,12},{14,15},{15,14... | collective-permute-start | bytes 1769480 | tf_op jit(solution)/shard_map/ppermute | solution.py:383
  10.1 9.8 %collective-permute-start = (f32[256,1152]{1,0:T(8,128)S(1)}, f32[256,1152]{1,0:T(8,128)S(1)}, u32[]{:S(2)}, u32[]{:S(2)}) collective-permute-start(f32[256,1152]{1,0:T(8,128)S(1)} %strip_2B.1.refs_6_), channel_id=1, source_target_pairs={{0,1},{1,0},{4,5},{5,4},{8,9},{9,8},{12,13},{13,12},{14,15},{15,14... | collective-permute-start | bytes 3538952 | tf_op jit(solution)/shard_map/ppermute | solution.py:383
  11.5 8.4 %collective-permute-start.3 = (f32[128,640]{1,0:T(8,128)S(1)}, f32[128,640]{1,0:T(8,128)S(1)}, u32[]{:S(2)}, u32[]{:S(2)}) collective-permute-start(f32[128,640]{1,0:T(8,128)S(1)} %strip_1A_far.1.refs_6_), channel_id=1, source_target_pairs={{0,4},{1,3},{4,8},{5,1},{8,12},{9,5},{12,14},{13,9},{14,10},{15,13... | collective-permute-start | bytes 983048 | tf_op jit(solution)/shard_map/ppermute | solution.py:383
  15.7 7.8 %collective-permute-start.2 = (f32[128,512]{1,0:T(8,128)S(1)}, f32[128,512]{1,0:T(8,128)S(1)}, u32[]{:S(2)}, u32[]{:S(2)}) collective-permute-start(f32[128,512]{1,0:T(8,128)S(1)} %strip_1A_near.1.refs_5_), channel_id=1, source_target_pairs={{0,4},{1,3},{4,8},{5,1},{8,12},{9,5},{12,14},{13,9},{14,10},{15,13... | collective-permute-start | bytes 786440 | tf_op jit(solution)/shard_map/ppermute | solution.py:383
  19.8 11.9 %collective-permute-start.4 = (f32[256,1152]{1,0:T(8,128)S(1)}, f32[256,1152]{1,0:T(8,128)S(1)}, u32[]{:S(2)}, u32[]{:S(2)}) collective-permute-start(f32[256,1152]{1,0:T(8,128)S(1)} %strip_3B.1.refs_7_), channel_id=1, source_target_pairs={{0,1},{1,0},{4,5},{5,4},{8,9},{9,8},{12,13},{13,12},{14,15},{15,14... | collective-permute-start | bytes 3538952 | tf_op jit(solution)/shard_map/ppermute | solution.py:383
  21.8 10.6 %collective-permute-start.6 = (f32[256,640]{1,0:T(8,128)S(1)}, f32[256,640]{1,0:T(8,128)S(1)}, u32[]{:S(2)}, u32[]{:S(2)}) collective-permute-start(f32[256,640]{1,0:T(8,128)S(1)} %strip_2A_far.1.refs_7_), channel_id=1, source_target_pairs={{0,4},{1,3},{4,8},{5,1},{8,12},{9,5},{12,14},{13,9},{14,10},{15,13... | collective-permute-start | bytes 1966088 | tf_op jit(solution)/shard_map/ppermute | solution.py:383
  25.0 12.4 %collective-permute-start.5 = (f32[128,896]{1,0:T(8,128)S(1)}, f32[128,896]{1,0:T(8,128)S(1)}, u32[]{:S(2)}, u32[]{:S(2)}) collective-permute-start(f32[128,896]{1,0:T(8,128)S(1)} %strip_2A_near.1.refs_5_), channel_id=1, source_target_pairs={{0,4},{1,3},{4,8},{5,1},{8,12},{9,5},{12,14},{13,9},{14,10},{15,13... | collective-permute-start | bytes 1376264 | tf_op jit(solution)/shard_map/ppermute | solution.py:383
  29.2 12.4 %collective-permute-start.7 = (f32[256,1152]{1,0:T(8,128)S(1)}, f32[256,1152]{1,0:T(8,128)S(1)}, u32[]{:S(2)}, u32[]{:S(2)}) collective-permute-start(f32[256,1152]{1,0:T(8,128)S(1)} %strip_4B.1.refs_5_), channel_id=1, source_target_pairs={{0,1},{1,0},{4,5},{5,4},{8,9},{9,8},{12,13},{13,12},{14,15},{15,14... | collective-permute-start | bytes 3538952 | tf_op jit(solution)/shard_map/ppermute | solution.py:383
  32.5 11.8 %collective-permute-start.8 = (f32[256,640]{1,0:T(8,128)S(1)}, f32[256,640]{1,0:T(8,128)S(1)}, u32[]{:S(2)}, u32[]{:S(2)}) collective-permute-start(f32[256,640]{1,0:T(8,128)S(1)} %sum_3_far.1.refs_3_), channel_id=1, source_target_pairs={{0,4},{1,3},{4,8},{5,1},{8,12},{9,5},{12,14},{13,9},{14,10},{15,13... | collective-permute-start | bytes 1966088 | tf_op jit(solution)/shard_map/ppermute | solution.py:383
  37.4 11.8 %collective-permute-start.12 = (f32[128,896]{1,0:T(8,128)S(1)}, f32[128,896]{1,0:T(8,128)S(1)}, u32[]{:S(2)}, u32[]{:S(2)}) collective-permute-start(f32[128,896]{1,0:T(8,128)S(1)} %sum_3_near.1.refs_5_), channel_id=1, source_target_pairs={{0,4},{1,3},{4,8},{5,1},{8,12},{9,5},{12,14},{13,9},{14,10},{15,13... | collective-permute-start | bytes 1376264 | tf_op jit(solution)/shard_map/ppermute | solution.py:383
  44.4 11.8 %collective-permute-start.10 = (f32[256,640]{1,0:T(8,128)S(1)}, f32[256,640]{1,0:T(8,128)S(1)}, u32[]{:S(2)}, u32[]{:S(2)}) collective-permute-start(f32[256,640]{1,0:T(8,128)S(1)} %sum_4_far.1.refs_5_), channel_id=1, source_target_pairs={{0,4},{1,3},{4,8},{5,1},{8,12},{9,5},{12,14},{13,9},{14,10},{15,13... | collective-permute-start | bytes 1966088 | tf_op jit(solution)/shard_map/ppermute | solution.py:383
  48.0 9.6 %collective-permute-start.9 = (f32[256,640]{1,0:T(8,128)S(1)}, f32[256,640]{1,0:T(8,128)S(1)}, u32[]{:S(2)}, u32[]{:S(2)}) collective-permute-start(f32[256,640]{1,0:T(8,128)S(1)} %strip_5_far.1.refs_3_.refs_1_), channel_id=1, source_target_pairs={{0,1},{1,0},{4,5},{5,4},{8,9},{9,8},{12,13},{13,12},{14,15},{15,14... | collective-permute-start | bytes 1966088 | tf_op jit(solution)/shard_map/ppermute | solution.py:383
  49.3 11.9 %collective-permute-start.13 = (f32[128,896]{1,0:T(8,128)S(1)}, f32[128,896]{1,0:T(8,128)S(1)}, u32[]{:S(2)}, u32[]{:S(2)}) collective-permute-start(f32[128,896]{1,0:T(8,128)S(1)} %sum_4_near.1.refs_5_), channel_id=1, source_target_pairs={{0,4},{1,3},{4,8},{5,1},{8,12},{9,5},{12,14},{13,9},{14,10},{15,13... | collective-permute-start | bytes 1376264 | tf_op jit(solution)/shard_map/ppermute | solution.py:383
  56.3 2.1 %collective-permute-start.11 = (f32[256,640]{1,0:T(8,128)S(1)}, f32[256,640]{1,0:T(8,128)S(1)}, u32[]{:S(2)}, u32[]{:S(2)}) collective-permute-start(f32[256,640]{1,0:T(8,128)S(1)} %collective-permute-done.10.refs_3_), channel_id=1, source_target_pairs={{0,1},{1,0},{4,5},{5,4},{8,9},{9,8},{12,13},{13,12},{14,15},{15,14... | collective-permute-start | bytes 1966088 | tf_op jit(solution)/shard_map/ppermute | solution.py:383
  61.3 3.8 %collective-permute-start.14 = (f32[128,896]{1,0:T(8,128)S(1)}, f32[128,896]{1,0:T(8,128)S(1)}, u32[]{:S(2)}, u32[]{:S(2)}) collective-permute-start(f32[128,896]{1,0:T(8,128)S(1)} %add_own.1.a), channel_id=1, source_target_pairs={{0,1},{1,0},{4,5},{5,4},{8,9},{9,8},{12,13},{13,12},{14,15},{15,14... | collective-permute-start | bytes 1376264 | tf_op jit(solution)/shard_map/ppermute | solution.py:383
  61.3 13.5 %collective-permute-start.16 = (f32[256,128]{1,0:T(8,128)S(1)}, f32[256,128]{1,0:T(8,128)S(1)}, u32[]{:S(2)}, u32[]{:S(2)}) collective-permute-start(f32[256,128]{1,0:T(8,128)S(1)} %get-tuple-element.22), channel_id=1, source_target_pairs={{0,10},{1,11},{4,6},{5,7},{8,14},{9,15},{12,0},{13,1},{14,4},{15,5... | collective-permute-start | bytes 393224 | tf_op jit(solution)/shard_map/ppermute | solution.py:383
  65.1 10.7 %collective-permute-start.17 = (f32[256,128]{1,0:T(8,128)S(1)}, f32[256,128]{1,0:T(8,128)S(1)}, u32[]{:S(2)}, u32[]{:S(2)}) collective-permute-start(f32[256,128]{1,0:T(8,128)S(1)} %get-tuple-element.23), channel_id=1, source_target_pairs={{0,4},{1,5},{4,8},{5,9},{8,10},{9,11},{12,6},{13,7},{14,12},{15,13... | collective-permute-start | bytes 393224 | tf_op jit(solution)/shard_map/ppermute | solution.py:383
  65.7 10.1 %collective-permute-start.18 = (f32[256,128]{1,0:T(8,128)S(1)}, f32[256,128]{1,0:T(8,128)S(1)}, u32[]{:S(2)}, u32[]{:S(2)}) collective-permute-start(f32[256,128]{1,0:T(8,128)S(1)} %get-tuple-element.24), channel_id=1, source_target_pairs={{0,2},{1,3},{4,12},{5,13},{8,0},{9,1},{12,8},{13,9},{14,10},{15,11... | collective-permute-start | bytes 393224 | tf_op jit(solution)/shard_map/ppermute | solution.py:383
  67.6 7.3 %collective-permute-start.15 = (f32[128,128]{1,0:T(8,128)S(1)}, f32[128,128]{1,0:T(8,128)S(1)}, u32[]{:S(2)}, u32[]{:S(2)}) collective-permute-start(f32[128,128]{1,0:T(8,128)S(1)} %get-tuple-element.21), channel_id=1, source_target_pairs={{0,14},{1,15},{4,10},{5,11},{8,6},{9,7},{12,2},{13,3},{14,1},{15,0... | collective-permute-start | bytes 196616 | tf_op jit(solution)/shard_map/ppermute | solution.py:383

commit v5 on v4

--- a/solution.py
+++ b/solution.py
@@ -16,10 +16,11 @@
 TWO = 2 * SUB
 
 
-def prep_kernel(scale, block_hbm, mass_hbm, x_hbm, xh, xl, wh, wl, x, table, both, block_of, mass, sems, small):
+def prep_kernel(scale, axis, block_hbm, mass_hbm, x_hbm, places, xh, xl, wh, wl, place, x, table, both, block_of, mass, sems, small):
     rows, order = x_hbm.shape
     nodes, _, classes = mass.shape
-    first = [pltpu.make_async_copy(block_hbm, block_of, small.at[0]), pltpu.make_async_copy(mass_hbm, mass, small.at[1])]
+    pairs = ((block_hbm, block_of), (mass_hbm, mass), (places.at[lax.axis_index(axis)], place))
+    first = [pltpu.make_async_copy(a, b, small.at[i]) for i, (a, b) in enumerate(pairs)]
     for copy in first:
         copy.start()
     per_element = rows // block_of.shape[0]
@@ -74,17 +75,17 @@
 PIECES = 1
 
 
-def prepare(snapshots, block_of, mass_table, scale):
+def prepare(snapshots, block_of, mass_table, scale, places, axis):
     rows, order = snapshots.shape
     band = TWO
     bands = rows // band
     smem = pl.BlockSpec(memory_space=pltpu.SMEM)
     vmem = pl.BlockSpec(memory_space=pltpu.VMEM)
     return pl.pallas_call(
-        functools.partial(prep_kernel, scale),
-        out_shape=[pltpu.VMEM((rows, order), BF16)] * 4,
-        in_specs=[pl.BlockSpec(memory_space=pl.ANY)] * 3,
-        out_specs=[vmem] * 4,
+        functools.partial(prep_kernel, scale, axis),
+        out_shape=[pltpu.VMEM((rows, order), BF16)] * 4 + [pltpu.SMEM(places.shape[1:], jnp.int32)],
+        in_specs=[pl.BlockSpec(memory_space=pl.ANY)] * 4,
+        out_specs=[vmem] * 4 + [smem],
         scratch_shapes=[
             pltpu.VMEM((rows, order), F32),
             pltpu.VMEM((8 * mass_table.shape[0], band), F32),
@@ -92,14 +93,14 @@
             pltpu.SMEM(block_of.shape, jnp.int32),
             pltpu.SMEM(mass_table.shape[1:] + mass_table.shape[:1], F32),
             pltpu.SemaphoreType.DMA((PIECES * bands,)),
-            pltpu.SemaphoreType.DMA((2,)),
+            pltpu.SemaphoreType.DMA((3,)),
         ],
         compiler_params=pltpu.CompilerParams(vmem_limit_bytes=32 * MIB),
         cost_estimate=pl.CostEstimate(
             flops=6 * rows * order * band, bytes_accessed=6 * rows * order, transcendentals=0
         ),
         name="weighting",
-    )(*(pltpu.with_memory_space_constraint(x, pltpu.HBM) for x in (block_of, mass_table.transpose(1, 2, 0), snapshots)))
+    )(*(pltpu.with_memory_space_constraint(x, pltpu.HBM) for x in (block_of, mass_table.transpose(1, 2, 0), snapshots, places)))
 
 
 LHS, K0, K1, K2, K3, K4A, K4B = range(7)
@@ -109,7 +110,6 @@
 COSTS = {"sum_4_far": 0.02, "sum_4_near": 10, "strip_5_far": 0.02, "strip_5_near": 3, "total_far": 0.1, "total_near": 0.02, "add_own": 0.02}
 INSTANCES = {name: 7 * i for i, name in enumerate(("1A", "1B", "2A", "2B", "3A", "3B", "4A", "4B", "5"))}
 CORE, R1, R2, R3, R4, FOUR = range(63, 69)
-TABLE = 69
 
 
 def ring_chip(p):
@@ -133,7 +133,7 @@
 
 
 def position_table():
-    table = np.zeros((2 * CHIPS, TABLE), np.int32)
+    table = np.zeros((2 * CHIPS, 1, 128), np.int32)
 
     def strip(q, half=None):
         at = TWO * ring_chip(q)
@@ -153,7 +153,7 @@
             row += [SUB * c] + [TWO * ring_chip(q) for k in (1, 2, 3) for q in range(CHIPS) if pair(q, k) % CHIPS == p]
             row += [TWO * ring_chip(p + 4) + SUB * (c if (p + 4) % CHIPS < 4 else 1 - c)]
             row += [strip(p, c)[K4A]]
-            table[ring_device(p, c)] = row
+            table[ring_device(p, c), 0, : len(row)] = row
     return table
 
 
@@ -192,7 +192,7 @@
     width = sum(map(width_of, group))
 
     def entry(i):
-        return pl.multiple_of(table[base + i], SUB)
+        return pl.multiple_of(table[0, base + i], SUB)
 
     def dot(a, b):
         return jnp.dot(a, b, preferred_element_type=F32)
@@ -223,7 +223,7 @@
         if name == "half" and pack:
             for mine in range(2):
 
-                @pl.when(table[CORE] == SUB * mine)
+                @pl.when(table[0, CORE] == SUB * mine)
                 def _():
                     for k, r, c0, n, at in PACKED:
                         if r == SUB * mine:
@@ -231,7 +231,7 @@
                             out[:, at : at + n] = out[:, at : at + n] + ref[:, c : c + n]
 
         elif name == "half":
-            rows = pl.ds(pl.multiple_of(table[CORE], SUB), SUB)
+            rows = pl.ds(pl.multiple_of(table[0, CORE], SUB), SUB)
             out[rows, :] = out[rows, :] + ref[...]
 
 
@@ -276,7 +276,7 @@
 
 
 def total_far_kernel(table, a, b, c, d, own, four, *sends):
-    core = pl.multiple_of(table[CORE], SUB)
+    core = pl.multiple_of(table[0, CORE], SUB)
 
     def add(rows, columns):
         return (a[rows, columns] + b[rows, columns]) + (c[rows, columns] + d[rows, columns])
@@ -288,7 +288,7 @@
 
 
 def total_near_kernel(table, a, b, own, sent):
-    core = pl.multiple_of(table[CORE], SUB)
+    core = pl.multiple_of(table[0, CORE], SUB)
 
     def add(at, n):
         columns = pl.ds(at, n)
@@ -329,7 +329,7 @@
     copies = []
 
     def put(entry, source):
-        columns = pl.ds(pl.multiple_of(table[entry], SUB), source.shape[1])
+        columns = pl.ds(pl.multiple_of(table[0, entry], SUB), source.shape[1])
         copy = pltpu.make_async_copy(source, out.at[:, columns], sems.at[len(copies)])
         copy.start()
         copies.append(copy)
@@ -378,8 +378,8 @@
             fours.append((here, ring_device(p + 4, fourth(p, c))))
             for k in far:
                 far[k].append((here, ring_device(pair(p, k), c)))
-    table = jnp.asarray(position_table())[lax.axis_index(axis)]
-    operands = prepare(snapshots, block_of, mass_table, 1.0 / (rows * 2 * CHIPS))
+    places = jnp.asarray(position_table())
+    *operands, table = prepare(snapshots, block_of, mass_table, 1.0 / (rows * 2 * CHIPS), places, axis)
     send = lambda x, pairs: lax.ppermute(x, axis, pairs)
     compute = lambda name, group, height, *rest, **adds: strip(
         name, group, height, operands, table, *rest, **adds
@@ -418,7 +418,9 @@
 
 def scattered_gram(snapshots, block_of, mass_table, axis):
     rows, order = snapshots.shape
-    xh, xl, wh, wl = prepare(snapshots, block_of, mass_table, 1.0 / (rows * lax.axis_size(axis)))
+    scale = 1.0 / (rows * lax.axis_size(axis))
+    places = jnp.zeros((lax.axis_size(axis), 1, 128), jnp.int32)
+    xh, xl, wh, wl, _ = prepare(snapshots, block_of, mass_table, scale, places, axis)
 
     def dot(a, b):
         return lax.dot_general(a, b, (((0,), (0,)), ((), ())), preferred_element_type=F32)

time: 78.4 us -> 74.9 us (0.955)
  Pallas kernels: 30.7 us -> 22.5 us
  waiting for transfers between devices: 21.3 us -> 24.7 us
  starting transfers between devices: 24.4 us -> 26.6 us
    pallas_call x19, Pallas kernels: 24.3 us -> 16.7 us  [in_order(): pl.pallas_call(kernel, out_shape=out_shape, in_specs=[pl.BlockSpec(memory...]
    ppermute x19, waiting for transfers between devices: 21.3 us -> 24.7 us  [ring_gram(): send = lambda x, pairs: lax.ppermute(x, axis, pairs)]
    ppermute x19, starting transfers between devices: 24.4 us -> 26.6 us  [ring_gram(): send = lambda x, pairs: lax.ppermute(x, axis, pairs)]
  transfers between devices with their start and end apart: 19 -> 19, of which waited for: 9 -> 10; matrix products, arithmetic and copies ran while one was open for 0% -> 0% of each run, Pallas kernels for 29% -> 21%
where the time goes in v5:
time: 74.9 us; the launch traced here: 74.1 us
  starting transfers between devices  26.6 us (36%)
  waiting for transfers between devices  24.7 us (33%)
  Pallas kernels  22.5 us (30%)
    ppermute x19, starting transfers between devices, ring_gram(): send = lambda x, pairs: lax.ppermute(x, axis, pairs)  26.6 us
    ppermute x19, waiting for transfers between devices, ring_gram(): send = lambda x, pairs: lax.ppermute(x, axis, pairs)  24.7 us
    pallas_call x19, Pallas kernels, in_order(): pl.pallas_call(kernel, out_shape=out_shape, in_specs=[pl.BlockSpec(memory...  16.7 us
    pallas_call x1, Pallas kernels, prepare(): pl.pallas_call(functools.partial(prep_kernel, scale, axis), out_shape=[pl...  4.82 us
  transfers between devices with their start and end apart: 19, of which 10 were waited for; matrix products, arithmetic and copies ran while one was open for 0% of the time, Pallas kernels for 21%

profile of v5, /device:TPU:0, one launch (start us, length us, event | category | flops | bytes accessed | tf_op | source)
XLA Modules:
  0.0 74.1 jit_solution(12278710552215233854)
XLA Ops:
  0.0 4.8 %weighting.1 = (bf16[768,2048]{1,0:T(8,128)(2,1)S(1)}, bf16[768,2048]{1,0:T(8,128)(2,1)S(1)}, bf16[768,2048]{1,0:T(8,128)(2,1)S(1)}, bf16[768,2048]{1,0:T(8,128)(2,1)S(1)}, s32[1,128]{1,0:T(1,128)S(4)}) custom-call(s32[16]{0:T(128)} %block_hbm.1, f32[4,4,8]{2,1,0:T(4,128)} %bitcast.1, f32[768,2048]{1,0:T(8,128)} %x_hbm.1, s32[16,1,128]{2,1,0:T(1,128)} %constant.2.clone.places), custom_call_target="tpu_custom_call" | custom-call | flops 2415919104 | bytes 9437184 | tf_op jit(solution)/shard_map/weighting/pallas_call | solution.py:84
  6.4 1.9 %strip_2B.1.refs_6_ = f32[256,1152]{1,0:T(8,128)S(1)} custom-call(s32[1,128]{1,0:T(1,128)S(4)} %get-tuple-element.16.table.refs_0_, bf16[768,2048]{1,0:T(8,128)(2,1)S(1)} %get-tuple-element.17.xh.refs_1_, bf16[768,2048]{1,0:T(8,128)(2,1)S(1)} %get-tuple-element.18.xl.refs_2_, bf16[768,2048]{1,0:T(8,128)(2,1)S(1)} %get-tuple-element.19.wh.refs_3_, ...), custom_call_target="tpu_custom_call" | custom-call | flops 5000000000 | tf_op jit(solution)/shard_map/strip_2B/pallas_call | solution.py:177
  9.2 3.1 %collective-permute-start.3 = (f32[128,640]{1,0:T(8,128)S(1)}, f32[128,640]{1,0:T(8,128)S(1)}, u32[]{:S(2)}, u32[]{:S(2)}) collective-permute-start(f32[128,640]{1,0:T(8,128)S(1)} %strip_1A_far.1.refs_6_), channel_id=1, source_target_pairs={{0,4},{1,3},{4,8},{5,1},{8,12},{9,5},{12,14},{13,9},{14,10},{15,13... | collective-permute-start | bytes 983048 | tf_op jit(solution)/shard_map/ppermute | solution.py:383
  12.9 1.6 %collective-permute-start.2 = (f32[128,512]{1,0:T(8,128)S(1)}, f32[128,512]{1,0:T(8,128)S(1)}, u32[]{:S(2)}, u32[]{:S(2)}) collective-permute-start(f32[128,512]{1,0:T(8,128)S(1)} %strip_1A_near.1.refs_5_), channel_id=1, source_target_pairs={{0,4},{1,3},{4,8},{5,1},{8,12},{9,5},{12,14},{13,9},{14,10},{15,13... | collective-permute-start | bytes 786440 | tf_op jit(solution)/shard_map/ppermute | solution.py:383
  14.5 1.9 %strip_3B.1.refs_7_ = f32[256,1152]{1,0:T(8,128)S(1)} custom-call(s32[1,128]{1,0:T(1,128)S(4)} %get-tuple-element.16.table.refs_0_, bf16[768,2048]{1,0:T(8,128)(2,1)S(1)} %get-tuple-element.17.xh.refs_1_, bf16[768,2048]{1,0:T(8,128)(2,1)S(1)} %get-tuple-element.18.xl.refs_2_, bf16[768,2048]{1,0:T(8,128)(2,1)S(1)} %get-tuple-element.19.wh.refs_3_, ...), custom_call_target="tpu_custom_call" | custom-call | flops 5000000000 | tf_op jit(solution)/shard_map/strip_3B/pallas_call | solution.py:177
  18.5 2.1 %collective-permute-start.6 = (f32[256,640]{1,0:T(8,128)S(1)}, f32[256,640]{1,0:T(8,128)S(1)}, u32[]{:S(2)}, u32[]{:S(2)}) collective-permute-start(f32[256,640]{1,0:T(8,128)S(1)} %strip_2A_far.1.refs_7_), channel_id=1, source_target_pairs={{0,4},{1,3},{4,8},{5,1},{8,12},{9,5},{12,14},{13,9},{14,10},{15,13... | collective-permute-start | bytes 1966088 | tf_op jit(solution)/shard_map/ppermute | solution.py:383
  21.6 1.8 %collective-permute-start.5 = (f32[128,896]{1,0:T(8,128)S(1)}, f32[128,896]{1,0:T(8,128)S(1)}, u32[]{:S(2)}, u32[]{:S(2)}) collective-permute-start(f32[128,896]{1,0:T(8,128)S(1)} %strip_2A_near.1.refs_5_), channel_id=1, source_target_pairs={{0,4},{1,3},{4,8},{5,1},{8,12},{9,5},{12,14},{13,9},{14,10},{15,13... | collective-permute-start | bytes 1376264 | tf_op jit(solution)/shard_map/ppermute | solution.py:383
  23.4 1.9 %strip_4B.1.refs_5_ = f32[256,1152]{1,0:T(8,128)S(1)} custom-call(s32[1,128]{1,0:T(1,128)S(4)} %get-tuple-element.16.table.refs_0_, bf16[768,2048]{1,0:T(8,128)(2,1)S(1)} %get-tuple-element.17.xh.refs_1_, bf16[768,2048]{1,0:T(8,128)(2,1)S(1)} %get-tuple-element.18.xl.refs_2_, bf16[768,2048]{1,0:T(8,128)(2,1)S(1)} %get-tuple-element.19.wh.refs_3_, ...), custom_call_target="tpu_custom_call" | custom-call | flops 5000000000 | tf_op jit(solution)/shard_map/strip_4B/pallas_call | solution.py:177
  25.4 1.9 %strip_3A.1.refs_0_.refs_3_ = f32[256,1152]{1,0:T(8,128)S(1)} custom-call(s32[1,128]{1,0:T(1,128)S(4)} %get-tuple-element.16.table.refs_0_, bf16[768,2048]{1,0:T(8,128)(2,1)S(1)} %get-tuple-element.17.xh.refs_1_, bf16[768,2048]{1,0:T(8,128)(2,1)S(1)} %get-tuple-element.18.xl.refs_2_, bf16[768,2048]{1,0:T(8,128)(2,1)S(1)} %get-tuple-element.19.wh.refs_3_, ...), custom_call_target="tpu_custom_call" | custom-call | flops 5000000000 | tf_op jit(solution)/shard_map/strip_3A/pallas_call | solution.py:177
  27.3 1.9 %collective-permute-done.6.refs_2_ = f32[256,640]{1,0:T(8,128)S(1)} collective-permute-done((f32[256,640]{1,0:T(8,128)S(1)}, f32[256,640]{1,0:T(8,128)S(1)}, u32[]{:S(2)}, u32[]{:S(2)}) %collective-permute-start.6) | collective-permute-done | bytes 655392 | tf_op jit(solution)/shard_map/ppermute | solution.py:383
  29.3 2.1 %collective-permute-start.8 = (f32[256,640]{1,0:T(8,128)S(1)}, f32[256,640]{1,0:T(8,128)S(1)}, u32[]{:S(2)}, u32[]{:S(2)}) collective-permute-start(f32[256,640]{1,0:T(8,128)S(1)} %sum_3_far.1.refs_3_), channel_id=1, source_target_pairs={{0,4},{1,3},{4,8},{5,1},{8,12},{9,5},{12,14},{13,9},{14,10},{15,13... | collective-permute-start | bytes 1966088 | tf_op jit(solution)/shard_map/ppermute | solution.py:383
  31.4 2.7 %collective-permute-done.5.refs_2_ = f32[128,896]{1,0:T(8,128)S(1)} collective-permute-done((f32[128,896]{1,0:T(8,128)S(1)}, f32[128,896]{1,0:T(8,128)S(1)}, u32[]{:S(2)}, u32[]{:S(2)}) %collective-permute-start.5) | collective-permute-done | bytes 458784 | tf_op jit(solution)/shard_map/ppermute | solution.py:383
  34.2 2.1 %collective-permute-start.12 = (f32[128,896]{1,0:T(8,128)S(1)}, f32[128,896]{1,0:T(8,128)S(1)}, u32[]{:S(2)}, u32[]{:S(2)}) collective-permute-start(f32[128,896]{1,0:T(8,128)S(1)} %sum_3_near.1.refs_5_), channel_id=1, source_target_pairs={{0,4},{1,3},{4,8},{5,1},{8,12},{9,5},{12,14},{13,9},{14,10},{15,13... | collective-permute-start | bytes 1376264 | tf_op jit(solution)/shard_map/ppermute | solution.py:383
  36.3 1.9 %strip_4A.1.refs_0_.refs_3_ = f32[256,1152]{1,0:T(8,128)S(1)} custom-call(s32[1,128]{1,0:T(1,128)S(4)} %get-tuple-element.16.table.refs_0_, bf16[768,2048]{1,0:T(8,128)(2,1)S(1)} %get-tuple-element.17.xh.refs_1_, bf16[768,2048]{1,0:T(8,128)(2,1)S(1)} %get-tuple-element.18.xl.refs_2_, bf16[768,2048]{1,0:T(8,128)(2,1)S(1)} %get-tuple-element.19.wh.refs_3_, ...), custom_call_target="tpu_custom_call" | custom-call | flops 5000000000 | tf_op jit(solution)/shard_map/strip_4A/pallas_call | solution.py:177
  38.2 2.9 %collective-permute-done.8.refs_2_ = f32[256,640]{1,0:T(8,128)S(1)} collective-permute-done((f32[256,640]{1,0:T(8,128)S(1)}, f32[256,640]{1,0:T(8,128)S(1)}, u32[]{:S(2)}, u32[]{:S(2)}) %collective-permute-start.8) | collective-permute-done | bytes 655392 | tf_op jit(solution)/shard_map/ppermute | solution.py:383
  41.2 2.1 %collective-permute-start.10 = (f32[256,640]{1,0:T(8,128)S(1)}, f32[256,640]{1,0:T(8,128)S(1)}, u32[]{:S(2)}, u32[]{:S(2)}) collective-permute-start(f32[256,640]{1,0:T(8,128)S(1)} %sum_4_far.1.refs_5_), channel_id=1, source_target_pairs={{0,4},{1,3},{4,8},{5,1},{8,12},{9,5},{12,14},{13,9},{14,10},{15,13... | collective-permute-start | bytes 1966088 | tf_op jit(solution)/shard_map/ppermute | solution.py:383
  46.1 2.1 %collective-permute-start.13 = (f32[128,896]{1,0:T(8,128)S(1)}, f32[128,896]{1,0:T(8,128)S(1)}, u32[]{:S(2)}, u32[]{:S(2)}) collective-permute-start(f32[128,896]{1,0:T(8,128)S(1)} %sum_4_near.1.refs_5_), channel_id=1, source_target_pairs={{0,4},{1,3},{4,8},{5,1},{8,12},{9,5},{12,14},{13,9},{14,10},{15,13... | collective-permute-start | bytes 1376264 | tf_op jit(solution)/shard_map/ppermute | solution.py:383
  48.2 4.8 %collective-permute-done.10.refs_3_ = f32[256,640]{1,0:T(8,128)S(1)} collective-permute-done((f32[256,640]{1,0:T(8,128)S(1)}, f32[256,640]{1,0:T(8,128)S(1)}, u32[]{:S(2)}, u32[]{:S(2)}) %collective-permute-start.10) | collective-permute-done | bytes 655392 | tf_op jit(solution)/shard_map/ppermute | solution.py:383
  55.3 2.7 %collective-permute-done.13.refs_1_ = f32[128,896]{1,0:T(8,128)S(1)} collective-permute-done((f32[128,896]{1,0:T(8,128)S(1)}, f32[128,896]{1,0:T(8,128)S(1)}, u32[]{:S(2)}, u32[]{:S(2)}) %collective-permute-start.13) | collective-permute-done | bytes 458784 | tf_op jit(solution)/shard_map/ppermute | solution.py:383
  58.1 4.1 %collective-permute-start.16 = (f32[256,128]{1,0:T(8,128)S(1)}, f32[256,128]{1,0:T(8,128)S(1)}, u32[]{:S(2)}, u32[]{:S(2)}) collective-permute-start(f32[256,128]{1,0:T(8,128)S(1)} %get-tuple-element.24), channel_id=1, source_target_pairs={{0,10},{1,11},{4,6},{5,7},{8,14},{9,15},{12,0},{13,1},{14,4},{15,5... | collective-permute-start | bytes 393224 | tf_op jit(solution)/shard_map/ppermute | solution.py:383
  62.3 1.9 %collective-permute-start.18 = (f32[256,128]{1,0:T(8,128)S(1)}, f32[256,128]{1,0:T(8,128)S(1)}, u32[]{:S(2)}, u32[]{:S(2)}) collective-permute-start(f32[256,128]{1,0:T(8,128)S(1)} %get-tuple-element.26), channel_id=1, source_target_pairs={{0,2},{1,3},{4,12},{5,13},{8,0},{9,1},{12,8},{13,9},{14,10},{15,11... | collective-permute-start | bytes 393224 | tf_op jit(solution)/shard_map/ppermute | solution.py:383
  64.2 2.5 %collective-permute-start.15 = (f32[128,128]{1,0:T(8,128)S(1)}, f32[128,128]{1,0:T(8,128)S(1)}, u32[]{:S(2)}, u32[]{:S(2)}) collective-permute-start(f32[128,128]{1,0:T(8,128)S(1)} %get-tuple-element.23), channel_id=1, source_target_pairs={{0,14},{1,15},{4,10},{5,11},{8,6},{9,7},{12,2},{13,3},{14,1},{15,0... | collective-permute-start | bytes 196616 | tf_op jit(solution)/shard_map/ppermute | solution.py:383
  66.7 4.8 %collective-permute-done.15.refs_0_ = f32[128,128]{1,0:T(8,128)S(1)} collective-permute-done((f32[128,128]{1,0:T(8,128)S(1)}, f32[128,128]{1,0:T(8,128)S(1)}, u32[]{:S(2)}, u32[]{:S(2)}) %collective-permute-start.15) | collective-permute-done | bytes 65568 | tf_op jit(solution)/shard_map/ppermute | solution.py:383
  71.4 1.5 %collective-permute-done.17.refs_2_ = f32[256,128]{1,0:T(8,128)S(1)} collective-permute-done((f32[256,128]{1,0:T(8,128)S(1)}, f32[256,128]{1,0:T(8,128)S(1)}, u32[]{:S(2)}, u32[]{:S(2)}) %collective-permute-start.17) | collective-permute-done | bytes 131104 | tf_op jit(solution)/shard_map/ppermute | solution.py:383
  (35 shorter events, 12.6 us)
Async XLA Ops:
  5.9 2.5 %collective-permute-start.1 = (f32[128,1152]{1,0:T(8,128)S(1)}, f32[128,1152]{1,0:T(8,128)S(1)}, u32[]{:S(2)}, u32[]{:S(2)}) collective-permute-start(f32[128,1152]{1,0:T(8,128)S(1)} %strip_1B.1.refs_5_), channel_id=1, source_target_pairs={{0,1},{1,0},{4,5},{5,4},{8,9},{9,8},{12,13},{13,12},{14,15},{15,14... | collective-permute-start | bytes 1769480 | tf_op jit(solution)/shard_map/ppermute | solution.py:383
  8.3 8.9 %collective-permute-start = (f32[256,1152]{1,0:T(8,128)S(1)}, f32[256,1152]{1,0:T(8,128)S(1)}, u32[]{:S(2)}, u32[]{:S(2)}) collective-permute-start(f32[256,1152]{1,0:T(8,128)S(1)} %strip_2B.1.refs_6_), channel_id=1, source_target_pairs={{0,1},{1,0},{4,5},{5,4},{8,9},{9,8},{12,13},{13,12},{14,15},{15,14... | collective-permute-start | bytes 3538952 | tf_op jit(solution)/shard_map/ppermute | solution.py:383
  9.2 8.1 %collective-permute-start.3 = (f32[128,640]{1,0:T(8,128)S(1)}, f32[128,640]{1,0:T(8,128)S(1)}, u32[]{:S(2)}, u32[]{:S(2)}) collective-permute-start(f32[128,640]{1,0:T(8,128)S(1)} %strip_1A_far.1.refs_6_), channel_id=1, source_target_pairs={{0,4},{1,3},{4,8},{5,1},{8,12},{9,5},{12,14},{13,9},{14,10},{15,13... | collective-permute-start | bytes 983048 | tf_op jit(solution)/shard_map/ppermute | solution.py:383
  12.9 7.8 %collective-permute-start.2 = (f32[128,512]{1,0:T(8,128)S(1)}, f32[128,512]{1,0:T(8,128)S(1)}, u32[]{:S(2)}, u32[]{:S(2)}) collective-permute-start(f32[128,512]{1,0:T(8,128)S(1)} %strip_1A_near.1.refs_5_), channel_id=1, source_target_pairs={{0,4},{1,3},{4,8},{5,1},{8,12},{9,5},{12,14},{13,9},{14,10},{15,13... | collective-permute-start | bytes 786440 | tf_op jit(solution)/shard_map/ppermute | solution.py:383
  16.4 10.8 %collective-permute-start.4 = (f32[256,1152]{1,0:T(8,128)S(1)}, f32[256,1152]{1,0:T(8,128)S(1)}, u32[]{:S(2)}, u32[]{:S(2)}) collective-permute-start(f32[256,1152]{1,0:T(8,128)S(1)} %strip_3B.1.refs_7_), channel_id=1, source_target_pairs={{0,1},{1,0},{4,5},{5,4},{8,9},{9,8},{12,13},{13,12},{14,15},{15,14... | collective-permute-start | bytes 3538952 | tf_op jit(solution)/shard_map/ppermute | solution.py:383
  18.5 10.7 %collective-permute-start.6 = (f32[256,640]{1,0:T(8,128)S(1)}, f32[256,640]{1,0:T(8,128)S(1)}, u32[]{:S(2)}, u32[]{:S(2)}) collective-permute-start(f32[256,640]{1,0:T(8,128)S(1)} %strip_2A_far.1.refs_7_), channel_id=1, source_target_pairs={{0,4},{1,3},{4,8},{5,1},{8,12},{9,5},{12,14},{13,9},{14,10},{15,13... | collective-permute-start | bytes 1966088 | tf_op jit(solution)/shard_map/ppermute | solution.py:383
  21.6 12.6 %collective-permute-start.5 = (f32[128,896]{1,0:T(8,128)S(1)}, f32[128,896]{1,0:T(8,128)S(1)}, u32[]{:S(2)}, u32[]{:S(2)}) collective-permute-start(f32[128,896]{1,0:T(8,128)S(1)} %strip_2A_near.1.refs_5_), channel_id=1, source_target_pairs={{0,4},{1,3},{4,8},{5,1},{8,12},{9,5},{12,14},{13,9},{14,10},{15,13... | collective-permute-start | bytes 1376264 | tf_op jit(solution)/shard_map/ppermute | solution.py:383
  25.3 12.9 %collective-permute-start.7 = (f32[256,1152]{1,0:T(8,128)S(1)}, f32[256,1152]{1,0:T(8,128)S(1)}, u32[]{:S(2)}, u32[]{:S(2)}) collective-permute-start(f32[256,1152]{1,0:T(8,128)S(1)} %strip_4B.1.refs_5_), channel_id=1, source_target_pairs={{0,1},{1,0},{4,5},{5,4},{8,9},{9,8},{12,13},{13,12},{14,15},{15,14... | collective-permute-start | bytes 3538952 | tf_op jit(solution)/shard_map/ppermute | solution.py:383
  29.3 11.8 %collective-permute-start.8 = (f32[256,640]{1,0:T(8,128)S(1)}, f32[256,640]{1,0:T(8,128)S(1)}, u32[]{:S(2)}, u32[]{:S(2)}) collective-permute-start(f32[256,640]{1,0:T(8,128)S(1)} %sum_3_far.1.refs_3_), channel_id=1, source_target_pairs={{0,4},{1,3},{4,8},{5,1},{8,12},{9,5},{12,14},{13,9},{14,10},{15,13... | collective-permute-start | bytes 1966088 | tf_op jit(solution)/shard_map/ppermute | solution.py:383
  34.2 11.9 %collective-permute-start.12 = (f32[128,896]{1,0:T(8,128)S(1)}, f32[128,896]{1,0:T(8,128)S(1)}, u32[]{:S(2)}, u32[]{:S(2)}) collective-permute-start(f32[128,896]{1,0:T(8,128)S(1)} %sum_3_near.1.refs_5_), channel_id=1, source_target_pairs={{0,4},{1,3},{4,8},{5,1},{8,12},{9,5},{12,14},{13,9},{14,10},{15,13... | collective-permute-start | bytes 1376264 | tf_op jit(solution)/shard_map/ppermute | solution.py:383
  41.2 11.8 %collective-permute-start.10 = (f32[256,640]{1,0:T(8,128)S(1)}, f32[256,640]{1,0:T(8,128)S(1)}, u32[]{:S(2)}, u32[]{:S(2)}) collective-permute-start(f32[256,640]{1,0:T(8,128)S(1)} %sum_4_far.1.refs_5_), channel_id=1, source_target_pairs={{0,4},{1,3},{4,8},{5,1},{8,12},{9,5},{12,14},{13,9},{14,10},{15,13... | collective-permute-start | bytes 1966088 | tf_op jit(solution)/shard_map/ppermute | solution.py:383
  44.6 9.3 %collective-permute-start.9 = (f32[256,640]{1,0:T(8,128)S(1)}, f32[256,640]{1,0:T(8,128)S(1)}, u32[]{:S(2)}, u32[]{:S(2)}) collective-permute-start(f32[256,640]{1,0:T(8,128)S(1)} %strip_5_far.1.refs_3_.refs_1_), channel_id=1, source_target_pairs={{0,1},{1,0},{4,5},{5,4},{8,9},{9,8},{12,13},{13,12},{14,15},{15,14... | collective-permute-start | bytes 1966088 | tf_op jit(solution)/shard_map/ppermute | solution.py:383
  46.1 11.9 %collective-permute-start.13 = (f32[128,896]{1,0:T(8,128)S(1)}, f32[128,896]{1,0:T(8,128)S(1)}, u32[]{:S(2)}, u32[]{:S(2)}) collective-permute-start(f32[128,896]{1,0:T(8,128)S(1)} %sum_4_near.1.refs_5_), channel_id=1, source_target_pairs={{0,4},{1,3},{4,8},{5,1},{8,12},{9,5},{12,14},{13,9},{14,10},{15,13... | collective-permute-start | bytes 1376264 | tf_op jit(solution)/shard_map/ppermute | solution.py:383
  53.1 2.1 %collective-permute-start.11 = (f32[256,640]{1,0:T(8,128)S(1)}, f32[256,640]{1,0:T(8,128)S(1)}, u32[]{:S(2)}, u32[]{:S(2)}) collective-permute-start(f32[256,640]{1,0:T(8,128)S(1)} %collective-permute-done.10.refs_3_), channel_id=1, source_target_pairs={{0,1},{1,0},{4,5},{5,4},{8,9},{9,8},{12,13},{13,12},{14,15},{15,14... | collective-permute-start | bytes 1966088 | tf_op jit(solution)/shard_map/ppermute | solution.py:383
  58.0 4.2 %collective-permute-start.14 = (f32[128,896]{1,0:T(8,128)S(1)}, f32[128,896]{1,0:T(8,128)S(1)}, u32[]{:S(2)}, u32[]{:S(2)}) collective-permute-start(f32[128,896]{1,0:T(8,128)S(1)} %add_own.1.a), channel_id=1, source_target_pairs={{0,1},{1,0},{4,5},{5,4},{8,9},{9,8},{12,13},{13,12},{14,15},{15,14... | collective-permute-start | bytes 1376264 | tf_op jit(solution)/shard_map/ppermute | solution.py:383
  58.1 13.3 %collective-permute-start.16 = (f32[256,128]{1,0:T(8,128)S(1)}, f32[256,128]{1,0:T(8,128)S(1)}, u32[]{:S(2)}, u32[]{:S(2)}) collective-permute-start(f32[256,128]{1,0:T(8,128)S(1)} %get-tuple-element.24), channel_id=1, source_target_pairs={{0,10},{1,11},{4,6},{5,7},{8,14},{9,15},{12,0},{13,1},{14,4},{15,5... | collective-permute-start | bytes 393224 | tf_op jit(solution)/shard_map/ppermute | solution.py:383
  62.2 10.7 %collective-permute-start.17 = (f32[256,128]{1,0:T(8,128)S(1)}, f32[256,128]{1,0:T(8,128)S(1)}, u32[]{:S(2)}, u32[]{:S(2)}) collective-permute-start(f32[256,128]{1,0:T(8,128)S(1)} %get-tuple-element.25), channel_id=1, source_target_pairs={{0,4},{1,5},{4,8},{5,9},{8,10},{9,11},{12,6},{13,7},{14,12},{15,13... | collective-permute-start | bytes 393224 | tf_op jit(solution)/shard_map/ppermute | solution.py:383
  62.3 10.6 %collective-permute-start.18 = (f32[256,128]{1,0:T(8,128)S(1)}, f32[256,128]{1,0:T(8,128)S(1)}, u32[]{:S(2)}, u32[]{:S(2)}) collective-permute-start(f32[256,128]{1,0:T(8,128)S(1)} %get-tuple-element.26), channel_id=1, source_target_pairs={{0,2},{1,3},{4,12},{5,13},{8,0},{9,1},{12,8},{13,9},{14,10},{15,11... | collective-permute-start | bytes 393224 | tf_op jit(solution)/shard_map/ppermute | solution.py:383
  64.2 7.3 %collective-permute-start.15 = (f32[128,128]{1,0:T(8,128)S(1)}, f32[128,128]{1,0:T(8,128)S(1)}, u32[]{:S(2)}, u32[]{:S(2)}) collective-permute-start(f32[128,128]{1,0:T(8,128)S(1)} %get-tuple-element.23), channel_id=1, source_target_pairs={{0,14},{1,15},{4,10},{5,11},{8,6},{9,7},{12,2},{13,3},{14,1},{15,0... | collective-permute-start | bytes 196616 | tf_op jit(solution)/shard_map/ppermute | solution.py:383

commit v6 on v5

--- a/solution.py
+++ b/solution.py
@@ -121,7 +121,7 @@
     return 2 * ring_chip(p) + core
 
 
-PAIRS = ((7, 3, 0, 2, 5, 6, 4, 1), (1, 2, 5, 6, 3, 7, 0, 4), (5, 6, 4, 0, 1, 3, 7, 2))
+PAIRS = ((7, 3, 0, 2, 5, 6, 4, 1), (5, 6, 4, 0, 1, 3, 7, 2), (1, 2, 5, 6, 3, 7, 0, 4))
 
 
 def pair(q, k):

time: 74.9 us -> 76 us (1.015)
  no operation moved by 1% of the time
where the time goes in v6:
time: 76 us; the launch traced here: 74.8 us
  starting transfers between devices  26.5 us (35%)
  waiting for transfers between devices  25.4 us (33%)
  Pallas kernels  22.5 us (30%)
    ppermute x19, starting transfers between devices, ring_gram(): send = lambda x, pairs: lax.ppermute(x, axis, pairs)  26.5 us
    ppermute x19, waiting for transfers between devices, ring_gram(): send = lambda x, pairs: lax.ppermute(x, axis, pairs)  25.4 us
    pallas_call x19, Pallas kernels, in_order(): pl.pallas_call(kernel, out_shape=out_shape, in_specs=[pl.BlockSpec(memory...  16.7 us
    pallas_call x1, Pallas kernels, prepare(): pl.pallas_call(functools.partial(prep_kernel, scale, axis), out_shape=[pl...  4.82 us
  transfers between devices with their start and end apart: 19, of which 10 were waited for; matrix products, arithmetic and copies ran while one was open for 0% of the time, Pallas kernels for 21%

profile of v6, /device:TPU:0, one launch (start us, length us, event | category | flops | bytes accessed | tf_op | source)
XLA Modules:
  0.0 74.8 jit_solution(15085205535927506813)
XLA Ops:
  0.0 4.8 %weighting.1 = (bf16[768,2048]{1,0:T(8,128)(2,1)S(1)}, bf16[768,2048]{1,0:T(8,128)(2,1)S(1)}, bf16[768,2048]{1,0:T(8,128)(2,1)S(1)}, bf16[768,2048]{1,0:T(8,128)(2,1)S(1)}, s32[1,128]{1,0:T(1,128)S(4)}) custom-call(s32[16]{0:T(128)} %block_hbm.1, f32[4,4,8]{2,1,0:T(4,128)} %bitcast.1, f32[768,2048]{1,0:T(8,128)} %x_hbm.1, s32[16,1,128]{2,1,0:T(1,128)} %constant.2.clone.places), custom_call_target="tpu_custom_call" | custom-call | flops 2415919104 | bytes 9437184 | tf_op jit(solution)/shard_map/weighting/pallas_call | solution.py:84
  6.4 1.9 %strip_2B.1.refs_6_ = f32[256,1152]{1,0:T(8,128)S(1)} custom-call(s32[1,128]{1,0:T(1,128)S(4)} %get-tuple-element.16.table.refs_0_, bf16[768,2048]{1,0:T(8,128)(2,1)S(1)} %get-tuple-element.17.xh.refs_1_, bf16[768,2048]{1,0:T(8,128)(2,1)S(1)} %get-tuple-element.18.xl.refs_2_, bf16[768,2048]{1,0:T(8,128)(2,1)S(1)} %get-tuple-element.19.wh.refs_3_, ...), custom_call_target="tpu_custom_call" | custom-call | flops 5000000000 | tf_op jit(solution)/shard_map/strip_2B/pallas_call | solution.py:177
  9.2 3.1 %collective-permute-start.3 = (f32[128,640]{1,0:T(8,128)S(1)}, f32[128,640]{1,0:T(8,128)S(1)}, u32[]{:S(2)}, u32[]{:S(2)}) collective-permute-start(f32[128,640]{1,0:T(8,128)S(1)} %strip_1A_far.1.refs_6_), channel_id=1, source_target_pairs={{0,4},{1,3},{4,8},{5,1},{8,12},{9,5},{12,14},{13,9},{14,10},{15,13... | collective-permute-start | bytes 983048 | tf_op jit(solution)/shard_map/ppermute | solution.py:383
  12.9 1.6 %collective-permute-start.2 = (f32[128,512]{1,0:T(8,128)S(1)}, f32[128,512]{1,0:T(8,128)S(1)}, u32[]{:S(2)}, u32[]{:S(2)}) collective-permute-start(f32[128,512]{1,0:T(8,128)S(1)} %strip_1A_near.1.refs_5_), channel_id=1, source_target_pairs={{0,4},{1,3},{4,8},{5,1},{8,12},{9,5},{12,14},{13,9},{14,10},{15,13... | collective-permute-start | bytes 786440 | tf_op jit(solution)/shard_map/ppermute | solution.py:383
  14.5 1.9 %strip_3B.1.refs_7_ = f32[256,1152]{1,0:T(8,128)S(1)} custom-call(s32[1,128]{1,0:T(1,128)S(4)} %get-tuple-element.16.table.refs_0_, bf16[768,2048]{1,0:T(8,128)(2,1)S(1)} %get-tuple-element.17.xh.refs_1_, bf16[768,2048]{1,0:T(8,128)(2,1)S(1)} %get-tuple-element.18.xl.refs_2_, bf16[768,2048]{1,0:T(8,128)(2,1)S(1)} %get-tuple-element.19.wh.refs_3_, ...), custom_call_target="tpu_custom_call" | custom-call | flops 5000000000 | tf_op jit(solution)/shard_map/strip_3B/pallas_call | solution.py:177
  18.6 2.1 %collective-permute-start.6 = (f32[256,640]{1,0:T(8,128)S(1)}, f32[256,640]{1,0:T(8,128)S(1)}, u32[]{:S(2)}, u32[]{:S(2)}) collective-permute-start(f32[256,640]{1,0:T(8,128)S(1)} %strip_2A_far.1.refs_7_), channel_id=1, source_target_pairs={{0,4},{1,3},{4,8},{5,1},{8,12},{9,5},{12,14},{13,9},{14,10},{15,13... | collective-permute-start | bytes 1966088 | tf_op jit(solution)/shard_map/ppermute | solution.py:383
  21.6 1.8 %collective-permute-start.5 = (f32[128,896]{1,0:T(8,128)S(1)}, f32[128,896]{1,0:T(8,128)S(1)}, u32[]{:S(2)}, u32[]{:S(2)}) collective-permute-start(f32[128,896]{1,0:T(8,128)S(1)} %strip_2A_near.1.refs_5_), channel_id=1, source_target_pairs={{0,4},{1,3},{4,8},{5,1},{8,12},{9,5},{12,14},{13,9},{14,10},{15,13... | collective-permute-start | bytes 1376264 | tf_op jit(solution)/shard_map/ppermute | solution.py:383
  23.4 1.9 %strip_4B.1.refs_5_ = f32[256,1152]{1,0:T(8,128)S(1)} custom-call(s32[1,128]{1,0:T(1,128)S(4)} %get-tuple-element.16.table.refs_0_, bf16[768,2048]{1,0:T(8,128)(2,1)S(1)} %get-tuple-element.17.xh.refs_1_, bf16[768,2048]{1,0:T(8,128)(2,1)S(1)} %get-tuple-element.18.xl.refs_2_, bf16[768,2048]{1,0:T(8,128)(2,1)S(1)} %get-tuple-element.19.wh.refs_3_, ...), custom_call_target="tpu_custom_call" | custom-call | flops 5000000000 | tf_op jit(solution)/shard_map/strip_4B/pallas_call | solution.py:177
  25.4 1.9 %strip_3A.1.refs_0_.refs_3_ = f32[256,1152]{1,0:T(8,128)S(1)} custom-call(s32[1,128]{1,0:T(1,128)S(4)} %get-tuple-element.16.table.refs_0_, bf16[768,2048]{1,0:T(8,128)(2,1)S(1)} %get-tuple-element.17.xh.refs_1_, bf16[768,2048]{1,0:T(8,128)(2,1)S(1)} %get-tuple-element.18.xl.refs_2_, bf16[768,2048]{1,0:T(8,128)(2,1)S(1)} %get-tuple-element.19.wh.refs_3_, ...), custom_call_target="tpu_custom_call" | custom-call | flops 5000000000 | tf_op jit(solution)/shard_map/strip_3A/pallas_call | solution.py:177
  27.3 1.9 %collective-permute-done.6.refs_2_ = f32[256,640]{1,0:T(8,128)S(1)} collective-permute-done((f32[256,640]{1,0:T(8,128)S(1)}, f32[256,640]{1,0:T(8,128)S(1)}, u32[]{:S(2)}, u32[]{:S(2)}) %collective-permute-start.6) | collective-permute-done | bytes 655392 | tf_op jit(solution)/shard_map/ppermute | solution.py:383
  29.3 2.1 %collective-permute-start.8 = (f32[256,640]{1,0:T(8,128)S(1)}, f32[256,640]{1,0:T(8,128)S(1)}, u32[]{:S(2)}, u32[]{:S(2)}) collective-permute-start(f32[256,640]{1,0:T(8,128)S(1)} %sum_3_far.1.refs_3_), channel_id=1, source_target_pairs={{0,4},{1,3},{4,8},{5,1},{8,12},{9,5},{12,14},{13,9},{14,10},{15,13... | collective-permute-start | bytes 1966088 | tf_op jit(solution)/shard_map/ppermute | solution.py:383
  31.4 2.7 %collective-permute-done.5.refs_2_ = f32[128,896]{1,0:T(8,128)S(1)} collective-permute-done((f32[128,896]{1,0:T(8,128)S(1)}, f32[128,896]{1,0:T(8,128)S(1)}, u32[]{:S(2)}, u32[]{:S(2)}) %collective-permute-start.5) | collective-permute-done | bytes 458784 | tf_op jit(solution)/shard_map/ppermute | solution.py:383
  34.2 2.1 %collective-permute-start.12 = (f32[128,896]{1,0:T(8,128)S(1)}, f32[128,896]{1,0:T(8,128)S(1)}, u32[]{:S(2)}, u32[]{:S(2)}) collective-permute-start(f32[128,896]{1,0:T(8,128)S(1)} %sum_3_near.1.refs_5_), channel_id=1, source_target_pairs={{0,4},{1,3},{4,8},{5,1},{8,12},{9,5},{12,14},{13,9},{14,10},{15,13... | collective-permute-start | bytes 1376264 | tf_op jit(solution)/shard_map/ppermute | solution.py:383
  36.3 1.9 %strip_4A.1.refs_0_.refs_3_ = f32[256,1152]{1,0:T(8,128)S(1)} custom-call(s32[1,128]{1,0:T(1,128)S(4)} %get-tuple-element.16.table.refs_0_, bf16[768,2048]{1,0:T(8,128)(2,1)S(1)} %get-tuple-element.17.xh.refs_1_, bf16[768,2048]{1,0:T(8,128)(2,1)S(1)} %get-tuple-element.18.xl.refs_2_, bf16[768,2048]{1,0:T(8,128)(2,1)S(1)} %get-tuple-element.19.wh.refs_3_, ...), custom_call_target="tpu_custom_call" | custom-call | flops 5000000000 | tf_op jit(solution)/shard_map/strip_4A/pallas_call | solution.py:177
  38.2 2.9 %collective-permute-done.8.refs_2_ = f32[256,640]{1,0:T(8,128)S(1)} collective-permute-done((f32[256,640]{1,0:T(8,128)S(1)}, f32[256,640]{1,0:T(8,128)S(1)}, u32[]{:S(2)}, u32[]{:S(2)}) %collective-permute-start.8) | collective-permute-done | bytes 655392 | tf_op jit(solution)/shard_map/ppermute | solution.py:383
  41.2 2.1 %collective-permute-start.10 = (f32[256,640]{1,0:T(8,128)S(1)}, f32[256,640]{1,0:T(8,128)S(1)}, u32[]{:S(2)}, u32[]{:S(2)}) collective-permute-start(f32[256,640]{1,0:T(8,128)S(1)} %sum_4_far.1.refs_5_), channel_id=1, source_target_pairs={{0,4},{1,3},{4,8},{5,1},{8,12},{9,5},{12,14},{13,9},{14,10},{15,13... | collective-permute-start | bytes 1966088 | tf_op jit(solution)/shard_map/ppermute | solution.py:383
  46.1 2.1 %collective-permute-start.13 = (f32[128,896]{1,0:T(8,128)S(1)}, f32[128,896]{1,0:T(8,128)S(1)}, u32[]{:S(2)}, u32[]{:S(2)}) collective-permute-start(f32[128,896]{1,0:T(8,128)S(1)} %sum_4_near.1.refs_5_), channel_id=1, source_target_pairs={{0,4},{1,3},{4,8},{5,1},{8,12},{9,5},{12,14},{13,9},{14,10},{15,13... | collective-permute-start | bytes 1376264 | tf_op jit(solution)/shard_map/ppermute | solution.py:383
  48.3 4.8 %collective-permute-done.10.refs_3_ = f32[256,640]{1,0:T(8,128)S(1)} collective-permute-done((f32[256,640]{1,0:T(8,128)S(1)}, f32[256,640]{1,0:T(8,128)S(1)}, u32[]{:S(2)}, u32[]{:S(2)}) %collective-permute-start.10) | collective-permute-done | bytes 655392 | tf_op jit(solution)/shard_map/ppermute | solution.py:383
  55.3 2.7 %collective-permute-done.13.refs_1_ = f32[128,896]{1,0:T(8,128)S(1)} collective-permute-done((f32[128,896]{1,0:T(8,128)S(1)}, f32[128,896]{1,0:T(8,128)S(1)}, u32[]{:S(2)}, u32[]{:S(2)}) %collective-permute-start.13) | collective-permute-done | bytes 458784 | tf_op jit(solution)/shard_map/ppermute | solution.py:383
  58.1 2.1 %collective-permute-start.16 = (f32[256,128]{1,0:T(8,128)S(1)}, f32[256,128]{1,0:T(8,128)S(1)}, u32[]{:S(2)}, u32[]{:S(2)}) collective-permute-start(f32[256,128]{1,0:T(8,128)S(1)} %get-tuple-element.24), channel_id=1, source_target_pairs={{0,4},{1,5},{4,8},{5,9},{8,10},{9,11},{12,6},{13,7},{14,12},{15,13... | collective-permute-start | bytes 393224 | tf_op jit(solution)/shard_map/ppermute | solution.py:383
  60.3 2.3 %collective-permute-start.17 = (f32[256,128]{1,0:T(8,128)S(1)}, f32[256,128]{1,0:T(8,128)S(1)}, u32[]{:S(2)}, u32[]{:S(2)}) collective-permute-start(f32[256,128]{1,0:T(8,128)S(1)} %get-tuple-element.25), channel_id=1, source_target_pairs={{0,10},{1,11},{4,6},{5,7},{8,14},{9,15},{12,0},{13,1},{14,4},{15,5... | collective-permute-start | bytes 393224 | tf_op jit(solution)/shard_map/ppermute | solution.py:383
  62.6 1.7 %collective-permute-start.18 = (f32[256,128]{1,0:T(8,128)S(1)}, f32[256,128]{1,0:T(8,128)S(1)}, u32[]{:S(2)}, u32[]{:S(2)}) collective-permute-start(f32[256,128]{1,0:T(8,128)S(1)} %get-tuple-element.26), channel_id=1, source_target_pairs={{0,2},{1,3},{4,12},{5,13},{8,0},{9,1},{12,8},{13,9},{14,10},{15,11... | collective-permute-start | bytes 393224 | tf_op jit(solution)/shard_map/ppermute | solution.py:383
  64.4 2.2 %collective-permute-start.15 = (f32[128,128]{1,0:T(8,128)S(1)}, f32[128,128]{1,0:T(8,128)S(1)}, u32[]{:S(2)}, u32[]{:S(2)}) collective-permute-start(f32[128,128]{1,0:T(8,128)S(1)} %get-tuple-element.23), channel_id=1, source_target_pairs={{0,14},{1,15},{4,10},{5,11},{8,6},{9,7},{12,2},{13,3},{14,1},{15,0... | collective-permute-start | bytes 196616 | tf_op jit(solution)/shard_map/ppermute | solution.py:383
  66.6 5.6 %collective-permute-done.15.refs_0_ = f32[128,128]{1,0:T(8,128)S(1)} collective-permute-done((f32[128,128]{1,0:T(8,128)S(1)}, f32[128,128]{1,0:T(8,128)S(1)}, u32[]{:S(2)}, u32[]{:S(2)}) %collective-permute-start.15) | collective-permute-done | bytes 65568 | tf_op jit(solution)/shard_map/ppermute | solution.py:383
  (35 shorter events, 14.0 us)
Async XLA Ops:
  5.9 2.5 %collective-permute-start.1 = (f32[128,1152]{1,0:T(8,128)S(1)}, f32[128,1152]{1,0:T(8,128)S(1)}, u32[]{:S(2)}, u32[]{:S(2)}) collective-permute-start(f32[128,1152]{1,0:T(8,128)S(1)} %strip_1B.1.refs_5_), channel_id=1, source_target_pairs={{0,1},{1,0},{4,5},{5,4},{8,9},{9,8},{12,13},{13,12},{14,15},{15,14... | collective-permute-start | bytes 1769480 | tf_op jit(solution)/shard_map/ppermute | solution.py:383
  8.3 8.9 %collective-permute-start = (f32[256,1152]{1,0:T(8,128)S(1)}, f32[256,1152]{1,0:T(8,128)S(1)}, u32[]{:S(2)}, u32[]{:S(2)}) collective-permute-start(f32[256,1152]{1,0:T(8,128)S(1)} %strip_2B.1.refs_6_), channel_id=1, source_target_pairs={{0,1},{1,0},{4,5},{5,4},{8,9},{9,8},{12,13},{13,12},{14,15},{15,14... | collective-permute-start | bytes 3538952 | tf_op jit(solution)/shard_map/ppermute | solution.py:383
  9.2 8.1 %collective-permute-start.3 = (f32[128,640]{1,0:T(8,128)S(1)}, f32[128,640]{1,0:T(8,128)S(1)}, u32[]{:S(2)}, u32[]{:S(2)}) collective-permute-start(f32[128,640]{1,0:T(8,128)S(1)} %strip_1A_far.1.refs_6_), channel_id=1, source_target_pairs={{0,4},{1,3},{4,8},{5,1},{8,12},{9,5},{12,14},{13,9},{14,10},{15,13... | collective-permute-start | bytes 983048 | tf_op jit(solution)/shard_map/ppermute | solution.py:383
  12.9 7.8 %collective-permute-start.2 = (f32[128,512]{1,0:T(8,128)S(1)}, f32[128,512]{1,0:T(8,128)S(1)}, u32[]{:S(2)}, u32[]{:S(2)}) collective-permute-start(f32[128,512]{1,0:T(8,128)S(1)} %strip_1A_near.1.refs_5_), channel_id=1, source_target_pairs={{0,4},{1,3},{4,8},{5,1},{8,12},{9,5},{12,14},{13,9},{14,10},{15,13... | collective-permute-start | bytes 786440 | tf_op jit(solution)/shard_map/ppermute | solution.py:383
  16.4 10.9 %collective-permute-start.4 = (f32[256,1152]{1,0:T(8,128)S(1)}, f32[256,1152]{1,0:T(8,128)S(1)}, u32[]{:S(2)}, u32[]{:S(2)}) collective-permute-start(f32[256,1152]{1,0:T(8,128)S(1)} %strip_3B.1.refs_7_), channel_id=1, source_target_pairs={{0,1},{1,0},{4,5},{5,4},{8,9},{9,8},{12,13},{13,12},{14,15},{15,14... | collective-permute-start | bytes 3538952 | tf_op jit(solution)/shard_map/ppermute | solution.py:383
  18.6 10.6 %collective-permute-start.6 = (f32[256,640]{1,0:T(8,128)S(1)}, f32[256,640]{1,0:T(8,128)S(1)}, u32[]{:S(2)}, u32[]{:S(2)}) collective-permute-start(f32[256,640]{1,0:T(8,128)S(1)} %strip_2A_far.1.refs_7_), channel_id=1, source_target_pairs={{0,4},{1,3},{4,8},{5,1},{8,12},{9,5},{12,14},{13,9},{14,10},{15,13... | collective-permute-start | bytes 1966088 | tf_op jit(solution)/shard_map/ppermute | solution.py:383
  21.6 12.6 %collective-permute-start.5 = (f32[128,896]{1,0:T(8,128)S(1)}, f32[128,896]{1,0:T(8,128)S(1)}, u32[]{:S(2)}, u32[]{:S(2)}) collective-permute-start(f32[128,896]{1,0:T(8,128)S(1)} %strip_2A_near.1.refs_5_), channel_id=1, source_target_pairs={{0,4},{1,3},{4,8},{5,1},{8,12},{9,5},{12,14},{13,9},{14,10},{15,13... | collective-permute-start | bytes 1376264 | tf_op jit(solution)/shard_map/ppermute | solution.py:383
  25.3 12.9 %collective-permute-start.7 = (f32[256,1152]{1,0:T(8,128)S(1)}, f32[256,1152]{1,0:T(8,128)S(1)}, u32[]{:S(2)}, u32[]{:S(2)}) collective-permute-start(f32[256,1152]{1,0:T(8,128)S(1)} %strip_4B.1.refs_5_), channel_id=1, source_target_pairs={{0,1},{1,0},{4,5},{5,4},{8,9},{9,8},{12,13},{13,12},{14,15},{15,14... | collective-permute-start | bytes 3538952 | tf_op jit(solution)/shard_map/ppermute | solution.py:383
  29.3 11.8 %collective-permute-start.8 = (f32[256,640]{1,0:T(8,128)S(1)}, f32[256,640]{1,0:T(8,128)S(1)}, u32[]{:S(2)}, u32[]{:S(2)}) collective-permute-start(f32[256,640]{1,0:T(8,128)S(1)} %sum_3_far.1.refs_3_), channel_id=1, source_target_pairs={{0,4},{1,3},{4,8},{5,1},{8,12},{9,5},{12,14},{13,9},{14,10},{15,13... | collective-permute-start | bytes 1966088 | tf_op jit(solution)/shard_map/ppermute | solution.py:383
  34.2 11.9 %collective-permute-start.12 = (f32[128,896]{1,0:T(8,128)S(1)}, f32[128,896]{1,0:T(8,128)S(1)}, u32[]{:S(2)}, u32[]{:S(2)}) collective-permute-start(f32[128,896]{1,0:T(8,128)S(1)} %sum_3_near.1.refs_5_), channel_id=1, source_target_pairs={{0,4},{1,3},{4,8},{5,1},{8,12},{9,5},{12,14},{13,9},{14,10},{15,13... | collective-permute-start | bytes 1376264 | tf_op jit(solution)/shard_map/ppermute | solution.py:383
  41.2 11.8 %collective-permute-start.10 = (f32[256,640]{1,0:T(8,128)S(1)}, f32[256,640]{1,0:T(8,128)S(1)}, u32[]{:S(2)}, u32[]{:S(2)}) collective-permute-start(f32[256,640]{1,0:T(8,128)S(1)} %sum_4_far.1.refs_5_), channel_id=1, source_target_pairs={{0,4},{1,3},{4,8},{5,1},{8,12},{9,5},{12,14},{13,9},{14,10},{15,13... | collective-permute-start | bytes 1966088 | tf_op jit(solution)/shard_map/ppermute | solution.py:383
  44.7 9.2 %collective-permute-start.9 = (f32[256,640]{1,0:T(8,128)S(1)}, f32[256,640]{1,0:T(8,128)S(1)}, u32[]{:S(2)}, u32[]{:S(2)}) collective-permute-start(f32[256,640]{1,0:T(8,128)S(1)} %strip_5_far.1.refs_3_.refs_1_), channel_id=1, source_target_pairs={{0,1},{1,0},{4,5},{5,4},{8,9},{9,8},{12,13},{13,12},{14,15},{15,14... | collective-permute-start | bytes 1966088 | tf_op jit(solution)/shard_map/ppermute | solution.py:383
  46.1 11.9 %collective-permute-start.13 = (f32[128,896]{1,0:T(8,128)S(1)}, f32[128,896]{1,0:T(8,128)S(1)}, u32[]{:S(2)}, u32[]{:S(2)}) collective-permute-start(f32[128,896]{1,0:T(8,128)S(1)} %sum_4_near.1.refs_5_), channel_id=1, source_target_pairs={{0,4},{1,3},{4,8},{5,1},{8,12},{9,5},{12,14},{13,9},{14,10},{15,13... | collective-permute-start | bytes 1376264 | tf_op jit(solution)/shard_map/ppermute | solution.py:383
  53.1 2.1 %collective-permute-start.11 = (f32[256,640]{1,0:T(8,128)S(1)}, f32[256,640]{1,0:T(8,128)S(1)}, u32[]{:S(2)}, u32[]{:S(2)}) collective-permute-start(f32[256,640]{1,0:T(8,128)S(1)} %collective-permute-done.10.refs_3_), channel_id=1, source_target_pairs={{0,1},{1,0},{4,5},{5,4},{8,9},{9,8},{12,13},{13,12},{14,15},{15,14... | collective-permute-start | bytes 1966088 | tf_op jit(solution)/shard_map/ppermute | solution.py:383
  58.0 4.5 %collective-permute-start.14 = (f32[128,896]{1,0:T(8,128)S(1)}, f32[128,896]{1,0:T(8,128)S(1)}, u32[]{:S(2)}, u32[]{:S(2)}) collective-permute-start(f32[128,896]{1,0:T(8,128)S(1)} %add_own.1.a), channel_id=1, source_target_pairs={{0,1},{1,0},{4,5},{5,4},{8,9},{9,8},{12,13},{13,12},{14,15},{15,14... | collective-permute-start | bytes 1376264 | tf_op jit(solution)/shard_map/ppermute | solution.py:383
  58.1 14.0 %collective-permute-start.16 = (f32[256,128]{1,0:T(8,128)S(1)}, f32[256,128]{1,0:T(8,128)S(1)}, u32[]{:S(2)}, u32[]{:S(2)}) collective-permute-start(f32[256,128]{1,0:T(8,128)S(1)} %get-tuple-element.24), channel_id=1, source_target_pairs={{0,4},{1,5},{4,8},{5,9},{8,10},{9,11},{12,6},{13,7},{14,12},{15,13... | collective-permute-start | bytes 393224 | tf_op jit(solution)/shard_map/ppermute | solution.py:383
  60.3 11.9 %collective-permute-start.17 = (f32[256,128]{1,0:T(8,128)S(1)}, f32[256,128]{1,0:T(8,128)S(1)}, u32[]{:S(2)}, u32[]{:S(2)}) collective-permute-start(f32[256,128]{1,0:T(8,128)S(1)} %get-tuple-element.25), channel_id=1, source_target_pairs={{0,10},{1,11},{4,6},{5,7},{8,14},{9,15},{12,0},{13,1},{14,4},{15,5... | collective-permute-start | bytes 393224 | tf_op jit(solution)/shard_map/ppermute | solution.py:383
  62.6 11.0 %collective-permute-start.18 = (f32[256,128]{1,0:T(8,128)S(1)}, f32[256,128]{1,0:T(8,128)S(1)}, u32[]{:S(2)}, u32[]{:S(2)}) collective-permute-start(f32[256,128]{1,0:T(8,128)S(1)} %get-tuple-element.26), channel_id=1, source_target_pairs={{0,2},{1,3},{4,12},{5,13},{8,0},{9,1},{12,8},{13,9},{14,10},{15,11... | collective-permute-start | bytes 393224 | tf_op jit(solution)/shard_map/ppermute | solution.py:383
  64.4 7.8 %collective-permute-start.15 = (f32[128,128]{1,0:T(8,128)S(1)}, f32[128,128]{1,0:T(8,128)S(1)}, u32[]{:S(2)}, u32[]{:S(2)}) collective-permute-start(f32[128,128]{1,0:T(8,128)S(1)} %get-tuple-element.23), channel_id=1, source_target_pairs={{0,14},{1,15},{4,10},{5,11},{8,6},{9,7},{12,2},{13,3},{14,1},{15,0... | collective-permute-start | bytes 196616 | tf_op jit(solution)/shard_map/ppermute | solution.py:383

commit v7 on v5

--- a/solution.py
+++ b/solution.py
@@ -65,8 +65,8 @@
             low = (value - high.astype(F32)).astype(BF16)
             xh[at] = high
             xl[at] = low
-            weighted = dot(both[b], high)
-            weighted = weighted[:band] + weighted[band:] + dot(both[b, :band], low)
+            mh, ml = both[b, :band], both[b, band:]
+            weighted = dot(mh, high) + dot(ml, high) + dot(mh, low)
             high = weighted.astype(BF16)
             wh[at] = high
             wl[at] = (weighted - high.astype(F32)).astype(BF16)

time: 74.9 us -> 75 us (level)
  no operation moved by 1% of the time
where the time goes in v7:
time: 75 us; the launch traced here: 74.2 us
  starting transfers between devices  26.4 us (35%)
  waiting for transfers between devices  24.8 us (33%)
  Pallas kernels  22.6 us (30%)
    ppermute x19, starting transfers between devices, ring_gram(): send = lambda x, pairs: lax.ppermute(x, axis, pairs)  26.4 us
    ppermute x19, waiting for transfers between devices, ring_gram(): send = lambda x, pairs: lax.ppermute(x, axis, pairs)  24.8 us
    pallas_call x19, Pallas kernels, in_order(): pl.pallas_call(kernel, out_shape=out_shape, in_specs=[pl.BlockSpec(memory...  16.7 us
    pallas_call x1, Pallas kernels, prepare(): pl.pallas_call(functools.partial(prep_kernel, scale, axis), out_shape=[pl...  4.86 us
  transfers between devices with their start and end apart: 19, of which 10 were waited for; matrix products, arithmetic and copies ran while one was open for 0% of the time, Pallas kernels for 21%

profile of v7, /device:TPU:0, one launch (start us, length us, event | category | flops | bytes accessed | tf_op | source)
XLA Modules:
  0.0 74.2 jit_solution(13637663103986685551)
XLA Ops:
  0.0 4.9 %weighting.1 = (bf16[768,2048]{1,0:T(8,128)(2,1)S(1)}, bf16[768,2048]{1,0:T(8,128)(2,1)S(1)}, bf16[768,2048]{1,0:T(8,128)(2,1)S(1)}, bf16[768,2048]{1,0:T(8,128)(2,1)S(1)}, s32[1,128]{1,0:T(1,128)S(4)}) custom-call(s32[16]{0:T(128)} %block_hbm.1, f32[4,4,8]{2,1,0:T(4,128)} %bitcast.1, f32[768,2048]{1,0:T(8,128)} %x_hbm.1, s32[16,1,128]{2,1,0:T(1,128)} %constant.2.clone.places), custom_call_target="tpu_custom_call" | custom-call | flops 2415919104 | bytes 9437184 | tf_op jit(solution)/shard_map/weighting/pallas_call | solution.py:84
  6.4 1.9 %strip_2B.1.refs_6_ = f32[256,1152]{1,0:T(8,128)S(1)} custom-call(s32[1,128]{1,0:T(1,128)S(4)} %get-tuple-element.16.table.refs_0_, bf16[768,2048]{1,0:T(8,128)(2,1)S(1)} %get-tuple-element.17.xh.refs_1_, bf16[768,2048]{1,0:T(8,128)(2,1)S(1)} %get-tuple-element.18.xl.refs_2_, bf16[768,2048]{1,0:T(8,128)(2,1)S(1)} %get-tuple-element.19.wh.refs_3_, ...), custom_call_target="tpu_custom_call" | custom-call | flops 5000000000 | tf_op jit(solution)/shard_map/strip_2B/pallas_call | solution.py:177
  9.2 3.1 %collective-permute-start.3 = (f32[128,640]{1,0:T(8,128)S(1)}, f32[128,640]{1,0:T(8,128)S(1)}, u32[]{:S(2)}, u32[]{:S(2)}) collective-permute-start(f32[128,640]{1,0:T(8,128)S(1)} %strip_1A_far.1.refs_6_), channel_id=1, source_target_pairs={{0,4},{1,3},{4,8},{5,1},{8,12},{9,5},{12,14},{13,9},{14,10},{15,13... | collective-permute-start | bytes 983048 | tf_op jit(solution)/shard_map/ppermute | solution.py:383
  12.9 1.6 %collective-permute-start.2 = (f32[128,512]{1,0:T(8,128)S(1)}, f32[128,512]{1,0:T(8,128)S(1)}, u32[]{:S(2)}, u32[]{:S(2)}) collective-permute-start(f32[128,512]{1,0:T(8,128)S(1)} %strip_1A_near.1.refs_5_), channel_id=1, source_target_pairs={{0,4},{1,3},{4,8},{5,1},{8,12},{9,5},{12,14},{13,9},{14,10},{15,13... | collective-permute-start | bytes 786440 | tf_op jit(solution)/shard_map/ppermute | solution.py:383
  14.5 1.9 %strip_3B.1.refs_7_ = f32[256,1152]{1,0:T(8,128)S(1)} custom-call(s32[1,128]{1,0:T(1,128)S(4)} %get-tuple-element.16.table.refs_0_, bf16[768,2048]{1,0:T(8,128)(2,1)S(1)} %get-tuple-element.17.xh.refs_1_, bf16[768,2048]{1,0:T(8,128)(2,1)S(1)} %get-tuple-element.18.xl.refs_2_, bf16[768,2048]{1,0:T(8,128)(2,1)S(1)} %get-tuple-element.19.wh.refs_3_, ...), custom_call_target="tpu_custom_call" | custom-call | flops 5000000000 | tf_op jit(solution)/shard_map/strip_3B/pallas_call | solution.py:177
  18.6 2.1 %collective-permute-start.6 = (f32[256,640]{1,0:T(8,128)S(1)}, f32[256,640]{1,0:T(8,128)S(1)}, u32[]{:S(2)}, u32[]{:S(2)}) collective-permute-start(f32[256,640]{1,0:T(8,128)S(1)} %strip_2A_far.1.refs_7_), channel_id=1, source_target_pairs={{0,4},{1,3},{4,8},{5,1},{8,12},{9,5},{12,14},{13,9},{14,10},{15,13... | collective-permute-start | bytes 1966088 | tf_op jit(solution)/shard_map/ppermute | solution.py:383
  21.6 1.8 %collective-permute-start.5 = (f32[128,896]{1,0:T(8,128)S(1)}, f32[128,896]{1,0:T(8,128)S(1)}, u32[]{:S(2)}, u32[]{:S(2)}) collective-permute-start(f32[128,896]{1,0:T(8,128)S(1)} %strip_2A_near.1.refs_5_), channel_id=1, source_target_pairs={{0,4},{1,3},{4,8},{5,1},{8,12},{9,5},{12,14},{13,9},{14,10},{15,13... | collective-permute-start | bytes 1376264 | tf_op jit(solution)/shard_map/ppermute | solution.py:383
  23.4 1.9 %strip_4B.1.refs_5_ = f32[256,1152]{1,0:T(8,128)S(1)} custom-call(s32[1,128]{1,0:T(1,128)S(4)} %get-tuple-element.16.table.refs_0_, bf16[768,2048]{1,0:T(8,128)(2,1)S(1)} %get-tuple-element.17.xh.refs_1_, bf16[768,2048]{1,0:T(8,128)(2,1)S(1)} %get-tuple-element.18.xl.refs_2_, bf16[768,2048]{1,0:T(8,128)(2,1)S(1)} %get-tuple-element.19.wh.refs_3_, ...), custom_call_target="tpu_custom_call" | custom-call | flops 5000000000 | tf_op jit(solution)/shard_map/strip_4B/pallas_call | solution.py:177
  25.4 1.9 %strip_3A.1.refs_0_.refs_3_ = f32[256,1152]{1,0:T(8,128)S(1)} custom-call(s32[1,128]{1,0:T(1,128)S(4)} %get-tuple-element.16.table.refs_0_, bf16[768,2048]{1,0:T(8,128)(2,1)S(1)} %get-tuple-element.17.xh.refs_1_, bf16[768,2048]{1,0:T(8,128)(2,1)S(1)} %get-tuple-element.18.xl.refs_2_, bf16[768,2048]{1,0:T(8,128)(2,1)S(1)} %get-tuple-element.19.wh.refs_3_, ...), custom_call_target="tpu_custom_call" | custom-call | flops 5000000000 | tf_op jit(solution)/shard_map/strip_3A/pallas_call | solution.py:177
  27.3 2.0 %collective-permute-done.6.refs_2_ = f32[256,640]{1,0:T(8,128)S(1)} collective-permute-done((f32[256,640]{1,0:T(8,128)S(1)}, f32[256,640]{1,0:T(8,128)S(1)}, u32[]{:S(2)}, u32[]{:S(2)}) %collective-permute-start.6) | collective-permute-done | bytes 655392 | tf_op jit(solution)/shard_map/ppermute | solution.py:383
  29.4 2.1 %collective-permute-start.8 = (f32[256,640]{1,0:T(8,128)S(1)}, f32[256,640]{1,0:T(8,128)S(1)}, u32[]{:S(2)}, u32[]{:S(2)}) collective-permute-start(f32[256,640]{1,0:T(8,128)S(1)} %sum_3_far.1.refs_3_), channel_id=1, source_target_pairs={{0,4},{1,3},{4,8},{5,1},{8,12},{9,5},{12,14},{13,9},{14,10},{15,13... | collective-permute-start | bytes 1966088 | tf_op jit(solution)/shard_map/ppermute | solution.py:383
  31.5 2.7 %collective-permute-done.5.refs_2_ = f32[128,896]{1,0:T(8,128)S(1)} collective-permute-done((f32[128,896]{1,0:T(8,128)S(1)}, f32[128,896]{1,0:T(8,128)S(1)}, u32[]{:S(2)}, u32[]{:S(2)}) %collective-permute-start.5) | collective-permute-done | bytes 458784 | tf_op jit(solution)/shard_map/ppermute | solution.py:383
  34.2 2.1 %collective-permute-start.12 = (f32[128,896]{1,0:T(8,128)S(1)}, f32[128,896]{1,0:T(8,128)S(1)}, u32[]{:S(2)}, u32[]{:S(2)}) collective-permute-start(f32[128,896]{1,0:T(8,128)S(1)} %sum_3_near.1.refs_5_), channel_id=1, source_target_pairs={{0,4},{1,3},{4,8},{5,1},{8,12},{9,5},{12,14},{13,9},{14,10},{15,13... | collective-permute-start | bytes 1376264 | tf_op jit(solution)/shard_map/ppermute | solution.py:383
  36.4 1.9 %strip_4A.1.refs_0_.refs_3_ = f32[256,1152]{1,0:T(8,128)S(1)} custom-call(s32[1,128]{1,0:T(1,128)S(4)} %get-tuple-element.16.table.refs_0_, bf16[768,2048]{1,0:T(8,128)(2,1)S(1)} %get-tuple-element.17.xh.refs_1_, bf16[768,2048]{1,0:T(8,128)(2,1)S(1)} %get-tuple-element.18.xl.refs_2_, bf16[768,2048]{1,0:T(8,128)(2,1)S(1)} %get-tuple-element.19.wh.refs_3_, ...), custom_call_target="tpu_custom_call" | custom-call | flops 5000000000 | tf_op jit(solution)/shard_map/strip_4A/pallas_call | solution.py:177
  38.2 2.9 %collective-permute-done.8.refs_2_ = f32[256,640]{1,0:T(8,128)S(1)} collective-permute-done((f32[256,640]{1,0:T(8,128)S(1)}, f32[256,640]{1,0:T(8,128)S(1)}, u32[]{:S(2)}, u32[]{:S(2)}) %collective-permute-start.8) | collective-permute-done | bytes 655392 | tf_op jit(solution)/shard_map/ppermute | solution.py:383
  41.3 2.1 %collective-permute-start.10 = (f32[256,640]{1,0:T(8,128)S(1)}, f32[256,640]{1,0:T(8,128)S(1)}, u32[]{:S(2)}, u32[]{:S(2)}) collective-permute-start(f32[256,640]{1,0:T(8,128)S(1)} %sum_4_far.1.refs_5_), channel_id=1, source_target_pairs={{0,4},{1,3},{4,8},{5,1},{8,12},{9,5},{12,14},{13,9},{14,10},{15,13... | collective-permute-start | bytes 1966088 | tf_op jit(solution)/shard_map/ppermute | solution.py:383
  46.2 2.1 %collective-permute-start.13 = (f32[128,896]{1,0:T(8,128)S(1)}, f32[128,896]{1,0:T(8,128)S(1)}, u32[]{:S(2)}, u32[]{:S(2)}) collective-permute-start(f32[128,896]{1,0:T(8,128)S(1)} %sum_4_near.1.refs_5_), channel_id=1, source_target_pairs={{0,4},{1,3},{4,8},{5,1},{8,12},{9,5},{12,14},{13,9},{14,10},{15,13... | collective-permute-start | bytes 1376264 | tf_op jit(solution)/shard_map/ppermute | solution.py:383
  48.3 4.8 %collective-permute-done.10.refs_3_ = f32[256,640]{1,0:T(8,128)S(1)} collective-permute-done((f32[256,640]{1,0:T(8,128)S(1)}, f32[256,640]{1,0:T(8,128)S(1)}, u32[]{:S(2)}, u32[]{:S(2)}) %collective-permute-start.10) | collective-permute-done | bytes 655392 | tf_op jit(solution)/shard_map/ppermute | solution.py:383
  55.4 2.7 %collective-permute-done.13.refs_1_ = f32[128,896]{1,0:T(8,128)S(1)} collective-permute-done((f32[128,896]{1,0:T(8,128)S(1)}, f32[128,896]{1,0:T(8,128)S(1)}, u32[]{:S(2)}, u32[]{:S(2)}) %collective-permute-start.13) | collective-permute-done | bytes 458784 | tf_op jit(solution)/shard_map/ppermute | solution.py:383
  58.2 4.1 %collective-permute-start.16 = (f32[256,128]{1,0:T(8,128)S(1)}, f32[256,128]{1,0:T(8,128)S(1)}, u32[]{:S(2)}, u32[]{:S(2)}) collective-permute-start(f32[256,128]{1,0:T(8,128)S(1)} %get-tuple-element.24), channel_id=1, source_target_pairs={{0,10},{1,11},{4,6},{5,7},{8,14},{9,15},{12,0},{13,1},{14,4},{15,5... | collective-permute-start | bytes 393224 | tf_op jit(solution)/shard_map/ppermute | solution.py:383
  62.3 1.9 %collective-permute-start.18 = (f32[256,128]{1,0:T(8,128)S(1)}, f32[256,128]{1,0:T(8,128)S(1)}, u32[]{:S(2)}, u32[]{:S(2)}) collective-permute-start(f32[256,128]{1,0:T(8,128)S(1)} %get-tuple-element.26), channel_id=1, source_target_pairs={{0,2},{1,3},{4,12},{5,13},{8,0},{9,1},{12,8},{13,9},{14,10},{15,11... | collective-permute-start | bytes 393224 | tf_op jit(solution)/shard_map/ppermute | solution.py:383
  64.2 2.5 %collective-permute-start.15 = (f32[128,128]{1,0:T(8,128)S(1)}, f32[128,128]{1,0:T(8,128)S(1)}, u32[]{:S(2)}, u32[]{:S(2)}) collective-permute-start(f32[128,128]{1,0:T(8,128)S(1)} %get-tuple-element.23), channel_id=1, source_target_pairs={{0,14},{1,15},{4,10},{5,11},{8,6},{9,7},{12,2},{13,3},{14,1},{15,0... | collective-permute-start | bytes 196616 | tf_op jit(solution)/shard_map/ppermute | solution.py:383
  66.7 4.8 %collective-permute-done.15.refs_0_ = f32[128,128]{1,0:T(8,128)S(1)} collective-permute-done((f32[128,128]{1,0:T(8,128)S(1)}, f32[128,128]{1,0:T(8,128)S(1)}, u32[]{:S(2)}, u32[]{:S(2)}) %collective-permute-start.15) | collective-permute-done | bytes 65568 | tf_op jit(solution)/shard_map/ppermute | solution.py:383
  71.5 1.5 %collective-permute-done.17.refs_2_ = f32[256,128]{1,0:T(8,128)S(1)} collective-permute-done((f32[256,128]{1,0:T(8,128)S(1)}, f32[256,128]{1,0:T(8,128)S(1)}, u32[]{:S(2)}, u32[]{:S(2)}) %collective-permute-start.17) | collective-permute-done | bytes 131104 | tf_op jit(solution)/shard_map/ppermute | solution.py:383
  (35 shorter events, 12.6 us)
Async XLA Ops:
  5.9 2.5 %collective-permute-start.1 = (f32[128,1152]{1,0:T(8,128)S(1)}, f32[128,1152]{1,0:T(8,128)S(1)}, u32[]{:S(2)}, u32[]{:S(2)}) collective-permute-start(f32[128,1152]{1,0:T(8,128)S(1)} %strip_1B.1.refs_5_), channel_id=1, source_target_pairs={{0,1},{1,0},{4,5},{5,4},{8,9},{9,8},{12,13},{13,12},{14,15},{15,14... | collective-permute-start | bytes 1769480 | tf_op jit(solution)/shard_map/ppermute | solution.py:383
  8.3 9.0 %collective-permute-start = (f32[256,1152]{1,0:T(8,128)S(1)}, f32[256,1152]{1,0:T(8,128)S(1)}, u32[]{:S(2)}, u32[]{:S(2)}) collective-permute-start(f32[256,1152]{1,0:T(8,128)S(1)} %strip_2B.1.refs_6_), channel_id=1, source_target_pairs={{0,1},{1,0},{4,5},{5,4},{8,9},{9,8},{12,13},{13,12},{14,15},{15,14... | collective-permute-start | bytes 3538952 | tf_op jit(solution)/shard_map/ppermute | solution.py:383
  9.2 8.1 %collective-permute-start.3 = (f32[128,640]{1,0:T(8,128)S(1)}, f32[128,640]{1,0:T(8,128)S(1)}, u32[]{:S(2)}, u32[]{:S(2)}) collective-permute-start(f32[128,640]{1,0:T(8,128)S(1)} %strip_1A_far.1.refs_6_), channel_id=1, source_target_pairs={{0,4},{1,3},{4,8},{5,1},{8,12},{9,5},{12,14},{13,9},{14,10},{15,13... | collective-permute-start | bytes 983048 | tf_op jit(solution)/shard_map/ppermute | solution.py:383
  12.9 7.8 %collective-permute-start.2 = (f32[128,512]{1,0:T(8,128)S(1)}, f32[128,512]{1,0:T(8,128)S(1)}, u32[]{:S(2)}, u32[]{:S(2)}) collective-permute-start(f32[128,512]{1,0:T(8,128)S(1)} %strip_1A_near.1.refs_5_), channel_id=1, source_target_pairs={{0,4},{1,3},{4,8},{5,1},{8,12},{9,5},{12,14},{13,9},{14,10},{15,13... | collective-permute-start | bytes 786440 | tf_op jit(solution)/shard_map/ppermute | solution.py:383
  16.4 10.8 %collective-permute-start.4 = (f32[256,1152]{1,0:T(8,128)S(1)}, f32[256,1152]{1,0:T(8,128)S(1)}, u32[]{:S(2)}, u32[]{:S(2)}) collective-permute-start(f32[256,1152]{1,0:T(8,128)S(1)} %strip_3B.1.refs_7_), channel_id=1, source_target_pairs={{0,1},{1,0},{4,5},{5,4},{8,9},{9,8},{12,13},{13,12},{14,15},{15,14... | collective-permute-start | bytes 3538952 | tf_op jit(solution)/shard_map/ppermute | solution.py:383
  18.6 10.6 %collective-permute-start.6 = (f32[256,640]{1,0:T(8,128)S(1)}, f32[256,640]{1,0:T(8,128)S(1)}, u32[]{:S(2)}, u32[]{:S(2)}) collective-permute-start(f32[256,640]{1,0:T(8,128)S(1)} %strip_2A_far.1.refs_7_), channel_id=1, source_target_pairs={{0,4},{1,3},{4,8},{5,1},{8,12},{9,5},{12,14},{13,9},{14,10},{15,13... | collective-permute-start | bytes 1966088 | tf_op jit(solution)/shard_map/ppermute | solution.py:383
  21.6 12.6 %collective-permute-start.5 = (f32[128,896]{1,0:T(8,128)S(1)}, f32[128,896]{1,0:T(8,128)S(1)}, u32[]{:S(2)}, u32[]{:S(2)}) collective-permute-start(f32[128,896]{1,0:T(8,128)S(1)} %strip_2A_near.1.refs_5_), channel_id=1, source_target_pairs={{0,4},{1,3},{4,8},{5,1},{8,12},{9,5},{12,14},{13,9},{14,10},{15,13... | collective-permute-start | bytes 1376264 | tf_op jit(solution)/shard_map/ppermute | solution.py:383
  25.3 12.9 %collective-permute-start.7 = (f32[256,1152]{1,0:T(8,128)S(1)}, f32[256,1152]{1,0:T(8,128)S(1)}, u32[]{:S(2)}, u32[]{:S(2)}) collective-permute-start(f32[256,1152]{1,0:T(8,128)S(1)} %strip_4B.1.refs_5_), channel_id=1, source_target_pairs={{0,1},{1,0},{4,5},{5,4},{8,9},{9,8},{12,13},{13,12},{14,15},{15,14... | collective-permute-start | bytes 3538952 | tf_op jit(solution)/shard_map/ppermute | solution.py:383
  29.4 11.8 %collective-permute-start.8 = (f32[256,640]{1,0:T(8,128)S(1)}, f32[256,640]{1,0:T(8,128)S(1)}, u32[]{:S(2)}, u32[]{:S(2)}) collective-permute-start(f32[256,640]{1,0:T(8,128)S(1)} %sum_3_far.1.refs_3_), channel_id=1, source_target_pairs={{0,4},{1,3},{4,8},{5,1},{8,12},{9,5},{12,14},{13,9},{14,10},{15,13... | collective-permute-start | bytes 1966088 | tf_op jit(solution)/shard_map/ppermute | solution.py:383
  34.2 11.9 %collective-permute-start.12 = (f32[128,896]{1,0:T(8,128)S(1)}, f32[128,896]{1,0:T(8,128)S(1)}, u32[]{:S(2)}, u32[]{:S(2)}) collective-permute-start(f32[128,896]{1,0:T(8,128)S(1)} %sum_3_near.1.refs_5_), channel_id=1, source_target_pairs={{0,4},{1,3},{4,8},{5,1},{8,12},{9,5},{12,14},{13,9},{14,10},{15,13... | collective-permute-start | bytes 1376264 | tf_op jit(solution)/shard_map/ppermute | solution.py:383
  41.3 11.8 %collective-permute-start.10 = (f32[256,640]{1,0:T(8,128)S(1)}, f32[256,640]{1,0:T(8,128)S(1)}, u32[]{:S(2)}, u32[]{:S(2)}) collective-permute-start(f32[256,640]{1,0:T(8,128)S(1)} %sum_4_far.1.refs_5_), channel_id=1, source_target_pairs={{0,4},{1,3},{4,8},{5,1},{8,12},{9,5},{12,14},{13,9},{14,10},{15,13... | collective-permute-start | bytes 1966088 | tf_op jit(solution)/shard_map/ppermute | solution.py:383
  44.7 9.3 %collective-permute-start.9 = (f32[256,640]{1,0:T(8,128)S(1)}, f32[256,640]{1,0:T(8,128)S(1)}, u32[]{:S(2)}, u32[]{:S(2)}) collective-permute-start(f32[256,640]{1,0:T(8,128)S(1)} %strip_5_far.1.refs_3_.refs_1_), channel_id=1, source_target_pairs={{0,1},{1,0},{4,5},{5,4},{8,9},{9,8},{12,13},{13,12},{14,15},{15,14... | collective-permute-start | bytes 1966088 | tf_op jit(solution)/shard_map/ppermute | solution.py:383
  46.2 11.9 %collective-permute-start.13 = (f32[128,896]{1,0:T(8,128)S(1)}, f32[128,896]{1,0:T(8,128)S(1)}, u32[]{:S(2)}, u32[]{:S(2)}) collective-permute-start(f32[128,896]{1,0:T(8,128)S(1)} %sum_4_near.1.refs_5_), channel_id=1, source_target_pairs={{0,4},{1,3},{4,8},{5,1},{8,12},{9,5},{12,14},{13,9},{14,10},{15,13... | collective-permute-start | bytes 1376264 | tf_op jit(solution)/shard_map/ppermute | solution.py:383
  53.1 2.1 %collective-permute-start.11 = (f32[256,640]{1,0:T(8,128)S(1)}, f32[256,640]{1,0:T(8,128)S(1)}, u32[]{:S(2)}, u32[]{:S(2)}) collective-permute-start(f32[256,640]{1,0:T(8,128)S(1)} %collective-permute-done.10.refs_3_), channel_id=1, source_target_pairs={{0,1},{1,0},{4,5},{5,4},{8,9},{9,8},{12,13},{13,12},{14,15},{15,14... | collective-permute-start | bytes 1966088 | tf_op jit(solution)/shard_map/ppermute | solution.py:383
  58.1 4.2 %collective-permute-start.14 = (f32[128,896]{1,0:T(8,128)S(1)}, f32[128,896]{1,0:T(8,128)S(1)}, u32[]{:S(2)}, u32[]{:S(2)}) collective-permute-start(f32[128,896]{1,0:T(8,128)S(1)} %add_own.1.a), channel_id=1, source_target_pairs={{0,1},{1,0},{4,5},{5,4},{8,9},{9,8},{12,13},{13,12},{14,15},{15,14... | collective-permute-start | bytes 1376264 | tf_op jit(solution)/shard_map/ppermute | solution.py:383
  58.2 13.3 %collective-permute-start.16 = (f32[256,128]{1,0:T(8,128)S(1)}, f32[256,128]{1,0:T(8,128)S(1)}, u32[]{:S(2)}, u32[]{:S(2)}) collective-permute-start(f32[256,128]{1,0:T(8,128)S(1)} %get-tuple-element.24), channel_id=1, source_target_pairs={{0,10},{1,11},{4,6},{5,7},{8,14},{9,15},{12,0},{13,1},{14,4},{15,5... | collective-permute-start | bytes 393224 | tf_op jit(solution)/shard_map/ppermute | solution.py:383
  62.3 10.7 %collective-permute-start.17 = (f32[256,128]{1,0:T(8,128)S(1)}, f32[256,128]{1,0:T(8,128)S(1)}, u32[]{:S(2)}, u32[]{:S(2)}) collective-permute-start(f32[256,128]{1,0:T(8,128)S(1)} %get-tuple-element.25), channel_id=1, source_target_pairs={{0,4},{1,5},{4,8},{5,9},{8,10},{9,11},{12,6},{13,7},{14,12},{15,13... | collective-permute-start | bytes 393224 | tf_op jit(solution)/shard_map/ppermute | solution.py:383
  62.3 10.6 %collective-permute-start.18 = (f32[256,128]{1,0:T(8,128)S(1)}, f32[256,128]{1,0:T(8,128)S(1)}, u32[]{:S(2)}, u32[]{:S(2)}) collective-permute-start(f32[256,128]{1,0:T(8,128)S(1)} %get-tuple-element.26), channel_id=1, source_target_pairs={{0,2},{1,3},{4,12},{5,13},{8,0},{9,1},{12,8},{13,9},{14,10},{15,11... | collective-permute-start | bytes 393224 | tf_op jit(solution)/shard_map/ppermute | solution.py:383
  64.2 7.3 %collective-permute-start.15 = (f32[128,128]{1,0:T(8,128)S(1)}, f32[128,128]{1,0:T(8,128)S(1)}, u32[]{:S(2)}, u32[]{:S(2)}) collective-permute-start(f32[128,128]{1,0:T(8,128)S(1)} %get-tuple-element.23), channel_id=1, source_target_pairs={{0,14},{1,15},{4,10},{5,11},{8,6},{9,7},{12,2},{13,3},{14,1},{15,0... | collective-permute-start | bytes 196616 | tf_op jit(solution)/shard_map/ppermute | solution.py:383
